TPU v7x, 32 devices: a whole 2x2x4 slice. The times are simulated.
32 devices in a mesh: flow: 8 (over z, x), shear: 4 (over y, core).
Axes of the slice: x: 2, y: 2, z: 4, core: 2. Of those that a mesh axis runs over, the one named last changes fastest.
Arguments:
- populations: float32 [19, 8, 128, 512], P(None, None, 'flow', 'shear'), may hold values from 0.5 to 2
- le_cells: int32 [2], replicated, may hold values from 0 to 127
- le_weight: int32 [2], replicated, may hold values from 0 to 255
Outputs:
- result: float32 [19, 8, 128, 512], P(None, None, 'flow', 'shear')
Inputs may be any that keep to these rules, and one draw needn't show every extreme that they name: `le_cells`: offset in whole cells, any value in the range. `le_weight`: fraction numerator, any value in the range.
All inputs are finite; a program needn't handle non-finite values.
Results may differ from a plain program's by a relative error of at most 0.0001.
Values sent between devices are 32-bit elements; how exact they have to be, the bound alone decides.
No kernel may reach another device: no remote copies, remote signals or barrier semaphores. Data moves between devices by JAX's collectives and lax.ppermute only.
A program may use at most 64 MiB of HBM per device.

v0:
```python
import jax
import jax.numpy as jnp
from jax import lax
from jax.sharding import PartitionSpec as P

STEPS = 2
WEIGHT_DENOM = 256


VELOCITY = [
    (0, 0, 0),
    (1, 0, 0),
    (-1, 0, 0),
    (0, 1, 0),
    (0, -1, 0),
    (0, 0, 1),
    (0, 0, -1),
    (1, 1, 0),
    (-1, -1, 0),
    (1, -1, 0),
    (-1, 1, 0),
    (1, 0, 1),
    (-1, 0, -1),
    (1, 0, -1),
    (-1, 0, 1),
    (0, 1, 1),
    (0, -1, -1),
    (0, 1, -1),
    (0, -1, 1),
]
WEIGHTS = [1.0 / 3.0] + [1.0 / 18.0] * 6 + [1.0 / 36.0] * 12
EASTWARD = [1, 7, 9, 11, 13]
WESTWARD = [2, 8, 10, 12, 14]
UPWARD = [3, 7, 10, 15, 17]
DOWNWARD = [4, 8, 9, 16, 18]
RISING = [5, 11, 14, 15, 18]
FALLING = [6, 12, 13, 16, 17]
RELAX_TIME = 0.6
WALL_SPEED = 0.1


def shifted(x, axis, by):
    devices = lax.axis_size(axis)
    return lax.ppermute(x, axis, [(i, (i + by) % devices) for i in range(devices)])


def lane_total(planes, lanes):
    total = planes[lanes[0]]
    for lane_id in lanes[1:]:
        total = total + planes[lane_id]
    return total


def collide(planes):
    density = lane_total(planes, list(range(19)))
    flux_x = lane_total(planes, EASTWARD) - lane_total(planes, WESTWARD)
    flux_y = lane_total(planes, UPWARD) - lane_total(planes, DOWNWARD)
    flux_z = lane_total(planes, RISING) - lane_total(planes, FALLING)
    speed_x = flux_x / density
    speed_y = flux_y / density
    speed_z = flux_z / density
    square = speed_x * speed_x + speed_y * speed_y + speed_z * speed_z
    relaxed = []
    for lane_id in range(19):
        move_x, move_y, move_z = VELOCITY[lane_id]
        along = move_x * speed_x + move_y * speed_y + move_z * speed_z
        balance = (
            WEIGHTS[lane_id] * density * (1.0 + 3.0 * along + 4.5 * along * along - 1.5 * square)
        )
        relaxed.append(planes[lane_id] - (planes[lane_id] - balance) / RELAX_TIME)
    return (relaxed, density)


def boost(pops, rho, push, lanes):
    factor = jnp.array([3.0 * WEIGHTS[k] * VELOCITY[k][0] for k in lanes], jnp.float32)
    return pops + factor[:, None, None] * (rho * push)[None]


def stream_rows(relaxed, low_pops, high_pops):
    moved = []
    for lane_id in range(19):
        move_y = VELOCITY[lane_id][1]
        plane = relaxed[lane_id]
        if move_y == 1:
            ghost = low_pops[UPWARD.index(lane_id)]
            plane = jnp.concatenate([ghost[:, :, None], plane[:, :, :-1]], axis=2)
        elif move_y == -1:
            ghost = high_pops[DOWNWARD.index(lane_id)]
            plane = jnp.concatenate([plane[:, :, 1:], ghost[:, :, None]], axis=2)
        moved.append(plane)
    return moved


def per_device(populations, le_cells, le_weight):
    width_x = populations.shape[2]
    width_y = populations.shape[3]
    flow_count = lax.axis_size("flow")
    shear_count = lax.axis_size("shear")
    flow_place = lax.axis_index("flow")
    shear_place = lax.axis_index("shear")
    at_bottom = shear_place == 0
    at_top = shear_place == shear_count - 1
    total_x = width_x * flow_count
    planes_now = [populations[k] for k in range(19)]
    for turn in range(STEPS):
        relaxed, density = collide(planes_now)
        upper_row = jnp.stack(
            [relaxed[k][:, :, width_y - 1] for k in UPWARD] + [density[:, :, width_y - 1]]
        )
        lower_row = jnp.stack([relaxed[k][:, :, 0] for k in DOWNWARD] + [density[:, :, 0]])
        from_below = shifted(upper_row, "shear", 1)
        from_above = shifted(lower_row, "shear", -1)
        offset_cells = le_cells[turn]
        fraction = le_weight[turn].astype(jnp.float32) / WEIGHT_DENOM
        start_low = jnp.where(at_bottom, offset_cells, 0)
        start_high = jnp.where(at_top, -offset_cells - 1, 0)
        starts = jnp.stack([start_low, start_high])
        coef_first = jnp.stack(
            [jnp.where(at_bottom, 1.0 - fraction, 1.0), jnp.where(at_top, fraction, 1.0)]
        )
        coef_second = jnp.stack(
            [jnp.where(at_bottom, fraction, 0.0), jnp.where(at_top, 1.0 - fraction, 0.0)]
        )
        boundary = jnp.stack([from_below, from_above])
        target_x = flow_place * width_x + jnp.arange(width_x, dtype=jnp.int32)
        source_one = (target_x[None, :] + starts[:, None]) % total_x
        source_two = (source_one + 1) % total_x
        portion = lax.all_gather(boundary, "flow", axis=3, tiled=True)
        global_x = jnp.arange(portion.shape[3], dtype=jnp.int32)
        match_one = (global_x[None, :, None] == source_one[:, None, :]).astype(jnp.float32)
        match_two = (global_x[None, :, None] == source_two[:, None, :]).astype(jnp.float32)
        mixing = coef_first[:, None, None] * match_one + coef_second[:, None, None] * match_two
        ghosts = jnp.einsum("hqzc,hcx->hqzx", portion, mixing, precision=lax.Precision.HIGHEST)
        push_low = jnp.where(at_bottom, -WALL_SPEED, 0.0).astype(jnp.float32)
        push_high = jnp.where(at_top, WALL_SPEED, 0.0).astype(jnp.float32)
        low_pops = boost(ghosts[0, :5], ghosts[0, 5], push_low, UPWARD)
        high_pops = boost(ghosts[1, :5], ghosts[1, 5], push_high, DOWNWARD)
        shifted_rows = stream_rows(relaxed, low_pops, high_pops)
        passed = []
        from_left = shifted(jnp.stack([shifted_rows[k][:, -1:, :] for k in EASTWARD]), "flow", 1)
        from_right = shifted(jnp.stack([shifted_rows[k][:, :1, :] for k in WESTWARD]), "flow", -1)
        for lane_id in range(19):
            move_x, move_y, move_z = VELOCITY[lane_id]
            plane = shifted_rows[lane_id]
            if move_x == 1:
                plane = jnp.concatenate(
                    [from_left[EASTWARD.index(lane_id)], plane[:, :-1, :]], axis=1
                )
            elif move_x == -1:
                plane = jnp.concatenate(
                    [plane[:, 1:, :], from_right[WESTWARD.index(lane_id)]], axis=1
                )
            passed.append(jnp.roll(plane, move_z, axis=0))
        planes_now = passed
    return jnp.stack(planes_now)


def solution(mesh):
    return jax.shard_map(
        per_device,
        mesh=mesh,
        in_specs=(P(None, None, "flow", "shear"), P(), P()),
        out_specs=P(None, None, "flow", "shear"),
        check_vma=False,
    )
```

profile of v0, /device:TPU:0, one launch (start us, length us, event | category | flops | bytes accessed | tf_op | source)
XLA Modules:
  0.0 148.1 jit_solution(4445231420689109465)
XLA Ops:
  0.0 1.4 fusion.312
  2.1 0.6 fusion.111
  5.4 2.0 %collective-permute-start.1 = (f32[6,8,16]{2,1,0:T(8,128)S(1)}, f32[6,8,16]{2,1,0:T(8,128)S(1)}, u32[]{:S(2)}, u32[]{:S(2)}) collective-permute-start(f32[6,8,16]{2,1,0:T(8,128)S(1)} %constant_dynamic-update-slice_fusion.6), channel_id=1, source_target_pairs={{0,3},{1,0},{2,1},{3,2},{4,7},{5,4},{6,5},{7,6},{8,11},{9,8},{10,9... | collective-permute-start | bytes 9224 | tf_op jit(solution)/shard_map/ppermute | solution.py:44
  12.0 0.7 fusion.316
  12.7 0.6 constant_dynamic-update-slice_fusion.16
  13.3 0.6 constant_dynamic-update-slice_fusion.21
  13.9 0.7 fusion.318
  14.5 0.7 fusion.315
  15.2 0.6 fusion.314
  16.7 0.7 and_select_fusion.1
  17.4 0.6 pad_maximum_fusion.72
  18.6 33.2 %all_gather.6 = f32[2,6,8,128]{2,0,1,3:T(2,128)S(1)} all-gather(f32[2,6,8,16]{2,0,1,3:T(2,128)S(1)} %copy.7890), channel_id=1, replica_groups=mesh['flow'=8,'shear'=4] {'flow'}, dimensions={3}, use_global_device_ids=true | all-gather | bytes 55296 | tf_op jit(solution)/shard_map/all_gather | solution.py:128
  51.9 1.4 fusion.2
  54.3 0.7 pad_maximum_fusion.63
  55.2 0.7 fusion.325
  56.1 0.7 fusion.326
  57.0 0.7 fusion.327
  57.9 0.7 pad_maximum_fusion.56
  58.6 0.7 fusion.328
  59.3 0.7 fusion.331
  60.0 0.7 fusion.332
  60.7 0.7 fusion.333
  61.7 0.7 fusion.334
  62.4 0.7 constant_dynamic-update-slice_fusion.15
  63.1 0.7 constant_dynamic-update-slice_fusion.14
  63.7 1.3 constant_dynamic-update-slice_fusion.13
  65.0 1.3 constant_dynamic-update-slice_fusion.12
  66.3 1.5 collective-permute-start.2
  67.7 0.7 constant_dynamic-update-slice_fusion.20
  68.4 0.7 constant_dynamic-update-slice_fusion.19
  69.1 1.3 constant_dynamic-update-slice_fusion.18
  70.3 1.3 constant_dynamic-update-slice_fusion.17
  71.7 3.3 %collective-permute-start.3 = (f32[5,8,1,128]{3,1,2,0:T(8,128)}, f32[5,8,1,128]{3,1,2,0:T(8,128)S(1)}, u32[]{:S(2)}, u32[]{:S(2)}) collective-permute-start(f32[5,8,1,128]{3,1,2,0:T(8,128)} %constant_dynamic-update-slice_fusion.17), channel_id=1, source_target_pairs={{0,28},{4,0},{8,4},{12,8},{16,12},{20,16},{24,20},{28,24},{1,29},{... | collective-permute-start | bytes 61448 | tf_op jit(solution)/shard_map/ppermute | solution.py:44
  75.3 0.7 copy.7897
  76.0 0.7 copy.7899
  76.8 0.6 slice_bitcast_fusion.57
  77.4 0.6 pad_maximum_fusion.19
  78.0 0.6 slice_bitcast_fusion.56
  78.7 0.6 pad_maximum_fusion.18
  79.8 0.7 fusion.147
  81.2 0.6 fusion.329
  81.9 0.6 fusion.330
  82.7 0.6 constant_dynamic-update-slice_fusion.27
  84.3 0.6 constant_dynamic-update-slice_fusion.26
  84.9 0.6 constant_dynamic-update-slice_fusion.25
  86.1 0.6 constant_dynamic-update-slice_fusion.23
  86.7 0.6 constant_dynamic-update-slice_fusion.22
  87.5 0.6 constant_dynamic-update-slice_fusion.33
  88.7 0.6 constant_dynamic-update-slice_fusion.32
  89.3 0.6 constant_dynamic-update-slice_fusion.31
  91.0 0.6 constant_dynamic-update-slice_fusion.28
  91.6 1.7 %collective-permute-start.5 = (f32[6,8,16]{2,1,0:T(8,128)}, f32[6,8,16]{2,1,0:T(8,128)S(1)}, u32[]{:S(2)}, u32[]{:S(2)}) collective-permute-start(f32[6,8,16]{2,1,0:T(8,128)} %constant_dynamic-update-slice_fusion.28), channel_id=1, source_target_pairs={{0,3},{1,0},{2,1},{3,2},{4,7},{5,4},{6,5},{7,6},{8,11},{9,8},{10,9... | collective-permute-start | bytes 9224 | tf_op jit(solution)/shard_map/ppermute | solution.py:44
  93.9 2.2 %constant_dynamic-update-slice_fusion.62 = f32[19,8,16,128]{3,1,2,0:T(8,128)S(1)} fusion(f32[1,7,16,128]{3,1,2,0:T(8,128)} %fusion.334, f32[1,1,16,128]{3,1,2,0:T(1,128)} %bitcast.685, f32[1,1,16,128]{3,1,2,0:T(1,128)} %bitcast.684, f32[1,7,16,128]{3,1,2,0:T(8,128)} %fusion.333, f32[1,1,16,128]{3,1,2,0:T(1,128)S(1)} %bitcast.683, ...), kind=kLoop, calls=%fused_computation.66 | loop fusion | flops 2457599 | bytes 2490368
  96.2 0.6 constant_dynamic-update-slice_fusion.38
  97.4 0.7 pad_maximum_fusion.61
  98.3 32.0 %all_gather.7 = f32[2,6,8,128]{2,0,1,3:T(2,128)S(1)} all-gather(f32[2,6,8,16]{2,0,1,3:T(2,128)S(1)} %copy.7928), channel_id=1, replica_groups=mesh['flow'=8,'shear'=4] {'flow'}, dimensions={3}, use_global_device_ids=true | all-gather | bytes 55296 | tf_op jit(solution)/shard_map/all_gather | solution.py:128
  130.4 1.4 fusion
  132.3 3.9 %collective-permute-start.7 = (f32[5,8,1,128]{3,1,2,0:T(8,128)S(1)}, f32[5,8,1,128]{3,1,2,0:T(8,128)S(1)}, u32[]{:S(2)}, u32[]{:S(2)}) collective-permute-start(f32[5,8,1,128]{3,1,2,0:T(8,128)S(1)} %constant_dynamic-update-slice_fusion.39), channel_id=1, source_target_pairs={{0,28},{4,0},{8,4},{12,8},{16,12},{20,16},{24,20},{28,24},{1,29},{... | collective-permute-start | bytes 61448 | tf_op jit(solution)/shard_map/ppermute | solution.py:44
  136.5 0.7 constant_dynamic-update-slice_fusion.37
  137.2 0.7 constant_dynamic-update-slice_fusion.36
  137.8 0.6 constant_dynamic-update-slice_fusion.35
  138.4 0.6 constant_dynamic-update-slice_fusion.34
  140.0 5.7 %collective-permute-done.6 = f32[5,8,1,128]{3,1,2,0:T(8,128)S(1)} collective-permute-done((f32[5,8,1,128]{3,1,2,0:T(8,128)}, f32[5,8,1,128]{3,1,2,0:T(8,128)S(1)}, u32[]{:S(2)}, u32[]{:S(2)}) %collective-permute-start.6) | collective-permute-done | bytes 20512 | tf_op jit(solution)/shard_map/ppermute | solution.py:44
  146.9 1.3 copy.7940
  (231 shorter events, 16.2 us)
Async XLA Ops:
  2.7 15.7 %copy-start.5 = (f32[8,16,128]{2,0,1:T(8,128)}, f32[8,16,128]{2,0,1:T(8,128)S(1)}, u32[]{:S(2)}) copy-start(f32[8,16,128]{2,0,1:T(8,128)S(1)} %get-tuple-element.57) | copy-start | bytes 196612
  2.7 15.7 %copy-start.4 = (f32[8,16,128]{2,0,1:T(8,128)}, f32[8,16,128]{2,0,1:T(8,128)S(1)}, u32[]{:S(2)}) copy-start(f32[8,16,128]{2,0,1:T(8,128)S(1)} %get-tuple-element.55) | copy-start | bytes 196612
  2.7 15.7 %copy-start.6 = (f32[8,16,128]{2,0,1:T(8,128)}, f32[8,16,128]{2,0,1:T(8,128)S(1)}, u32[]{:S(2)}) copy-start(f32[8,16,128]{2,0,1:T(8,128)S(1)} %get-tuple-element.58) | copy-start | bytes 196612
  2.7 15.7 %copy-start.3 = (f32[8,16,128]{2,0,1:T(8,128)}, f32[8,16,128]{2,0,1:T(8,128)S(1)}, u32[]{:S(2)}) copy-start(f32[8,16,128]{2,0,1:T(8,128)S(1)} %get-tuple-element.54) | copy-start | bytes 196612
  2.7 4.7 %copy-start.28 = (s32[2]{0:T(128)S(1)}, s32[2]{0:T(128)}, u32[]{:S(2)}) copy-start(s32[2]{0:T(128)} %param.8) | copy-start | bytes 28
  2.8 7.9 %copy-start.29 = (s32[2]{0:T(128)S(1)}, s32[2]{0:T(128)}, u32[]{:S(2)}) copy-start(s32[2]{0:T(128)} %param.9) | copy-start | bytes 28
  4.1 14.4 %collective-permute-start = (f32[6,8,16]{2,1,0:T(8,128)S(1)}, f32[6,8,16]{2,1,0:T(8,128)S(1)}, u32[]{:S(2)}, u32[]{:S(2)}) collective-permute-start(f32[6,8,16]{2,1,0:T(8,128)S(1)} %constant_dynamic-update-slice_fusion), channel_id=1, source_target_pairs={{0,1},{1,2},{2,3},{3,0},{4,5},{5,6},{6,7},{7,4},{8,9},{9,10},{10,1... | collective-permute-start | bytes 9224 | tf_op jit(solution)/shard_map/ppermute | solution.py:44
  5.4 13.1 %collective-permute-start.1 = (f32[6,8,16]{2,1,0:T(8,128)S(1)}, f32[6,8,16]{2,1,0:T(8,128)S(1)}, u32[]{:S(2)}, u32[]{:S(2)}) collective-permute-start(f32[6,8,16]{2,1,0:T(8,128)S(1)} %constant_dynamic-update-slice_fusion.6), channel_id=1, source_target_pairs={{0,3},{1,0},{2,1},{3,2},{4,7},{5,4},{6,5},{7,6},{8,11},{9,8},{10,9... | collective-permute-start | bytes 9224 | tf_op jit(solution)/shard_map/ppermute | solution.py:44
  14.5 64.8 %copy-start = (f32[8,15,128]{2,0,1:T(8,128)}, f32[8,15,128]{2,0,1:T(8,128)S(1)}, u32[]{:S(2)}) copy-start(f32[8,15,128]{2,0,1:T(8,128)S(1)} %get-tuple-element.171) | copy-start | bytes 184324
  18.4 34.9 %copy-start.22 = (f32[5]{0:T(128)S(1)}, f32[5]{0:T(128)}, u32[]{:S(2)}) copy-start(f32[5]{0:T(128)} %constant.128.clone) | copy-start | bytes 64
  18.4 34.9 %copy-start.24 = (f32[5]{0:T(128)S(1)}, f32[5]{0:T(128)}, u32[]{:S(2)}) copy-start(f32[5]{0:T(128)} %constant.129.clone) | copy-start | bytes 64
  61.6 17.8 %copy-start.2 = (f32[8,15,128]{2,0,1:T(8,128)S(1)}, f32[8,15,128]{2,0,1:T(8,128)}, u32[]{:S(2)}) copy-start(f32[8,15,128]{2,0,1:T(8,128)} %pad_maximum_fusion.56) | copy-start | bytes 184324
  61.6 17.8 %copy-start.10 = (f32[7,16,128]{2,0,1:T(8,128)S(1)}, f32[7,16,128]{2,0,1:T(8,128)}, u32[]{:S(2)}) copy-start(f32[7,16,128]{2,0,1:T(8,128)} %get-tuple-element.167) | copy-start | bytes 172036
  61.6 17.8 %copy-start.11 = (f32[1,16,128]{2,0,1:T(1,128)S(1)}, f32[1,16,128]{2,0,1:T(1,128)}, u32[]{:S(2)}) copy-start(f32[1,16,128]{2,0,1:T(1,128)} %pad_maximum_fusion.63) | copy-start | bytes 24580
  61.6 17.8 %copy-start.17 = (f32[1,16,128]{2,0,1:T(1,128)S(1)}, f32[1,16,128]{2,0,1:T(1,128)}, u32[]{:S(2)}) copy-start(f32[1,16,128]{2,0,1:T(1,128)} %get-tuple-element.72) | copy-start | bytes 24580
  61.6 17.8 %copy-start.19 = (f32[1,16,128]{2,0,1:T(1,128)S(1)}, f32[1,16,128]{2,0,1:T(1,128)}, u32[]{:S(2)}) copy-start(f32[1,16,128]{2,0,1:T(1,128)} %get-tuple-element.165) | copy-start | bytes 24580
  66.3 10.5 %collective-permute-start.2 = (f32[5,8,1,128]{3,1,2,0:T(8,128)}, f32[5,8,1,128]{3,1,2,0:T(8,128)S(1)}, u32[]{:S(2)}, u32[]{:S(2)}) collective-permute-start(f32[5,8,1,128]{3,1,2,0:T(8,128)} %constant_dynamic-update-slice_fusion.12), channel_id=1, source_target_pairs={{0,4},{4,8},{8,12},{12,16},{16,20},{20,24},{24,28},{28,0},{1,5},{5... | collective-permute-start | bytes 61448 | tf_op jit(solution)/shard_map/ppermute | solution.py:44
  71.7 9.2 %copy-start.12 = (f32[1,16,128]{2,0,1:T(1,128)}, f32[1,16,128]{2,0,1:T(1,128)S(1)}, u32[]{:S(2)}) copy-start(f32[1,16,128]{2,0,1:T(1,128)S(1)} %pad_maximum_fusion.62) | copy-start | bytes 24580
  71.7 6.3 %collective-permute-start.3 = (f32[5,8,1,128]{3,1,2,0:T(8,128)}, f32[5,8,1,128]{3,1,2,0:T(8,128)S(1)}, u32[]{:S(2)}, u32[]{:S(2)}) collective-permute-start(f32[5,8,1,128]{3,1,2,0:T(8,128)} %constant_dynamic-update-slice_fusion.17), channel_id=1, source_target_pairs={{0,28},{4,0},{8,4},{12,8},{16,12},{20,16},{24,20},{28,24},{1,29},{... | collective-permute-start | bytes 61448 | tf_op jit(solution)/shard_map/ppermute | solution.py:44
  78.0 2.9 %copy-start.13 = (f32[1,16,128]{2,0,1:T(1,128)}, f32[1,16,128]{2,0,1:T(1,128)S(1)}, u32[]{:S(2)}) copy-start(f32[1,16,128]{2,0,1:T(1,128)S(1)} %pad_maximum_fusion.69) | copy-start | bytes 24580
  78.7 2.3 %copy-start.14 = (f32[1,16,128]{2,0,1:T(1,128)}, f32[1,16,128]{2,0,1:T(1,128)S(1)}, u32[]{:S(2)}) copy-start(f32[1,16,128]{2,0,1:T(1,128)S(1)} %pad_maximum_fusion.68) | copy-start | bytes 24580
  78.7 2.2 %copy-start.15 = (f32[1,16,128]{2,0,1:T(1,128)}, f32[1,16,128]{2,0,1:T(1,128)S(1)}, u32[]{:S(2)}) copy-start(f32[1,16,128]{2,0,1:T(1,128)S(1)} %pad_maximum_fusion.67) | copy-start | bytes 24580
  78.7 2.2 %copy-start.16 = (f32[1,16,128]{2,0,1:T(1,128)}, f32[1,16,128]{2,0,1:T(1,128)S(1)}, u32[]{:S(2)}) copy-start(f32[1,16,128]{2,0,1:T(1,128)S(1)} %pad_maximum_fusion.66) | copy-start | bytes 24580
  79.8 1.1 copy-start.1
  79.8 1.1 copy-start.18
  81.2 12.7 %copy-start.8 = (f32[8,16,128]{2,0,1:T(8,128)}, f32[8,16,128]{2,0,1:T(8,128)S(1)}, u32[]{:S(2)}) copy-start(f32[8,16,128]{2,0,1:T(8,128)S(1)} %get-tuple-element.39) | copy-start | bytes 196612
  87.3 10.1 %collective-permute-start.4 = (f32[6,8,16]{2,1,0:T(8,128)}, f32[6,8,16]{2,1,0:T(8,128)}, u32[]{:S(2)}, u32[]{:S(2)}) collective-permute-start(f32[6,8,16]{2,1,0:T(8,128)} %constant_dynamic-update-slice_fusion.22), channel_id=1, source_target_pairs={{0,1},{1,2},{2,3},{3,0},{4,5},{5,6},{6,7},{7,4},{8,9},{9,10},{10,1... | collective-permute-start | bytes 9224 | tf_op jit(solution)/shard_map/ppermute | solution.py:44
  91.6 5.8 %collective-permute-start.5 = (f32[6,8,16]{2,1,0:T(8,128)}, f32[6,8,16]{2,1,0:T(8,128)S(1)}, u32[]{:S(2)}, u32[]{:S(2)}) collective-permute-start(f32[6,8,16]{2,1,0:T(8,128)} %constant_dynamic-update-slice_fusion.28), channel_id=1, source_target_pairs={{0,3},{1,0},{2,1},{3,2},{4,7},{5,4},{6,5},{7,6},{8,11},{9,8},{10,9... | collective-permute-start | bytes 9224 | tf_op jit(solution)/shard_map/ppermute | solution.py:44
  93.9 2.2 %copy-start.7 = (f32[8,16,128]{2,0,1:T(8,128)S(1)}, f32[8,16,128]{2,0,1:T(8,128)}, u32[]{:S(2)}) copy-start(f32[8,16,128]{2,0,1:T(8,128)} %get-tuple-element.52) | copy-start | bytes 196612
  93.9 3.1 %copy-start.9 = (f32[8,16,128]{2,0,1:T(8,128)S(1)}, f32[8,16,128]{2,0,1:T(8,128)}, u32[]{:S(2)}) copy-start(f32[8,16,128]{2,0,1:T(8,128)} %copy-done.8) | copy-start | bytes 196612
  96.9 33.4 %copy-start.20 = (s32[2,16]{1,0:T(2,128)S(1)}, s32[2,16]{1,0:T(2,128)}, u32[]{:S(2)}) copy-start(s32[2,16]{1,0:T(2,128)} %get-tuple-element.150) | copy-start | bytes 388
  97.0 33.4 %copy-start.21 = (s32[2,16]{1,0:T(2,128)S(1)}, s32[2,16]{1,0:T(2,128)}, u32[]{:S(2)}) copy-start(s32[2,16]{1,0:T(2,128)} %get-tuple-element.151) | copy-start | bytes 388
  97.0 33.4 %copy-start.26 = (f32[2]{0:T(128)S(1)}, f32[2]{0:T(128)}, u32[]{:S(2)}) copy-start(f32[2]{0:T(128)} %get-tuple-element.172) | copy-start | bytes 28
  97.0 33.4 %copy-start.27 = (f32[2]{0:T(128)S(1)}, f32[2]{0:T(128)}, u32[]{:S(2)}) copy-start(f32[2]{0:T(128)} %get-tuple-element.173) | copy-start | bytes 28
  97.3 34.4 %copy-start.23 = (f32[5]{0:T(128)S(1)}, f32[5]{0:T(128)}, u32[]{:S(2)}) copy-start(f32[5]{0:T(128)} %constant.128.clone) | copy-start | bytes 64
  97.3 34.4 %copy-start.25 = (f32[5]{0:T(128)S(1)}, f32[5]{0:T(128)}, u32[]{:S(2)}) copy-start(f32[5]{0:T(128)} %constant.129.clone) | copy-start | bytes 64
  97.4 34.7 %copy-start.30 = (f32[5,8,1,128]{3,1,2,0:T(8,128)S(1)}, f32[5,8,1,128]{3,1,2,0:T(8,128)}, u32[]{:S(2)}) copy-start(f32[5,8,1,128]{3,1,2,0:T(8,128)} %constant_dynamic-update-slice_fusion.43) | copy-start | bytes 61444
  132.3 13.4 %collective-permute-start.7 = (f32[5,8,1,128]{3,1,2,0:T(8,128)S(1)}, f32[5,8,1,128]{3,1,2,0:T(8,128)S(1)}, u32[]{:S(2)}, u32[]{:S(2)}) collective-permute-start(f32[5,8,1,128]{3,1,2,0:T(8,128)S(1)} %constant_dynamic-update-slice_fusion.39), channel_id=1, source_target_pairs={{0,28},{4,0},{8,4},{12,8},{16,12},{20,16},{24,20},{28,24},{1,29},{... | collective-permute-start | bytes 61448 | tf_op jit(solution)/shard_map/ppermute | solution.py:44
  139.0 6.7 %collective-permute-start.6 = (f32[5,8,1,128]{3,1,2,0:T(8,128)}, f32[5,8,1,128]{3,1,2,0:T(8,128)S(1)}, u32[]{:S(2)}, u32[]{:S(2)}) collective-permute-start(f32[5,8,1,128]{3,1,2,0:T(8,128)} %constant_dynamic-update-slice_fusion.34), channel_id=1, source_target_pairs={{0,4},{4,8},{8,12},{12,16},{16,20},{20,24},{24,28},{28,0},{1,5},{5... | collective-permute-start | bytes 61448 | tf_op jit(solution)/shard_map/ppermute | solution.py:44
where the time goes:
time: 149 us; the launch traced here: 148 us
  blocking collectives  65.3 us (44%)
  local copies, waits for them, and re-layouts  33 us (22%)
  other arithmetic  23.4 us (16%)
  starting transfers between devices  13 us (9%)
  waiting for transfers between devices  5.73 us (4%)
  between operations  5.03 us (3%)
  matrix products  2.77 us (2%)
    all_gather x2, blocking collectives, per_device(): portion = lax.all_gather(boundary, 'flow', axis=3, tiled=True)  65.3 us
    ppermute x8, starting transfers between devices, shifted(): lax.ppermute(x, axis, [(i, (i + by) % devices) for i in range(devices)])  13 us
    unnamed x90, local copies, waits for them, and re-layouts  11.6 us
    unnamed x26, other arithmetic  7.27 us
    ppermute x8, waiting for transfers between devices, shifted(): lax.ppermute(x, axis, [(i, (i + by) % devices) for i in range(devices)])  5.73 us
    concatenate x6, other arithmetic, per_device(): passed.append(jnp.roll(plane, move_z, axis=0))  4.13 us
  transfers between devices with their start and end apart: 8, of which 1 were waited for; matrix products, arithmetic and copies ran while one was open for 18% of the time, Pallas kernels for 0%

commit v1 on v0

v1 whole, which is shorter than its diff:
```python
import jax
import jax.numpy as jnp
from jax import lax
from jax.experimental import pallas as pl
from jax.experimental.pallas import tpu as pltpu
from jax.sharding import PartitionSpec as P

WEIGHT_DENOM = 256
VELOCITY = [
    (0, 0, 0),
    (1, 0, 0),
    (-1, 0, 0),
    (0, 1, 0),
    (0, -1, 0),
    (0, 0, 1),
    (0, 0, -1),
    (1, 1, 0),
    (-1, -1, 0),
    (1, -1, 0),
    (-1, 1, 0),
    (1, 0, 1),
    (-1, 0, -1),
    (1, 0, -1),
    (-1, 0, 1),
    (0, 1, 1),
    (0, -1, -1),
    (0, 1, -1),
    (0, -1, 1),
]
WEIGHTS = [1.0 / 3.0] + [1.0 / 18.0] * 6 + [1.0 / 36.0] * 12
EAST = [1, 7, 9, 11, 13]
WEST = [2, 8, 10, 12, 14]
UP = [3, 7, 10, 15, 17]
DOWN = [4, 8, 9, 16, 18]
OMEGA = 1.0 / 0.6
WALL_SPEED = 0.1
BOOST = 3.0 * WALL_SPEED / 36.0
NZ = 8
LANES = 128
GAP = 4
HALF = 64
BASE = 2


def lane_iota():
    return lax.broadcasted_iota(jnp.int32, (NZ, LANES), 1)


def roll_y(v, by):
    by = by % LANES
    return pltpu.roll(v, by, 1) if by else v


def roll_z(v, by):
    by = by % NZ
    return pltpu.roll(v, by, 0) if by else v


def moments(f):
    e = f[1] + f[11] + f[13]
    w = f[2] + f[12] + f[14]
    n = f[3] + f[15] + f[17]
    s = f[4] + f[16] + f[18]
    d79 = f[7] + f[9]
    d810 = f[8] + f[10]
    rho = ((f[0] + f[5]) + f[6]) + (e + w) + (n + s) + (d79 + d810)
    jx = (e - w) + (d79 - d810)
    jy = (n - s) + ((f[7] - f[9]) + (f[10] - f[8]))
    jz = (f[5] - f[6]) + ((f[11] - f[12]) + (f[14] - f[13])) + ((f[15] - f[16]) + (f[18] - f[17]))
    return rho, jx, jy, jz


def relax(rho, jx, jy, jz, f, wanted):
    inv = 1.0 / rho
    ux, uy, uz = jx * inv, jy * inv, jz * inv
    base = (rho - 1.5 * (jx * ux + jy * uy + jz * uz)) * (OMEGA / 36.0)
    keep = 1.0 - OMEGA
    post = {}
    done = set()
    for q in wanted:
        if q in done:
            continue
        cx, cy, cz = VELOCITY[q]
        if q == 0:
            post[0] = keep * f[0] + 12.0 * base
            continue
        opposite = VELOCITY.index((-cx, -cy, -cz))
        jc, uc = None, None
        for c, j, u in ((cx, jx, ux), (cy, jy, uy), (cz, jz, uz)):
            if c:
                if jc is None:
                    jc, uc = (j, u) if c > 0 else (-j, -u)
                else:
                    jc, uc = (jc + j, uc + u) if c > 0 else (jc - j, uc - u)
        scale = WEIGHTS[q] * 36.0
        even = base * scale if scale != 1.0 else base
        even = even + (jc * uc) * (4.5 * OMEGA * WEIGHTS[q])
        odd = jc * (3.0 * OMEGA * WEIGHTS[q])
        post[q] = keep * f[q] + (even + odd)
        done.add(q)
        if opposite in wanted:
            post[opposite] = keep * f[opposite] + (even - odd)
            done.add(opposite)
    return post


def classes(p, across):
    if across == "x":
        plus, minus = (1, 11, 13), (2, 12, 14)
    else:
        plus, minus = (3, 15, 17), (4, 16, 18)
    rising, falling = plus[1], plus[2]
    low, high = minus[1], minus[2]
    return [
        p[0] + p[5] + p[6],
        p[plus[0]] + p[rising] + p[falling],
        p[minus[0]] + p[low] + p[high],
        p[5] - p[6],
        p[rising] - p[falling],
        p[high] - p[low],
    ]


def column(ref, q, x, width):
    return ref[q, pl.ds(x, NZ, stride=width), :]


def pack_kernel(flows, shears, width, f_hbm, rows_ref, east_ref, west_ref, f_ref, sems):
    copies = [pltpu.make_async_copy(f_hbm.at[q], f_ref.at[q], sems.at[q]) for q in range(19)]
    for copy in copies:
        copy.start()
    shear = lax.axis_index("shear")
    lane = lane_iota()
    boost_up = jnp.where(shear == shears - 1, -BOOST, 0.0).astype(jnp.float32)
    boost_down = jnp.where(shear == 0, BOOST, 0.0).astype(jnp.float32)
    here = [(lane >= x * GAP) & (lane < (x + 1) * GAP) for x in range(width)]
    edge = []
    for q in range(19):
        copies[q].wait()
        total = jnp.ones((NZ, LANES), jnp.float32)
        for x in range(width):
            total = jnp.where(here[x], roll_y(column(f_ref, q, x, width), x * GAP + 2), total)
        edge.append(total)
    rho, jx, jy, jz = moments(edge)
    post = relax(rho, jx, jy, jz, edge, range(19))
    post = {q: roll_z(post[q], VELOCITY[q][2]) for q in range(19)}
    sums = classes(post, "x")

    def groups(ghosts, outer, at, far):
        planes = [(g, at) for g in ghosts] + [(s, at) for s in sums] + [(o, far) for o in outer]
        vregs = []
        for v in range(2):
            total = None
            for half in range(2):
                for slot in range(GAP):
                    plane, row = planes[(v * 2 + half) * GAP + slot]
                    moved = roll_y(plane, half * HALF + slot - row)
                    if total is None:
                        total = moved
                    else:
                        inside = (lane >= half * HALF) & (lane < (half + 1) * HALF)
                        total = jnp.where(inside & (lane % GAP == slot), moved, total)
            vregs.append(total)
        return vregs

    ups = [post[q] + VELOCITY[q][0] * boost_up * rho if VELOCITY[q][0] else post[q] for q in UP]
    downs = [post[q] + VELOCITY[q][0] * boost_down * rho if VELOCITY[q][0] else post[q] for q in DOWN]
    up0, up1 = groups(ups, [post[q] for q in UP], 1, 0)
    down0, down1 = groups(downs, [post[q] for q in DOWN], 2, 3)
    above = lax.rem(shear + 1, shears)
    below = lax.rem(shear + shears - 1, shears)

    def put(at):
        for to, first, second in ((above, up0, up1), (below, down0, down1), (shear, up0, down0)):
            rows_ref[at * shears + to, 0:NZ, :] = first
            rows_ref[at * shears + to, NZ : 2 * NZ, :] = second
        for extra in range(2, shears - 1):
            rows_ref[at * shears + lax.rem(shear + extra, shears)] = jnp.zeros((2 * NZ, LANES), jnp.float32)

    if flows <= 8:
        for at in range(flows):
            put(at)
    else:
        pl.loop(0, flows)(put)

    for out, near, far, lanes in ((east_ref, width - 1, width - 2, EAST), (west_ref, 0, 1, WEST)):
        for at, first in ((far, 0), (near, 5)):
            f = [column(f_ref, q, at, width) for q in range(19)]
            wanted = list(range(19)) if at == near else lanes
            post = relax(*moments(f), f, wanted)
            for q in wanted:
                post[q] = roll_y(roll_z(post[q], VELOCITY[q][2]), VELOCITY[q][1])
            for i, q in enumerate(lanes):
                out[first + i] = post[q]
            if at == near:
                for i, s in enumerate(classes(post, "y")):
                    out[10 + i] = s


def local_kernel(width, f_ref, a_ref):
    def step(x):
        f = [column(f_ref, q, x, width) for q in range(19)]
        post = relax(*moments(f), f, range(19))
        for q in range(19):
            cx, cy, cz = VELOCITY[q]
            a_ref[q, x + 1 + cx] = roll_y(roll_z(post[q], cz), cy)

    pl.loop(0, width, unroll=2)(step)
    for q in range(19):
        cx = VELOCITY[q][0]
        zero = jnp.zeros((NZ, LANES), jnp.float32)
        for x in (0, 1, width, width + 1):
            if not 0 <= x - 1 - cx < width:
                a_ref[q, x] = zero


def finish_kernel(
    flows, shears, width, cells, weight, a_hbm, rows_ref, west_ref, east_ref, out_hbm,
    a_ref, out_ref, sem_in, sem_out,
):
    load = pltpu.make_async_copy(a_hbm, a_ref, sem_in)
    load.start()
    flow = lax.axis_index("flow")
    shear = lax.axis_index("shear")
    lane = lane_iota()
    total_x = flows * width
    at_bottom = shear == 0
    at_top = shear == shears - 1
    above = lax.rem(shear + 1, shears)
    below = lax.rem(shear + shears - 1, shears)
    k1, k2 = cells[0], cells[1]
    frac = [weight[s].astype(jnp.float32) / WEIGHT_DENOM for s in range(2)]
    one, zero = jnp.float32(1.0), jnp.float32(0.0)

    def window(start, source, vreg, half):
        first = lax.rem(flow * width + start - BASE + 2 * total_x, total_x)
        block = lax.div(first, width)
        skip = (first - block * width) * GAP
        a, b, c = [
            rows_ref[lax.rem(block + k, flows) * shears + source, vreg * NZ : (vreg + 1) * NZ, :]
            for k in range(3)
        ]
        if half:
            a, c = roll_y(a, HALF), roll_y(c, HALF)
        else:
            b = roll_y(b, HALF)
        both = jnp.where(lane < HALF, a, b)
        return pltpu.roll(jnp.where(lane >= skip, both, c), lax.rem(LANES - skip, LANES), 1)

    def side(upward):
        lanes = UP if upward else DOWN
        others = DOWN if upward else UP
        active = at_bottom if upward else at_top
        source = below if upward else above

        def starts(k, low):
            return k if low else -k - 1

        def coefs(s, low):
            pair = (one - frac[s], frac[s]) if low else (frac[s], one - frac[s])
            return jnp.where(active, pair[0], one), jnp.where(active, pair[1], zero)

        def mixed(v, pair):
            return pair[0] * v + pair[1] * roll_y(v, -GAP)

        start1 = jnp.where(active, starts(k1, upward), 0)
        start2 = jnp.where(active, starts(k2, upward), 0)
        start3 = jnp.where(active, starts(k2, upward) + starts(k1, not upward), 0)
        near = [mixed(window(start1, source, 0, h), coefs(0, upward)) for h in range(2)]
        ghost1 = {q: (near[i // GAP], i % GAP) for i, q in enumerate(lanes)}
        packs = [None] + [window(start2, source, v, h) for v, h in ((0, 1), (1, 0), (1, 1))]
        pair3 = coefs(0, not upward)
        own = 1 if upward else 0
        back = [mixed(window(start3, shear, own, h), pair3) for h in range(2)]

        def plane(at, by):
            return roll_y(packs[at // GAP], by * GAP - at % GAP)

        f = {}
        for i, q in enumerate(lanes):
            f[q] = plane(11 + i, VELOCITY[q][0])
        for i, q in enumerate(others):
            f[q] = roll_y(back[i // GAP], VELOCITY[q][0] * GAP - i % GAP)
        mid, plus, minus = plane(5, 0), plane(6, 1), plane(7, -1)
        midz, plusz, minusz = plane(8, 0), plane(9, 1), plane(10, -1)
        up = [f[q] for q in UP]
        down = [f[q] for q in DOWN]
        sum_up = up[0] + up[1] + up[2] + up[3] + up[4]
        sum_down = down[0] + down[1] + down[2] + down[3] + down[4]
        rho = (mid + plus + minus) + (sum_up + sum_down)
        jx = (plus - minus) + ((f[7] - f[10]) + (f[9] - f[8]))
        jy = sum_up - sum_down
        jz = (midz + plusz + minusz) + ((f[15] - f[17]) + (f[18] - f[16]))
        post = relax(rho, jx, jy, jz, f, lanes)
        boost = jnp.where(active, -BOOST if upward else BOOST, 0.0).astype(jnp.float32)
        pair2 = coefs(1, upward)
        ghost2 = {}
        for q in lanes:
            cx, _, cz = VELOCITY[q]
            p = post[q] + cx * boost * rho if cx else post[q]
            ghost2[q] = (roll_z(mixed(p, pair2), cz), 0)
        return ghost1, ghost2

    up1, up2 = side(True)
    down1, down2 = side(False)
    ghosts1 = {**up1, **down1}
    ghosts2 = {**up2, **down2}
    at_first = lane == 0
    at_last = lane == LANES - 1

    def insert(v, ghosts, q, x):
        cy = VELOCITY[q][1]
        if cy == 0:
            return v
        g, slot = ghosts[q]
        by = (0 if cy > 0 else LANES - 1) - ((x + BASE) * GAP + slot)
        if isinstance(x, int):
            moved = roll_y(g, by)
        else:
            moved = pltpu.roll(g, lax.rem(by + LANES, LANES), 1)
        return jnp.where(at_first if cy > 0 else at_last, moved, v)

    load.wait()
    for i in range(5):
        a_ref[EAST[i], 1] = west_ref[5 + i]
        a_ref[WEST[i], width] = east_ref[5 + i]

    def put(q, x, post):
        cx, cy, cz = VELOCITY[q]
        v = insert(roll_y(roll_z(post[q], cz), cy), ghosts2, q, x)
        out_ref[q, pl.ds(x + cx, NZ, stride=width), :] = v

    def inner(x, keep):
        f = [insert(a_ref[q, x + 1], ghosts1, q, x - VELOCITY[q][0]) for q in range(19)]
        wanted = [q for q in range(19) if VELOCITY[q][0] != -keep or keep == 0]
        post = relax(*moments(f), f, wanted)
        for q in wanted:
            put(q, x, post)

    for x, halo, entering, leaving in ((-1, west_ref, EAST, WEST), (width, east_ref, WEST, EAST)):
        cx = VELOCITY[entering[0]][0]
        f = {q: insert(halo[i], ghosts1, q, x - cx) for i, q in enumerate(entering)}
        for q in leaving:
            f[q] = insert(a_ref[q, x + 1], ghosts1, q, x + cx)

        def edge_value(q):
            g, slot = ghosts1[q]
            return roll_y(g, (0 if VELOCITY[q][1] > 0 else LANES - 1) - ((x + BASE) * GAP + slot))

        n, np_, nm = edge_value(3), edge_value(15), edge_value(17)
        s, sm, sp = edge_value(4), edge_value(16), edge_value(18)
        plus = jnp.where(at_first, n + np_ + nm, halo[11])
        minus = jnp.where(at_last, s + sm + sp, halo[12])
        plusz = jnp.where(at_first, np_ - nm, halo[14])
        minusz = jnp.where(at_last, sp - sm, halo[15])
        sum_e = f[1] + f[7] + f[9] + f[11] + f[13]
        sum_w = f[2] + f[8] + f[10] + f[12] + f[14]
        rho = (halo[10] + plus + minus) + (sum_e + sum_w)
        jx = sum_e - sum_w
        jy = (plus - minus) + ((f[7] - f[8]) + (f[10] - f[9]))
        jz = (halo[13] + plusz + minusz) + ((f[11] - f[12]) + (f[14] - f[13]))
        post = relax(rho, jx, jy, jz, f, entering)
        for q in entering:
            put(q, x, post)

    inner(0, 1)
    pl.loop(1, width - 1, unroll=2)(lambda x: inner(x, 0))
    inner(width - 1, -1)
    store = pltpu.make_async_copy(out_ref, out_hbm, sem_out)
    store.start()
    store.wait()


def per_device(populations, le_cells, le_weight):
    width = populations.shape[2]
    height = populations.shape[3]
    flows = lax.axis_size("flow")
    shears = lax.axis_size("shear")
    assert populations.shape[:2] == (19, NZ) and height == LANES
    assert width * GAP == HALF and shears >= 3 and flows >= 3
    f32 = jnp.float32
    f = populations.reshape(19, NZ * width, height)
    vmem = pl.BlockSpec(memory_space=pltpu.VMEM)
    anyspace = pl.BlockSpec(memory_space=pl.ANY)
    smem = pl.BlockSpec(memory_space=pltpu.SMEM)
    params = pltpu.CompilerParams(vmem_limit_bytes=32 * 1024 * 1024)
    devices = flows * shears

    def body(kernel, *fixed):
        return lambda *refs: kernel(*fixed, *refs)

    rows, east, west = pl.pallas_call(
        body(pack_kernel, flows, shears, width),
        out_shape=[
            jax.ShapeDtypeStruct((devices, 2 * NZ, LANES), f32),
            jax.ShapeDtypeStruct((16, NZ, LANES), f32),
            jax.ShapeDtypeStruct((16, NZ, LANES), f32),
        ],
        in_specs=[anyspace],
        out_specs=[vmem] * 3,
        scratch_shapes=[pltpu.VMEM((19, NZ * width, LANES), f32), pltpu.SemaphoreType.DMA((19,))],
        compiler_params=params,
        name="pack",
    )(f)
    rows = lax.all_to_all(rows, ("flow", "shear"), 0, 0, tiled=True)
    from_west = lax.ppermute(east, "flow", [(i, (i + 1) % flows) for i in range(flows)])
    from_east = lax.ppermute(west, "flow", [(i, (i - 1) % flows) for i in range(flows)])
    streamed = pl.pallas_call(
        body(local_kernel, width),
        out_shape=jax.ShapeDtypeStruct((19, width + 2, NZ, LANES), f32),
        in_specs=[vmem],
        out_specs=vmem,
        compiler_params=params,
        cost_estimate=pl.CostEstimate(flops=8_000_000, bytes_accessed=2_700_000, transcendentals=0),
        name="local",
    )(f)
    out = pl.pallas_call(
        body(finish_kernel, flows, shears, width),
        out_shape=jax.ShapeDtypeStruct((19, NZ * width, LANES), f32),
        in_specs=[smem, smem, anyspace, vmem, vmem, vmem],
        out_specs=anyspace,
        scratch_shapes=[
            pltpu.VMEM((19, width + 2, NZ, LANES), f32),
            pltpu.VMEM((19, NZ * width, LANES), f32),
            pltpu.SemaphoreType.DMA,
            pltpu.SemaphoreType.DMA,
        ],
        compiler_params=params,
        name="finish",
    )(le_cells, le_weight, streamed, rows, from_west, from_east)
    return out.reshape(populations.shape)


def solution(mesh):
    return jax.shard_map(
        per_device,
        mesh=mesh,
        in_specs=(P(None, None, "flow", "shear"), P(), P()),
        out_specs=P(None, None, "flow", "shear"),
        check_vma=False,
    )
```

time: 149 us -> 28.8 us (0.19)
  blocking collectives: 65.3 us -> 0 us
  local copies, waits for them, and re-layouts: 33 us -> 1.3 us
  other arithmetic: 23.4 us -> 0 us
  Pallas kernels: 0 us -> 10.1 us
  between operations: 5.03 us -> 0.04 us
  matrix products: 2.77 us -> 0 us
    all_gather x2 -> x0, blocking collectives: 65.3 us -> none  [per_device(): portion = lax.all_gather(boundary, 'flow', axis=3, tiled=True)]
    concatenate x30 -> x0, other arithmetic: 10.5 us -> none  [the longest x6 4.13 us: per_device(): passed.append(jnp.roll(plane, move_z, axis=0))]
    unnamed x90 -> x8, local copies, waits for them, and re-layouts: 11.6 us -> 1.3 us
    slice x65 -> x0, local copies, waits for them, and re-layouts: 10.2 us -> none  [the longest x20 2.14 us: per_device(): relaxed[k][:, :, width_y - 1]]
    pallas_call x0 -> x3, Pallas kernels: none -> 10.1 us  [the longest x1 4.36 us: per_device(): pl.pallas_call(body(pack_kernel, flows, shears, width), out_shape=[jax.Sh...]
    another operation x35 -> x0, local copies, waits for them, and re-layouts: 8.45 us -> none  [the longest x2 1.86 us: per_device(): jnp.stack([shifted_rows[k][:, -1:, :] for k in EASTWARD])]
    ppermute x8 -> x2, starting transfers between devices: 13 us -> 4.78 us  [the longest x1 2.96 us: per_device(): lax.ppermute(west, 'flow', [(i, (i - 1) % flows) for i in range(flows)])]
    all_to_all x0 -> x1, starting transfers between devices: none -> 7.3 us  [per_device(): rows = lax.all_to_all(rows, ('flow', 'shear'), 0, 0, tiled=True)]
  transfers between devices with their start and end apart: 8 -> 3, of which waited for: 1 -> 1; matrix products, arithmetic and copies ran while one was open for 18% -> 0% of each run, Pallas kernels for 0% -> 5%
where the time goes in v1:
time: 28.8 us; the launch traced here: 28.6 us
  starting transfers between devices  12.1 us (42%)
  Pallas kernels  10.1 us (35%)
  waiting for transfers between devices  5.01 us (17%)
  local copies, waits for them, and re-layouts  1.3 us (5%)
    all_to_all x1, starting transfers between devices, per_device(): rows = lax.all_to_all(rows, ('flow', 'shear'), 0, 0, tiled=True)  7.3 us
    ppermute x1, waiting for transfers between devices, per_device(): lax.ppermute(east, 'flow', [(i, (i + 1) % flows) for i in range(flows)])  5 us
    pallas_call x1, Pallas kernels, per_device(): pl.pallas_call(body(pack_kernel, flows, shears, width), out_shape=[jax.Sh...  4.36 us
    pallas_call x1, Pallas kernels, per_device(): pl.pallas_call(body(finish_kernel, flows, shears, width), out_shape=jax.S...  4.33 us
    ppermute x1, starting transfers between devices, per_device(): lax.ppermute(west, 'flow', [(i, (i - 1) % flows) for i in range(flows)])  2.96 us
    ppermute x1, starting transfers between devices, per_device(): lax.ppermute(east, 'flow', [(i, (i + 1) % flows) for i in range(flows)])  1.82 us
    pallas_call x1, Pallas kernels, per_device(): pl.pallas_call(body(local_kernel, width), out_shape=jax.ShapeDtypeStruct(...  1.46 us
    unnamed x8, local copies, waits for them, and re-layouts  1.3 us
  transfers between devices with their start and end apart: 3, of which 1 were waited for; matrix products, arithmetic and copies ran while one was open for 0% of the time, Pallas kernels for 5%

profile of v1, /device:TPU:0, one launch (start us, length us, event | category | flops | bytes accessed | tf_op | source)
XLA Modules:
  0.0 28.6 jit_solution(693624966704062321)
XLA Ops:
  0.0 0.0 copy-start
  0.0 1.3 %copy-done = f32[19,8,16,128]{3,2,1,0:T(8,128)S(1)} copy-done((f32[19,8,16,128]{3,2,1,0:T(8,128)S(1)}, f32[19,8,16,128]{3,2,1,0:T(8,128)}, u32[]{:S(2)}) %copy-start) | copy-done | bytes 1245208
  1.3 0.0 copy-start.1
  1.3 4.4 %pack.1 = (f32[32,16,128]{2,1,0:T(8,128)}, f32[16,8,128]{2,1,0:T(8,128)S(1)}, f32[16,8,128]{2,1,0:T(8,128)S(1)}) custom-call(f32[19,128,128]{2,1,0:T(8,128)S(1)} %bitcast.2), custom_call_target="tpu_custom_call" | custom-call | tf_op jit(solution)/shard_map/pack/pallas_call | solution.py:392
  5.7 7.3 %all-to-all-start = ((f32[32,16,128]{2,1,0:T(8,128)}), f32[32,16,128]{2,1,0:T(8,128)S(1)}, u32[]{:S(2)}, u32[]{:S(2)}) async-start(f32[32,16,128]{2,1,0:T(8,128)} %get-tuple-element.8), calls=%async_computation | async-start | bytes 524288 | tf_op jit(solution)/shard_map/all_to_all | solution.py:405
  13.0 1.8 %collective-permute-start = (f32[16,8,128]{2,1,0:T(8,128)S(1)}, f32[16,8,128]{2,1,0:T(8,128)S(1)}, u32[]{:S(2)}, u32[]{:S(2)}) collective-permute-start(f32[16,8,128]{2,1,0:T(8,128)S(1)} %get-tuple-element.9), channel_id=1, source_target_pairs={{0,4},{4,8},{8,12},{12,16},{16,20},{20,24},{24,28},{28,0},{1,5},{5... | collective-permute-start | bytes 196616 | tf_op jit(solution)/shard_map/ppermute | solution.py:406
  14.8 0.0 copy-start.2
  14.8 0.0 copy-start.3
  14.8 3.0 %collective-permute-start.1 = (f32[16,8,128]{2,1,0:T(8,128)S(1)}, f32[16,8,128]{2,1,0:T(8,128)S(1)}, u32[]{:S(2)}, u32[]{:S(2)}) collective-permute-start(f32[16,8,128]{2,1,0:T(8,128)S(1)} %get-tuple-element.10), channel_id=1, source_target_pairs={{0,28},{4,0},{8,4},{12,8},{16,12},{20,16},{24,20},{28,24},{1,29},{... | collective-permute-start | bytes 196616 | tf_op jit(solution)/shard_map/ppermute | solution.py:407
  17.8 0.0 copy-done.1
  17.8 1.5 %local.1.refs_2_ = f32[19,18,8,128]{3,2,1,0:T(8,128)S(1)} custom-call(f32[19,128,128]{2,1,0:T(8,128)S(1)} %bitcast.3), custom_call_target="tpu_custom_call" | custom-call | flops 8000000 | bytes 2700000 | tf_op jit(solution)/shard_map/local/pallas_call | solution.py:408
  19.2 5.0 %collective-permute-done.refs_4_ = f32[16,8,128]{2,1,0:T(8,128)S(1)} collective-permute-done((f32[16,8,128]{2,1,0:T(8,128)S(1)}, f32[16,8,128]{2,1,0:T(8,128)S(1)}, u32[]{:S(2)}, u32[]{:S(2)}) %collective-permute-start) | collective-permute-done | bytes 65568 | tf_op jit(solution)/shard_map/ppermute | solution.py:406
  24.2 0.0 collective-permute-done.1.refs_5_
  24.2 0.0 all-to-all-done.refs_3_
  24.2 0.0 copy-done.2
  24.2 0.0 copy-done.3
  24.2 4.3 %finish.1 = f32[19,128,128]{2,1,0:T(8,128)} custom-call(s32[2]{0:T(128)S(1)} %copy-done.2, s32[2]{0:T(128)S(1)} %copy-done.3, f32[19,18,8,128]{3,2,1,0:T(8,128)S(1)} %local.1.refs_2_, f32[32,16,128]{2,1,0:T(8,128)S(1)} %all-to-all-done.refs_3_, f32[16,8,128]{2,1,0:T(8,128)S(1)} %collective-permute-done.refs_4_, f32[16,8,128]{2,1,0:T(8,128)S(1)} %collective-permute-done.1.refs_5_), custom_call_target="tpu_custom_call" | custom-call | tf_op jit(solution)/shard_map/finish/pallas_call | solution.py:417
Async XLA Ops:
  0.0 1.3 %copy-start = (f32[19,8,16,128]{3,2,1,0:T(8,128)S(1)}, f32[19,8,16,128]{3,2,1,0:T(8,128)}, u32[]{:S(2)}) copy-start(f32[19,8,16,128]{3,2,1,0:T(8,128)} %param.3) | copy-start | bytes 3735556
  1.3 16.5 %copy-start.1 = (f32[19,8,16,128]{3,2,1,0:T(8,128)S(1)}, f32[19,8,16,128]{3,2,1,0:T(8,128)}, u32[]{:S(2)}) copy-start(f32[19,8,16,128]{3,2,1,0:T(8,128)} %param.3) | copy-start | bytes 3735556
  5.7 18.6 %all-to-all-start = ((f32[32,16,128]{2,1,0:T(8,128)}), f32[32,16,128]{2,1,0:T(8,128)S(1)}, u32[]{:S(2)}, u32[]{:S(2)}) async-start(f32[32,16,128]{2,1,0:T(8,128)} %get-tuple-element.8), calls=%async_computation | async-start | bytes 524288 | tf_op jit(solution)/shard_map/all_to_all | solution.py:405
  13.0 11.2 %collective-permute-start = (f32[16,8,128]{2,1,0:T(8,128)S(1)}, f32[16,8,128]{2,1,0:T(8,128)S(1)}, u32[]{:S(2)}, u32[]{:S(2)}) collective-permute-start(f32[16,8,128]{2,1,0:T(8,128)S(1)} %get-tuple-element.9), channel_id=1, source_target_pairs={{0,4},{4,8},{8,12},{12,16},{16,20},{20,24},{24,28},{28,0},{1,5},{5... | collective-permute-start | bytes 196616 | tf_op jit(solution)/shard_map/ppermute | solution.py:406
  14.8 9.4 %copy-start.2 = (s32[2]{0:T(128)S(1)}, s32[2]{0:T(128)}, u32[]{:S(2)}) copy-start(s32[2]{0:T(128)} %refs_0_.1) | copy-start | bytes 28
  14.8 9.4 %copy-start.3 = (s32[2]{0:T(128)S(1)}, s32[2]{0:T(128)}, u32[]{:S(2)}) copy-start(s32[2]{0:T(128)} %refs_1_.1) | copy-start | bytes 28
  14.8 9.4 %collective-permute-start.1 = (f32[16,8,128]{2,1,0:T(8,128)S(1)}, f32[16,8,128]{2,1,0:T(8,128)S(1)}, u32[]{:S(2)}, u32[]{:S(2)}) collective-permute-start(f32[16,8,128]{2,1,0:T(8,128)S(1)} %get-tuple-element.10), channel_id=1, source_target_pairs={{0,28},{4,0},{8,4},{12,8},{16,12},{20,16},{24,20},{28,24},{1,29},{... | collective-permute-start | bytes 196616 | tf_op jit(solution)/shard_map/ppermute | solution.py:407

commit v2 on v1

--- a/solution.py
+++ b/solution.py
@@ -125,10 +125,7 @@
     return ref[q, pl.ds(x, NZ, stride=width), :]
 
 
-def pack_kernel(flows, shears, width, f_hbm, rows_ref, east_ref, west_ref, f_ref, sems):
-    copies = [pltpu.make_async_copy(f_hbm.at[q], f_ref.at[q], sems.at[q]) for q in range(19)]
-    for copy in copies:
-        copy.start()
+def pack_kernel(flows, shears, width, f_ref, rows_ref, east_ref, west_ref):
     shear = lax.axis_index("shear")
     lane = lane_iota()
     boost_up = jnp.where(shear == shears - 1, -BOOST, 0.0).astype(jnp.float32)
@@ -136,7 +133,6 @@
     here = [(lane >= x * GAP) & (lane < (x + 1) * GAP) for x in range(width)]
     edge = []
     for q in range(19):
-        copies[q].wait()
         total = jnp.ones((NZ, LANES), jnp.float32)
         for x in range(width):
             total = jnp.where(here[x], roll_y(column(f_ref, q, x, width), x * GAP + 2), total)
@@ -215,11 +211,9 @@
 
 
 def finish_kernel(
-    flows, shears, width, cells, weight, a_hbm, rows_ref, west_ref, east_ref, out_hbm,
-    a_ref, out_ref, sem_in, sem_out,
+    flows, shears, width, cells, weight, a_ref, rows_ref, west_ref, east_ref, out_hbm,
+    out_ref, sem_out,
 ):
-    load = pltpu.make_async_copy(a_hbm, a_ref, sem_in)
-    load.start()
     flow = lax.axis_index("flow")
     shear = lax.axis_index("shear")
     lane = lane_iota()
@@ -320,10 +314,12 @@
             moved = pltpu.roll(g, lax.rem(by + LANES, LANES), 1)
         return jnp.where(at_first if cy > 0 else at_last, moved, v)
 
-    load.wait()
-    for i in range(5):
-        a_ref[EAST[i], 1] = west_ref[5 + i]
-        a_ref[WEST[i], width] = east_ref[5 + i]
+    def arrived(q, x):
+        if isinstance(x, int) and x == 0 and q in EAST:
+            return west_ref[5 + EAST.index(q)]
+        if isinstance(x, int) and x == width - 1 and q in WEST:
+            return east_ref[5 + WEST.index(q)]
+        return a_ref[q, x + 1]
 
     def put(q, x, post):
         cx, cy, cz = VELOCITY[q]
@@ -331,7 +327,7 @@
         out_ref[q, pl.ds(x + cx, NZ, stride=width), :] = v
 
     def inner(x, keep):
-        f = [insert(a_ref[q, x + 1], ghosts1, q, x - VELOCITY[q][0]) for q in range(19)]
+        f = [insert(arrived(q, x), ghosts1, q, x - VELOCITY[q][0]) for q in range(19)]
         wanted = [q for q in range(19) if VELOCITY[q][0] != -keep or keep == 0]
         post = relax(*moments(f), f, wanted)
         for q in wanted:
@@ -364,7 +360,7 @@
             put(q, x, post)
 
     inner(0, 1)
-    pl.loop(1, width - 1, unroll=2)(lambda x: inner(x, 0))
+    pl.loop(1, width - 1, unroll=7)(lambda x: inner(x, 0))
     inner(width - 1, -1)
     store = pltpu.make_async_copy(out_ref, out_hbm, sem_out)
     store.start()
@@ -382,6 +378,7 @@
     f = populations.reshape(19, NZ * width, height)
     vmem = pl.BlockSpec(memory_space=pltpu.VMEM)
     anyspace = pl.BlockSpec(memory_space=pl.ANY)
+    hbm = pl.BlockSpec(memory_space=pltpu.HBM)
     smem = pl.BlockSpec(memory_space=pltpu.SMEM)
     params = pltpu.CompilerParams(vmem_limit_bytes=32 * 1024 * 1024)
     devices = flows * shears
@@ -396,9 +393,8 @@
             jax.ShapeDtypeStruct((16, NZ, LANES), f32),
             jax.ShapeDtypeStruct((16, NZ, LANES), f32),
         ],
-        in_specs=[anyspace],
+        in_specs=[vmem],
         out_specs=[vmem] * 3,
-        scratch_shapes=[pltpu.VMEM((19, NZ * width, LANES), f32), pltpu.SemaphoreType.DMA((19,))],
         compiler_params=params,
         name="pack",
     )(f)
@@ -417,12 +413,10 @@
     out = pl.pallas_call(
         body(finish_kernel, flows, shears, width),
         out_shape=jax.ShapeDtypeStruct((19, NZ * width, LANES), f32),
-        in_specs=[smem, smem, anyspace, vmem, vmem, vmem],
+        in_specs=[smem, smem, vmem, vmem, vmem, vmem],
         out_specs=anyspace,
         scratch_shapes=[
-            pltpu.VMEM((19, width + 2, NZ, LANES), f32),
             pltpu.VMEM((19, NZ * width, LANES), f32),
-            pltpu.SemaphoreType.DMA,
             pltpu.SemaphoreType.DMA,
         ],
         compiler_params=params,

time: 28.8 us -> 25 us (0.87)
  Pallas kernels: 10.1 us -> 6.41 us
    pallas_call x1, Pallas kernels: 4.36 us -> 1.34 us  [per_device(): pl.pallas_call(body(pack_kernel, flows, shears, width), out_shape=[jax.Sh...]
    pallas_call x1, Pallas kernels: 4.33 us -> 3.62 us  [per_device(): pl.pallas_call(body(finish_kernel, flows, shears, width), out_shape=jax.S...]
  transfers between devices with their start and end apart: 3 -> 3, of which waited for: 1 -> 1; matrix products, arithmetic and copies ran while one was open for 0% -> 0% of each run, Pallas kernels for 5% -> 6%
where the time goes in v2:
time: 25 us; the launch traced here: 24.8 us
  starting transfers between devices  12.1 us (48%)
  Pallas kernels  6.41 us (26%)
  waiting for transfers between devices  5.01 us (20%)
  local copies, waits for them, and re-layouts  1.3 us (5%)
    all_to_all x1, starting transfers between devices, per_device(): rows = lax.all_to_all(rows, ('flow', 'shear'), 0, 0, tiled=True)  7.3 us
    ppermute x1, waiting for transfers between devices, per_device(): lax.ppermute(east, 'flow', [(i, (i + 1) % flows) for i in range(flows)])  5 us
    pallas_call x1, Pallas kernels, per_device(): pl.pallas_call(body(finish_kernel, flows, shears, width), out_shape=jax.S...  3.62 us
    ppermute x1, starting transfers between devices, per_device(): lax.ppermute(west, 'flow', [(i, (i - 1) % flows) for i in range(flows)])  2.96 us
    ppermute x1, starting transfers between devices, per_device(): lax.ppermute(east, 'flow', [(i, (i + 1) % flows) for i in range(flows)])  1.82 us
    pallas_call x1, Pallas kernels, per_device(): pl.pallas_call(body(local_kernel, width), out_shape=jax.ShapeDtypeStruct(...  1.46 us
    pallas_call x1, Pallas kernels, per_device(): pl.pallas_call(body(pack_kernel, flows, shears, width), out_shape=[jax.Sh...  1.34 us
    unnamed x8, local copies, waits for them, and re-layouts  1.3 us
  transfers between devices with their start and end apart: 3, of which 1 were waited for; matrix products, arithmetic and copies ran while one was open for 0% of the time, Pallas kernels for 6%

profile of v2, /device:TPU:0, one launch (start us, length us, event | category | flops | bytes accessed | tf_op | source)
XLA Modules:
  0.0 24.8 jit_solution(2638987948613218400)
XLA Ops:
  0.0 0.0 copy-start
  0.0 1.3 %copy-done = f32[19,8,16,128]{3,2,1,0:T(8,128)S(1)} copy-done((f32[19,8,16,128]{3,2,1,0:T(8,128)S(1)}, f32[19,8,16,128]{3,2,1,0:T(8,128)}, u32[]{:S(2)}) %copy-start) | copy-done | bytes 1245208
  1.3 0.0 copy-start.1
  1.3 1.3 %pack.1 = (f32[32,16,128]{2,1,0:T(8,128)}, f32[16,8,128]{2,1,0:T(8,128)S(1)}, f32[16,8,128]{2,1,0:T(8,128)S(1)}) custom-call(f32[19,128,128]{2,1,0:T(8,128)S(1)} %bitcast.2), custom_call_target="tpu_custom_call" | custom-call | tf_op jit(solution)/shard_map/pack/pallas_call | solution.py:389
  2.6 7.3 %all-to-all-start = ((f32[32,16,128]{2,1,0:T(8,128)}), f32[32,16,128]{2,1,0:T(8,128)S(1)}, u32[]{:S(2)}, u32[]{:S(2)}) async-start(f32[32,16,128]{2,1,0:T(8,128)} %get-tuple-element.8), calls=%async_computation | async-start | bytes 524288 | tf_op jit(solution)/shard_map/all_to_all | solution.py:401
  9.9 1.8 %collective-permute-start = (f32[16,8,128]{2,1,0:T(8,128)S(1)}, f32[16,8,128]{2,1,0:T(8,128)S(1)}, u32[]{:S(2)}, u32[]{:S(2)}) collective-permute-start(f32[16,8,128]{2,1,0:T(8,128)S(1)} %get-tuple-element.9), channel_id=1, source_target_pairs={{0,4},{4,8},{8,12},{12,16},{16,20},{20,24},{24,28},{28,0},{1,5},{5... | collective-permute-start | bytes 196616 | tf_op jit(solution)/shard_map/ppermute | solution.py:402
  11.8 0.0 copy-start.2
  11.8 0.0 copy-start.3
  11.8 3.0 %collective-permute-start.1 = (f32[16,8,128]{2,1,0:T(8,128)S(1)}, f32[16,8,128]{2,1,0:T(8,128)S(1)}, u32[]{:S(2)}, u32[]{:S(2)}) collective-permute-start(f32[16,8,128]{2,1,0:T(8,128)S(1)} %get-tuple-element.10), channel_id=1, source_target_pairs={{0,28},{4,0},{8,4},{12,8},{16,12},{20,16},{24,20},{28,24},{1,29},{... | collective-permute-start | bytes 196616 | tf_op jit(solution)/shard_map/ppermute | solution.py:403
  14.7 0.0 copy-done.1
  14.7 1.5 %local.1.refs_2_ = f32[19,18,8,128]{3,2,1,0:T(8,128)S(1)} custom-call(f32[19,128,128]{2,1,0:T(8,128)S(1)} %bitcast.3), custom_call_target="tpu_custom_call" | custom-call | flops 8000000 | bytes 2700000 | tf_op jit(solution)/shard_map/local/pallas_call | solution.py:404
  16.2 5.0 %collective-permute-done.refs_4_ = f32[16,8,128]{2,1,0:T(8,128)S(1)} collective-permute-done((f32[16,8,128]{2,1,0:T(8,128)S(1)}, f32[16,8,128]{2,1,0:T(8,128)S(1)}, u32[]{:S(2)}, u32[]{:S(2)}) %collective-permute-start) | collective-permute-done | bytes 65568 | tf_op jit(solution)/shard_map/ppermute | solution.py:402
  21.2 0.0 collective-permute-done.1.refs_5_
  21.2 0.0 all-to-all-done.refs_3_
  21.2 0.0 copy-done.2
  21.2 0.0 copy-done.3
  21.2 3.6 %finish.1 = f32[19,128,128]{2,1,0:T(8,128)} custom-call(s32[2]{0:T(128)S(1)} %copy-done.2, s32[2]{0:T(128)S(1)} %copy-done.3, f32[19,18,8,128]{3,2,1,0:T(8,128)S(1)} %local.1.refs_2_, f32[32,16,128]{2,1,0:T(8,128)S(1)} %all-to-all-done.refs_3_, f32[16,8,128]{2,1,0:T(8,128)S(1)} %collective-permute-done.refs_4_, f32[16,8,128]{2,1,0:T(8,128)S(1)} %collective-permute-done.1.refs_5_), custom_call_target="tpu_custom_call" | custom-call | tf_op jit(solution)/shard_map/finish/pallas_call | solution.py:413
Async XLA Ops:
  0.0 1.3 %copy-start = (f32[19,8,16,128]{3,2,1,0:T(8,128)S(1)}, f32[19,8,16,128]{3,2,1,0:T(8,128)}, u32[]{:S(2)}) copy-start(f32[19,8,16,128]{3,2,1,0:T(8,128)} %param.3) | copy-start | bytes 3735556
  1.3 13.4 %copy-start.1 = (f32[19,8,16,128]{3,2,1,0:T(8,128)S(1)}, f32[19,8,16,128]{3,2,1,0:T(8,128)}, u32[]{:S(2)}) copy-start(f32[19,8,16,128]{3,2,1,0:T(8,128)} %param.3) | copy-start | bytes 3735556
  2.6 18.6 %all-to-all-start = ((f32[32,16,128]{2,1,0:T(8,128)}), f32[32,16,128]{2,1,0:T(8,128)S(1)}, u32[]{:S(2)}, u32[]{:S(2)}) async-start(f32[32,16,128]{2,1,0:T(8,128)} %get-tuple-element.8), calls=%async_computation | async-start | bytes 524288 | tf_op jit(solution)/shard_map/all_to_all | solution.py:401
  9.9 11.2 %collective-permute-start = (f32[16,8,128]{2,1,0:T(8,128)S(1)}, f32[16,8,128]{2,1,0:T(8,128)S(1)}, u32[]{:S(2)}, u32[]{:S(2)}) collective-permute-start(f32[16,8,128]{2,1,0:T(8,128)S(1)} %get-tuple-element.9), channel_id=1, source_target_pairs={{0,4},{4,8},{8,12},{12,16},{16,20},{20,24},{24,28},{28,0},{1,5},{5... | collective-permute-start | bytes 196616 | tf_op jit(solution)/shard_map/ppermute | solution.py:402
  11.8 9.4 %copy-start.2 = (s32[2]{0:T(128)S(1)}, s32[2]{0:T(128)}, u32[]{:S(2)}) copy-start(s32[2]{0:T(128)} %refs_0_.1) | copy-start | bytes 28
  11.8 9.4 %copy-start.3 = (s32[2]{0:T(128)S(1)}, s32[2]{0:T(128)}, u32[]{:S(2)}) copy-start(s32[2]{0:T(128)} %refs_1_.1) | copy-start | bytes 28
  11.8 9.4 %collective-permute-start.1 = (f32[16,8,128]{2,1,0:T(8,128)S(1)}, f32[16,8,128]{2,1,0:T(8,128)S(1)}, u32[]{:S(2)}, u32[]{:S(2)}) collective-permute-start(f32[16,8,128]{2,1,0:T(8,128)S(1)} %get-tuple-element.10), channel_id=1, source_target_pairs={{0,28},{4,0},{8,4},{12,8},{16,12},{20,16},{24,20},{28,24},{1,29},{... | collective-permute-start | bytes 196616 | tf_op jit(solution)/shard_map/ppermute | solution.py:403

commit v3 on v2

--- a/solution.py
+++ b/solution.py
@@ -125,7 +125,7 @@
     return ref[q, pl.ds(x, NZ, stride=width), :]
 
 
-def pack_kernel(flows, shears, width, f_ref, rows_ref, east_ref, west_ref):
+def pack_kernel(flows, shears, width, f_ref, rows_ref, near_ref, far_ref):
     shear = lax.axis_index("shear")
     lane = lane_iota()
     boost_up = jnp.where(shear == shears - 1, -BOOST, 0.0).astype(jnp.float32)
@@ -179,18 +179,24 @@
     else:
         pl.loop(0, flows)(put)
 
-    for out, near, far, lanes in ((east_ref, width - 1, width - 2, EAST), (west_ref, 0, 1, WEST)):
-        for at, first in ((far, 0), (near, 5)):
+    packs = []
+    for near, far, lanes in ((width - 1, width - 2, EAST), (0, 1, WEST)):
+        planes = []
+        for at in (far, near):
             f = [column(f_ref, q, at, width) for q in range(19)]
             wanted = list(range(19)) if at == near else lanes
             post = relax(*moments(f), f, wanted)
             for q in wanted:
                 post[q] = roll_y(roll_z(post[q], VELOCITY[q][2]), VELOCITY[q][1])
-            for i, q in enumerate(lanes):
-                out[first + i] = post[q]
-            if at == near:
-                for i, s in enumerate(classes(post, "y")):
-                    out[10 + i] = s
+            planes += [post[q] for q in lanes]
+        still, plus, minus, still_z, plus_z, minus_z = classes(post, "y")
+        plus, plus_z = [jnp.where(lane == 0, 0.0, v) for v in (plus, plus_z)]
+        minus, minus_z = [jnp.where(lane == LANES - 1, 0.0, v) for v in (minus, minus_z)]
+        packs.append(planes + [still + (plus + minus), plus - minus, still_z + (plus_z + minus_z)])
+    even = lax.rem(lax.axis_index("flow"), 2) == 0
+    for i, (to_east, to_west) in enumerate(zip(*packs)):
+        near_ref[i] = jnp.where(even, to_east, to_west)
+        far_ref[i] = jnp.where(even, to_west, to_east)
 
 
 def local_kernel(width, f_ref, a_ref):
@@ -211,13 +217,14 @@
 
 
 def finish_kernel(
-    flows, shears, width, cells, weight, a_ref, rows_ref, west_ref, east_ref, out_hbm,
+    flows, shears, width, cells, weight, a_ref, rows_ref, far_ref, near_ref, out_hbm,
     out_ref, sem_out,
 ):
     flow = lax.axis_index("flow")
     shear = lax.axis_index("shear")
     lane = lane_iota()
     total_x = flows * width
+    even = lax.rem(flow, 2) == 0
     at_bottom = shear == 0
     at_top = shear == shears - 1
     above = lax.rem(shear + 1, shears)
@@ -297,71 +304,76 @@
 
     up1, up2 = side(True)
     down1, down2 = side(False)
-    ghosts1 = {**up1, **down1}
-    ghosts2 = {**up2, **down2}
     at_first = lane == 0
     at_last = lane == LANES - 1
-
-    def insert(v, ghosts, q, x):
-        cy = VELOCITY[q][1]
-        if cy == 0:
-            return v
-        g, slot = ghosts[q]
-        by = (0 if cy > 0 else LANES - 1) - ((x + BASE) * GAP + slot)
-        if isinstance(x, int):
-            moved = roll_y(g, by)
-        else:
-            moved = pltpu.roll(g, lax.rem(by + LANES, LANES), 1)
-        return jnp.where(at_first if cy > 0 else at_last, moved, v)
+    odd = lane % GAP == 1
+
+    def pairs(ups, downs, streamed):
+        found = []
+        for u, d in zip(UP, DOWN):
+            (gu, su), (gd, sd) = ups[u], downs[d]
+            along = [VELOCITY[q][0] * GAP if streamed else 0 for q in (u, d)]
+            found.append(jnp.where(odd, roll_y(gu, along[0] + 1 - su), roll_y(gd, along[1] - sd)))
+        return found
+
+    pairs1 = pairs(up1, down1, True)
+    pairs2 = pairs(up2, down2, False)
+
+    def beyond(found, x):
+        return [roll_y(v, -1 - (x + BASE) * GAP) for v in found]
+
+    def insert(v, q, edge):
+        if q in UP:
+            return jnp.where(at_first, edge[UP.index(q)], v)
+        if q in DOWN:
+            return jnp.where(at_last, edge[DOWN.index(q)], v)
+        return v
+
+    def from_west(i):
+        return jnp.where(even, far_ref[i], near_ref[i])
+
+    def from_east(i):
+        return jnp.where(even, near_ref[i], far_ref[i])
 
     def arrived(q, x):
-        if isinstance(x, int) and x == 0 and q in EAST:
-            return west_ref[5 + EAST.index(q)]
-        if isinstance(x, int) and x == width - 1 and q in WEST:
-            return east_ref[5 + WEST.index(q)]
+        if x == 0 and q in EAST:
+            return from_west(5 + EAST.index(q))
+        if x == width - 1 and q in WEST:
+            return from_east(5 + WEST.index(q))
         return a_ref[q, x + 1]
 
-    def put(q, x, post):
-        cx, cy, cz = VELOCITY[q]
-        v = insert(roll_y(roll_z(post[q], cz), cy), ghosts2, q, x)
-        out_ref[q, pl.ds(x + cx, NZ, stride=width), :] = v
-
-    def inner(x, keep):
-        f = [insert(arrived(q, x), ghosts1, q, x - VELOCITY[q][0]) for q in range(19)]
-        wanted = [q for q in range(19) if VELOCITY[q][0] != -keep or keep == 0]
-        post = relax(*moments(f), f, wanted)
-        for q in wanted:
-            put(q, x, post)
-
-    for x, halo, entering, leaving in ((-1, west_ref, EAST, WEST), (width, east_ref, WEST, EAST)):
-        cx = VELOCITY[entering[0]][0]
-        f = {q: insert(halo[i], ghosts1, q, x - cx) for i, q in enumerate(entering)}
+    def put(post, x):
+        edge = beyond(pairs2, x)
+        for q in post:
+            cx, cy, cz = VELOCITY[q]
+            if 0 <= x + cx < width:
+                v = insert(roll_y(roll_z(post[q], cz), cy), q, edge)
+                out_ref[q, pl.ds(x + cx, NZ, stride=width), :] = v
+
+    for x, halo, entering, leaving in ((-1, from_west, EAST, WEST), (width, from_east, WEST, EAST)):
+        edge = beyond(pairs1, x)
+        f = {q: insert(halo(i), q, edge) for i, q in enumerate(entering)}
         for q in leaving:
-            f[q] = insert(a_ref[q, x + 1], ghosts1, q, x + cx)
-
-        def edge_value(q):
-            g, slot = ghosts1[q]
-            return roll_y(g, (0 if VELOCITY[q][1] > 0 else LANES - 1) - ((x + BASE) * GAP + slot))
-
-        n, np_, nm = edge_value(3), edge_value(15), edge_value(17)
-        s, sm, sp = edge_value(4), edge_value(16), edge_value(18)
-        plus = jnp.where(at_first, n + np_ + nm, halo[11])
-        minus = jnp.where(at_last, s + sm + sp, halo[12])
-        plusz = jnp.where(at_first, np_ - nm, halo[14])
-        minusz = jnp.where(at_last, sp - sm, halo[15])
+            f[q] = insert(a_ref[q, x + 1], q, edge)
+        level, rising, falling = edge[0] + edge[3] + edge[4], edge[3], edge[4]
+        more = jnp.where(at_first | at_last, level, 0.0)
+        more_y = jnp.where(at_first, level, jnp.where(at_last, -level, 0.0))
+        turn = rising - falling
+        more_z = jnp.where(at_first, turn, jnp.where(at_last, -turn, 0.0))
         sum_e = f[1] + f[7] + f[9] + f[11] + f[13]
         sum_w = f[2] + f[8] + f[10] + f[12] + f[14]
-        rho = (halo[10] + plus + minus) + (sum_e + sum_w)
+        rho = (halo(10) + more) + (sum_e + sum_w)
         jx = sum_e - sum_w
-        jy = (plus - minus) + ((f[7] - f[8]) + (f[10] - f[9]))
-        jz = (halo[13] + plusz + minusz) + ((f[11] - f[12]) + (f[14] - f[13]))
-        post = relax(rho, jx, jy, jz, f, entering)
-        for q in entering:
-            put(q, x, post)
-
-    inner(0, 1)
-    pl.loop(1, width - 1, unroll=7)(lambda x: inner(x, 0))
-    inner(width - 1, -1)
+        jy = (halo(11) + more_y) + ((f[7] - f[8]) + (f[10] - f[9]))
+        jz = (halo(12) + more_z) + ((f[11] - f[12]) + (f[14] - f[13]))
+        put(relax(rho, jx, jy, jz, f, entering), x)
+
+    for x in range(width):
+        edge = beyond(pairs1, x)
+        f = [insert(arrived(q, x), q, edge) for q in range(19)]
+        post = relax(*moments(f), f, range(19))
+        put(post, x)
+
     store = pltpu.make_async_copy(out_ref, out_hbm, sem_out)
     store.start()
     store.wait()
@@ -373,7 +385,7 @@
     flows = lax.axis_size("flow")
     shears = lax.axis_size("shear")
     assert populations.shape[:2] == (19, NZ) and height == LANES
-    assert width * GAP == HALF and shears >= 3 and flows >= 3
+    assert width * GAP == HALF and shears >= 3 and flows >= 4 and flows % 2 == 0
     f32 = jnp.float32
     f = populations.reshape(19, NZ * width, height)
     vmem = pl.BlockSpec(memory_space=pltpu.VMEM)
@@ -386,12 +398,12 @@
     def body(kernel, *fixed):
         return lambda *refs: kernel(*fixed, *refs)
 
-    rows, east, west = pl.pallas_call(
+    rows, near, far = pl.pallas_call(
         body(pack_kernel, flows, shears, width),
         out_shape=[
             jax.ShapeDtypeStruct((devices, 2 * NZ, LANES), f32),
-            jax.ShapeDtypeStruct((16, NZ, LANES), f32),
-            jax.ShapeDtypeStruct((16, NZ, LANES), f32),
+            jax.ShapeDtypeStruct((13, NZ, LANES), f32),
+            jax.ShapeDtypeStruct((13, NZ, LANES), f32),
         ],
         in_specs=[vmem],
         out_specs=[vmem] * 3,
@@ -399,8 +411,8 @@
         name="pack",
     )(f)
     rows = lax.all_to_all(rows, ("flow", "shear"), 0, 0, tiled=True)
-    from_west = lax.ppermute(east, "flow", [(i, (i + 1) % flows) for i in range(flows)])
-    from_east = lax.ppermute(west, "flow", [(i, (i - 1) % flows) for i in range(flows)])
+    from_far = lax.ppermute(far, "flow", [(i, (i - 1 + i % 2 * 2) % flows) for i in range(flows)])
+    from_near = lax.ppermute(near, "flow", [(i, i + 1 - i % 2 * 2) for i in range(flows)])
     streamed = pl.pallas_call(
         body(local_kernel, width),
         out_shape=jax.ShapeDtypeStruct((19, width + 2, NZ, LANES), f32),
@@ -421,7 +433,7 @@
         ],
         compiler_params=params,
         name="finish",
-    )(le_cells, le_weight, streamed, rows, from_west, from_east)
+    )(le_cells, le_weight, streamed, rows, from_far, from_near)
     return out.reshape(populations.shape)
 
 

time: 25 us -> 24.1 us (0.964)
  Pallas kernels: 6.41 us -> 5.74 us
    pallas_call x1, Pallas kernels: 3.62 us -> 2.94 us  [per_device(): pl.pallas_call(body(finish_kernel, flows, shears, width), out_shape=jax.S...]
where the time goes in v3:
time: 24.1 us; the launch traced here: 23.9 us
  starting transfers between devices  11.9 us (49%)
  Pallas kernels  5.74 us (24%)
  waiting for transfers between devices  4.91 us (20%)
  local copies, waits for them, and re-layouts  1.3 us (5%)
    all_to_all x1, starting transfers between devices, per_device(): rows = lax.all_to_all(rows, ('flow', 'shear'), 0, 0, tiled=True)  7.3 us
    ppermute x1, waiting for transfers between devices, per_device(): lax.ppermute(far, 'flow', [(i, (i - 1 + i % 2 * 2) % flows) for i in rang...  4.91 us
    ppermute x1, starting transfers between devices, per_device(): lax.ppermute(far, 'flow', [(i, (i - 1 + i % 2 * 2) % flows) for i in rang...  4.6 us
    pallas_call x1, Pallas kernels, per_device(): pl.pallas_call(body(finish_kernel, flows, shears, width), out_shape=jax.S...  2.94 us
    pallas_call x1, Pallas kernels, per_device(): pl.pallas_call(body(local_kernel, width), out_shape=jax.ShapeDtypeStruct(...  1.46 us
    pallas_call x1, Pallas kernels, per_device(): pl.pallas_call(body(pack_kernel, flows, shears, width), out_shape=[jax.Sh...  1.34 us
    unnamed x8, local copies, waits for them, and re-layouts  1.3 us
  transfers between devices with their start and end apart: 3, of which 1 were waited for; matrix products, arithmetic and copies ran while one was open for 0% of the time, Pallas kernels for 6%

profile of v3, /device:TPU:0, one launch (start us, length us, event | category | flops | bytes accessed | tf_op | source)
XLA Modules:
  0.0 23.9 jit_solution(3677359763683279297)
XLA Ops:
  0.0 0.0 copy-start
  0.0 1.3 %copy-done = f32[19,8,16,128]{3,2,1,0:T(8,128)S(1)} copy-done((f32[19,8,16,128]{3,2,1,0:T(8,128)S(1)}, f32[19,8,16,128]{3,2,1,0:T(8,128)}, u32[]{:S(2)}) %copy-start) | copy-done | bytes 1245208
  1.3 0.0 copy-start.1
  1.3 1.3 %pack.1 = (f32[32,16,128]{2,1,0:T(8,128)}, f32[13,8,128]{2,1,0:T(8,128)S(1)}, f32[13,8,128]{2,1,0:T(8,128)S(1)}) custom-call(f32[19,128,128]{2,1,0:T(8,128)S(1)} %bitcast.2), custom_call_target="tpu_custom_call" | custom-call | tf_op jit(solution)/shard_map/pack/pallas_call | solution.py:401
  2.6 7.3 %all-to-all-start = ((f32[32,16,128]{2,1,0:T(8,128)}), f32[32,16,128]{2,1,0:T(8,128)S(1)}, u32[]{:S(2)}, u32[]{:S(2)}) async-start(f32[32,16,128]{2,1,0:T(8,128)} %get-tuple-element.8), calls=%async_computation | async-start | bytes 524288 | tf_op jit(solution)/shard_map/all_to_all | solution.py:413
  9.9 4.6 %collective-permute-start = (f32[13,8,128]{2,1,0:T(8,128)S(1)}, f32[13,8,128]{2,1,0:T(8,128)S(1)}, u32[]{:S(2)}, u32[]{:S(2)}) collective-permute-start(f32[13,8,128]{2,1,0:T(8,128)S(1)} %get-tuple-element.9), channel_id=1, source_target_pairs={{0,28},{4,8},{8,4},{12,16},{16,12},{20,24},{24,20},{28,0},{1,29},{... | collective-permute-start | bytes 159752 | tf_op jit(solution)/shard_map/ppermute | solution.py:414
  14.5 0.0 copy-start.2
  14.5 0.0 copy-start.3
  14.6 0.0 collective-permute-start.1
  14.6 0.0 copy-done.1
  14.6 1.5 %local.1.refs_2_ = f32[19,18,8,128]{3,2,1,0:T(8,128)S(1)} custom-call(f32[19,128,128]{2,1,0:T(8,128)S(1)} %bitcast.3), custom_call_target="tpu_custom_call" | custom-call | flops 8000000 | bytes 2700000 | tf_op jit(solution)/shard_map/local/pallas_call | solution.py:416
  16.0 4.9 %collective-permute-done.refs_4_ = f32[13,8,128]{2,1,0:T(8,128)S(1)} collective-permute-done((f32[13,8,128]{2,1,0:T(8,128)S(1)}, f32[13,8,128]{2,1,0:T(8,128)S(1)}, u32[]{:S(2)}, u32[]{:S(2)}) %collective-permute-start) | collective-permute-done | bytes 53280 | tf_op jit(solution)/shard_map/ppermute | solution.py:414
  20.9 0.0 collective-permute-done.1.refs_5_
  20.9 0.0 all-to-all-done.refs_3_
  20.9 0.0 copy-done.2
  20.9 0.0 copy-done.3
  21.0 2.9 %finish.1 = f32[19,128,128]{2,1,0:T(8,128)} custom-call(s32[2]{0:T(128)S(1)} %copy-done.2, s32[2]{0:T(128)S(1)} %copy-done.3, f32[19,18,8,128]{3,2,1,0:T(8,128)S(1)} %local.1.refs_2_, f32[32,16,128]{2,1,0:T(8,128)S(1)} %all-to-all-done.refs_3_, f32[13,8,128]{2,1,0:T(8,128)S(1)} %collective-permute-done.refs_4_, f32[13,8,128]{2,1,0:T(8,128)S(1)} %collective-permute-done.1.refs_5_), custom_call_target="tpu_custom_call" | custom-call | tf_op jit(solution)/shard_map/finish/pallas_call | solution.py:425
Async XLA Ops:
  0.0 1.3 %copy-start = (f32[19,8,16,128]{3,2,1,0:T(8,128)S(1)}, f32[19,8,16,128]{3,2,1,0:T(8,128)}, u32[]{:S(2)}) copy-start(f32[19,8,16,128]{3,2,1,0:T(8,128)} %param.3) | copy-start | bytes 3735556
  1.3 13.3 %copy-start.1 = (f32[19,8,16,128]{3,2,1,0:T(8,128)S(1)}, f32[19,8,16,128]{3,2,1,0:T(8,128)}, u32[]{:S(2)}) copy-start(f32[19,8,16,128]{3,2,1,0:T(8,128)} %param.3) | copy-start | bytes 3735556
  2.6 18.3 %all-to-all-start = ((f32[32,16,128]{2,1,0:T(8,128)}), f32[32,16,128]{2,1,0:T(8,128)S(1)}, u32[]{:S(2)}, u32[]{:S(2)}) async-start(f32[32,16,128]{2,1,0:T(8,128)} %get-tuple-element.8), calls=%async_computation | async-start | bytes 524288 | tf_op jit(solution)/shard_map/all_to_all | solution.py:413
  9.9 11.0 %collective-permute-start = (f32[13,8,128]{2,1,0:T(8,128)S(1)}, f32[13,8,128]{2,1,0:T(8,128)S(1)}, u32[]{:S(2)}, u32[]{:S(2)}) collective-permute-start(f32[13,8,128]{2,1,0:T(8,128)S(1)} %get-tuple-element.9), channel_id=1, source_target_pairs={{0,28},{4,8},{8,4},{12,16},{16,12},{20,24},{24,20},{28,0},{1,29},{... | collective-permute-start | bytes 159752 | tf_op jit(solution)/shard_map/ppermute | solution.py:414
  14.5 6.4 %copy-start.2 = (s32[2]{0:T(128)S(1)}, s32[2]{0:T(128)}, u32[]{:S(2)}) copy-start(s32[2]{0:T(128)} %refs_0_.1) | copy-start | bytes 28
  14.5 6.4 %copy-start.3 = (s32[2]{0:T(128)S(1)}, s32[2]{0:T(128)}, u32[]{:S(2)}) copy-start(s32[2]{0:T(128)} %refs_1_.1) | copy-start | bytes 28
  14.6 6.4 %collective-permute-start.1 = (f32[13,8,128]{2,1,0:T(8,128)S(1)}, f32[13,8,128]{2,1,0:T(8,128)S(1)}, u32[]{:S(2)}, u32[]{:S(2)}) collective-permute-start(f32[13,8,128]{2,1,0:T(8,128)S(1)} %get-tuple-element.10), channel_id=1, source_target_pairs={{0,4},{4,0},{8,12},{12,8},{16,20},{20,16},{24,28},{28,24},{1,5},{5... | collective-permute-start | bytes 159752 | tf_op jit(solution)/shard_map/ppermute | solution.py:415

commit v4 on v3

--- a/solution.py
+++ b/solution.py
@@ -368,15 +368,24 @@
         jz = (halo(12) + more_z) + ((f[11] - f[12]) + (f[14] - f[13]))
         put(relax(rho, jx, jy, jz, f, entering), x)
 
+    rows_of = (19, NZ, width, LANES)
+    half = width // 2
+    stores = [
+        pltpu.make_async_copy(
+            out_ref.reshape(rows_of).at[:, :, a : a + half], out_hbm.reshape(rows_of).at[:, :, a : a + half], sem_out.at[i]
+        )
+        for i, a in enumerate((0, half))
+    ]
     for x in range(width):
         edge = beyond(pairs1, x)
         f = [insert(arrived(q, x), q, edge) for q in range(19)]
         post = relax(*moments(f), f, range(19))
         put(post, x)
-
-    store = pltpu.make_async_copy(out_ref, out_hbm, sem_out)
-    store.start()
-    store.wait()
+        if x == half:
+            stores[0].start()
+    stores[1].start()
+    for store in stores:
+        store.wait()
 
 
 def per_device(populations, le_cells, le_weight):
@@ -425,11 +434,11 @@
     out = pl.pallas_call(
         body(finish_kernel, flows, shears, width),
         out_shape=jax.ShapeDtypeStruct((19, NZ * width, LANES), f32),
-        in_specs=[smem, smem, vmem, vmem, vmem, vmem],
+        in_specs=[vmem, vmem, vmem, vmem, vmem, vmem],
         out_specs=anyspace,
         scratch_shapes=[
             pltpu.VMEM((19, NZ * width, LANES), f32),
-            pltpu.SemaphoreType.DMA,
+            pltpu.SemaphoreType.DMA((2,)),
         ],
         compiler_params=params,
         name="finish",

time: 24.1 us -> 23.5 us (0.975)
  Pallas kernels: 5.74 us -> 5.13 us
    pallas_call x1, Pallas kernels: 2.94 us -> 2.33 us  [per_device(): pl.pallas_call(body(finish_kernel, flows, shears, width), out_shape=jax.S...]
where the time goes in v4:
time: 23.5 us; the launch traced here: 23.3 us
  starting transfers between devices  11.9 us (51%)
  Pallas kernels  5.13 us (22%)
  waiting for transfers between devices  4.91 us (21%)
  local copies, waits for them, and re-layouts  1.3 us (6%)
    all_to_all x1, starting transfers between devices, per_device(): rows = lax.all_to_all(rows, ('flow', 'shear'), 0, 0, tiled=True)  7.3 us
    ppermute x1, waiting for transfers between devices, per_device(): lax.ppermute(far, 'flow', [(i, (i - 1 + i % 2 * 2) % flows) for i in rang...  4.91 us
    ppermute x1, starting transfers between devices, per_device(): lax.ppermute(far, 'flow', [(i, (i - 1 + i % 2 * 2) % flows) for i in rang...  4.6 us
    pallas_call x1, Pallas kernels, per_device(): pl.pallas_call(body(finish_kernel, flows, shears, width), out_shape=jax.S...  2.33 us
    pallas_call x1, Pallas kernels, per_device(): pl.pallas_call(body(local_kernel, width), out_shape=jax.ShapeDtypeStruct(...  1.46 us
    pallas_call x1, Pallas kernels, per_device(): pl.pallas_call(body(pack_kernel, flows, shears, width), out_shape=[jax.Sh...  1.34 us
    unnamed x8, local copies, waits for them, and re-layouts  1.3 us
  transfers between devices with their start and end apart: 3, of which 1 were waited for; matrix products, arithmetic and copies ran while one was open for 0% of the time, Pallas kernels for 6%

profile of v4, /device:TPU:0, one launch (start us, length us, event | category | flops | bytes accessed | tf_op | source)
XLA Modules:
  0.0 23.3 jit_solution(16875288359641482525)
XLA Ops:
  0.0 0.0 copy-start
  0.0 1.3 %copy-done = f32[19,8,16,128]{3,2,1,0:T(8,128)S(1)} copy-done((f32[19,8,16,128]{3,2,1,0:T(8,128)S(1)}, f32[19,8,16,128]{3,2,1,0:T(8,128)}, u32[]{:S(2)}) %copy-start) | copy-done | bytes 1245208
  1.3 0.0 copy-start.1
  1.3 1.3 %pack.1 = (f32[32,16,128]{2,1,0:T(8,128)}, f32[13,8,128]{2,1,0:T(8,128)S(1)}, f32[13,8,128]{2,1,0:T(8,128)S(1)}) custom-call(f32[19,128,128]{2,1,0:T(8,128)S(1)} %bitcast.2), custom_call_target="tpu_custom_call" | custom-call | tf_op jit(solution)/shard_map/pack/pallas_call | solution.py:410
  2.6 7.3 %all-to-all-start = ((f32[32,16,128]{2,1,0:T(8,128)}), f32[32,16,128]{2,1,0:T(8,128)S(1)}, u32[]{:S(2)}, u32[]{:S(2)}) async-start(f32[32,16,128]{2,1,0:T(8,128)} %get-tuple-element.8), calls=%async_computation | async-start | bytes 524288 | tf_op jit(solution)/shard_map/all_to_all | solution.py:422
  9.9 4.6 %collective-permute-start = (f32[13,8,128]{2,1,0:T(8,128)S(1)}, f32[13,8,128]{2,1,0:T(8,128)S(1)}, u32[]{:S(2)}, u32[]{:S(2)}) collective-permute-start(f32[13,8,128]{2,1,0:T(8,128)S(1)} %get-tuple-element.9), channel_id=1, source_target_pairs={{0,28},{4,8},{8,4},{12,16},{16,12},{20,24},{24,20},{28,0},{1,29},{... | collective-permute-start | bytes 159752 | tf_op jit(solution)/shard_map/ppermute | solution.py:423
  14.5 0.0 copy-start.2
  14.5 0.0 copy-start.3
  14.6 0.0 collective-permute-start.1
  14.6 0.0 copy-done.1
  14.6 1.5 %local.1.refs_2_ = f32[19,18,8,128]{3,2,1,0:T(8,128)S(1)} custom-call(f32[19,128,128]{2,1,0:T(8,128)S(1)} %bitcast.3), custom_call_target="tpu_custom_call" | custom-call | flops 8000000 | bytes 2700000 | tf_op jit(solution)/shard_map/local/pallas_call | solution.py:425
  16.0 4.9 %collective-permute-done.refs_4_ = f32[13,8,128]{2,1,0:T(8,128)S(1)} collective-permute-done((f32[13,8,128]{2,1,0:T(8,128)S(1)}, f32[13,8,128]{2,1,0:T(8,128)S(1)}, u32[]{:S(2)}, u32[]{:S(2)}) %collective-permute-start) | collective-permute-done | bytes 53280 | tf_op jit(solution)/shard_map/ppermute | solution.py:423
  20.9 0.0 collective-permute-done.1.refs_5_
  20.9 0.0 all-to-all-done.refs_3_
  20.9 0.0 copy-done.2
  20.9 0.0 copy-done.3
  21.0 2.3 %finish.1 = f32[19,128,128]{2,1,0:T(8,128)} custom-call(s32[2]{0:T(128)S(1)} %copy-done.2, s32[2]{0:T(128)S(1)} %copy-done.3, f32[19,18,8,128]{3,2,1,0:T(8,128)S(1)} %local.1.refs_2_, f32[32,16,128]{2,1,0:T(8,128)S(1)} %all-to-all-done.refs_3_, f32[13,8,128]{2,1,0:T(8,128)S(1)} %collective-permute-done.refs_4_, f32[13,8,128]{2,1,0:T(8,128)S(1)} %collective-permute-done.1.refs_5_), custom_call_target="tpu_custom_call" | custom-call | tf_op jit(solution)/shard_map/finish/pallas_call | solution.py:434
Async XLA Ops:
  0.0 1.3 %copy-start = (f32[19,8,16,128]{3,2,1,0:T(8,128)S(1)}, f32[19,8,16,128]{3,2,1,0:T(8,128)}, u32[]{:S(2)}) copy-start(f32[19,8,16,128]{3,2,1,0:T(8,128)} %param.3) | copy-start | bytes 3735556
  1.3 13.3 %copy-start.1 = (f32[19,8,16,128]{3,2,1,0:T(8,128)S(1)}, f32[19,8,16,128]{3,2,1,0:T(8,128)}, u32[]{:S(2)}) copy-start(f32[19,8,16,128]{3,2,1,0:T(8,128)} %param.3) | copy-start | bytes 3735556
  2.6 18.3 %all-to-all-start = ((f32[32,16,128]{2,1,0:T(8,128)}), f32[32,16,128]{2,1,0:T(8,128)S(1)}, u32[]{:S(2)}, u32[]{:S(2)}) async-start(f32[32,16,128]{2,1,0:T(8,128)} %get-tuple-element.8), calls=%async_computation | async-start | bytes 524288 | tf_op jit(solution)/shard_map/all_to_all | solution.py:422
  9.9 11.0 %collective-permute-start = (f32[13,8,128]{2,1,0:T(8,128)S(1)}, f32[13,8,128]{2,1,0:T(8,128)S(1)}, u32[]{:S(2)}, u32[]{:S(2)}) collective-permute-start(f32[13,8,128]{2,1,0:T(8,128)S(1)} %get-tuple-element.9), channel_id=1, source_target_pairs={{0,28},{4,8},{8,4},{12,16},{16,12},{20,24},{24,20},{28,0},{1,29},{... | collective-permute-start | bytes 159752 | tf_op jit(solution)/shard_map/ppermute | solution.py:423
  14.5 6.4 %copy-start.2 = (s32[2]{0:T(128)S(1)}, s32[2]{0:T(128)}, u32[]{:S(2)}) copy-start(s32[2]{0:T(128)} %refs_0_.1) | copy-start | bytes 28
  14.5 6.4 %copy-start.3 = (s32[2]{0:T(128)S(1)}, s32[2]{0:T(128)}, u32[]{:S(2)}) copy-start(s32[2]{0:T(128)} %refs_1_.1) | copy-start | bytes 28
  14.6 6.4 %collective-permute-start.1 = (f32[13,8,128]{2,1,0:T(8,128)S(1)}, f32[13,8,128]{2,1,0:T(8,128)S(1)}, u32[]{:S(2)}, u32[]{:S(2)}) collective-permute-start(f32[13,8,128]{2,1,0:T(8,128)S(1)} %get-tuple-element.10), channel_id=1, source_target_pairs={{0,4},{4,0},{8,12},{12,8},{16,20},{20,16},{24,28},{28,24},{1,5},{5... | collective-permute-start | bytes 159752 | tf_op jit(solution)/shard_map/ppermute | solution.py:424

commit v5 on v4

--- a/solution.py
+++ b/solution.py
@@ -125,7 +125,7 @@
     return ref[q, pl.ds(x, NZ, stride=width), :]
 
 
-def pack_kernel(flows, shears, width, f_ref, rows_ref, near_ref, far_ref):
+def pack_kernel(shears, width, f_ref, side_ref, gap_ref, own_ref, near_ref, far_ref):
     shear = lax.axis_index("shear")
     lane = lane_iota()
     boost_up = jnp.where(shear == shears - 1, -BOOST, 0.0).astype(jnp.float32)
@@ -163,21 +163,12 @@
     downs = [post[q] + VELOCITY[q][0] * boost_down * rho if VELOCITY[q][0] else post[q] for q in DOWN]
     up0, up1 = groups(ups, [post[q] for q in UP], 1, 0)
     down0, down1 = groups(downs, [post[q] for q in DOWN], 2, 3)
-    above = lax.rem(shear + 1, shears)
-    below = lax.rem(shear + shears - 1, shears)
-
-    def put(at):
-        for to, first, second in ((above, up0, up1), (below, down0, down1), (shear, up0, down0)):
-            rows_ref[at * shears + to, 0:NZ, :] = first
-            rows_ref[at * shears + to, NZ : 2 * NZ, :] = second
-        for extra in range(2, shears - 1):
-            rows_ref[at * shears + lax.rem(shear + extra, shears)] = jnp.zeros((2 * NZ, LANES), jnp.float32)
-
-    if flows <= 8:
-        for at in range(flows):
-            put(at)
-    else:
-        pl.loop(0, flows)(put)
+    low = lax.rem(shear, 2) == 0
+    for at, (up, down) in enumerate(((up0, down0), (up1, down1))):
+        side_ref[at] = jnp.where(low, up, down)
+        gap_ref[at] = jnp.where(low, down, up)
+    own_ref[0] = jnp.where(low, down0, up0)
+    own_ref[1] = jnp.where(low, up0, down0)
 
     packs = []
     for near, far, lanes in ((width - 1, width - 2, EAST), (0, 1, WEST)):
@@ -199,6 +190,24 @@
         far_ref[i] = jnp.where(even, to_west, to_east)
 
 
+def message_kernel(near_ref, far_ref, side_ref, own_ref, near_out, far_out):
+    for out, planes in ((near_out, near_ref), (far_out, far_ref)):
+        out[0:13] = planes[...]
+        out[13:15] = side_ref[...]
+        out[15] = own_ref[1]
+
+
+def block_kernel(gap_ref, own_ref, out_ref):
+    out_ref[0, 0:2] = gap_ref[...]
+    out_ref[0, 2] = own_ref[0]
+
+
+def join_kernel(count, mine_ref, theirs_ref, out_ref):
+    mine = lax.rem(lax.div(lax.axis_index("flow"), count), 2)
+    out_ref[pl.ds(mine * count, count)] = mine_ref[...]
+    out_ref[pl.ds((1 - mine) * count, count)] = theirs_ref[...]
+
+
 def local_kernel(width, f_ref, a_ref):
     def step(x):
         f = [column(f_ref, q, x, width) for q in range(19)]
@@ -217,8 +226,8 @@
 
 
 def finish_kernel(
-    flows, shears, width, cells, weight, a_ref, rows_ref, far_ref, near_ref, out_hbm,
-    out_ref, sem_out,
+    flows, shears, width, cells, weight, a_ref, mine_ref, theirs_ref, side_ref, own_ref,
+    far_ref, near_ref, out_hbm, out_ref, sem_out,
 ):
     flow = lax.axis_index("flow")
     shear = lax.axis_index("shear")
@@ -227,19 +236,29 @@
     even = lax.rem(flow, 2) == 0
     at_bottom = shear == 0
     at_top = shear == shears - 1
-    above = lax.rem(shear + 1, shears)
-    below = lax.rem(shear + shears - 1, shears)
+    half_flows = flows // 2
+    my_half = lax.div(flow, half_flows)
     k1, k2 = cells[0], cells[1]
     frac = [weight[s].astype(jnp.float32) / WEIGHT_DENOM for s in range(2)]
     one, zero = jnp.float32(1.0), jnp.float32(0.0)
 
-    def window(start, source, vreg, half):
+    def from_west(i):
+        return jnp.where(even, far_ref[i], near_ref[i])
+
+    def from_east(i):
+        return jnp.where(even, near_ref[i], far_ref[i])
+
+    def gathered(block, vreg):
+        at = lax.rem(block, half_flows)
+        return jnp.where(lax.div(block, half_flows) == my_half, mine_ref[at, vreg], theirs_ref[at, vreg])
+
+    def window(start, shifted, vreg, half):
         first = lax.rem(flow * width + start - BASE + 2 * total_x, total_x)
         block = lax.div(first, width)
         skip = (first - block * width) * GAP
+        beside = (from_west(13 + vreg), side_ref[vreg] if vreg < 2 else own_ref[1], from_east(13 + vreg))
         a, b, c = [
-            rows_ref[lax.rem(block + k, flows) * shears + source, vreg * NZ : (vreg + 1) * NZ, :]
-            for k in range(3)
+            jnp.where(shifted, gathered(lax.rem(block + k, flows), vreg), beside[k]) for k in range(3)
         ]
         if half:
             a, c = roll_y(a, HALF), roll_y(c, HALF)
@@ -252,7 +271,8 @@
         lanes = UP if upward else DOWN
         others = DOWN if upward else UP
         active = at_bottom if upward else at_top
-        source = below if upward else above
+        low = lax.rem(shear, 2) == 0
+        shifted = low if upward else jnp.logical_not(low)
 
         def starts(k, low):
             return k if low else -k - 1
@@ -267,12 +287,11 @@
         start1 = jnp.where(active, starts(k1, upward), 0)
         start2 = jnp.where(active, starts(k2, upward), 0)
         start3 = jnp.where(active, starts(k2, upward) + starts(k1, not upward), 0)
-        near = [mixed(window(start1, source, 0, h), coefs(0, upward)) for h in range(2)]
+        near = [mixed(window(start1, shifted, 0, h), coefs(0, upward)) for h in range(2)]
         ghost1 = {q: (near[i // GAP], i % GAP) for i, q in enumerate(lanes)}
-        packs = [None] + [window(start2, source, v, h) for v, h in ((0, 1), (1, 0), (1, 1))]
+        packs = [None] + [window(start2, shifted, v, h) for v, h in ((0, 1), (1, 0), (1, 1))]
         pair3 = coefs(0, not upward)
-        own = 1 if upward else 0
-        back = [mixed(window(start3, shear, own, h), pair3) for h in range(2)]
+        back = [mixed(window(start3, shifted, 2, h), pair3) for h in range(2)]
 
         def plane(at, by):
             return roll_y(packs[at // GAP], by * GAP - at % GAP)
@@ -329,12 +348,6 @@
             return jnp.where(at_last, edge[DOWN.index(q)], v)
         return v
 
-    def from_west(i):
-        return jnp.where(even, far_ref[i], near_ref[i])
-
-    def from_east(i):
-        return jnp.where(even, near_ref[i], far_ref[i])
-
     def arrived(q, x):
         if x == 0 and q in EAST:
             return from_west(5 + EAST.index(q))
@@ -394,7 +407,7 @@
     flows = lax.axis_size("flow")
     shears = lax.axis_size("shear")
     assert populations.shape[:2] == (19, NZ) and height == LANES
-    assert width * GAP == HALF and shears >= 3 and flows >= 4 and flows % 2 == 0
+    assert width * GAP == HALF and shears >= 4 and shears % 2 == 0 and flows >= 4 and flows & (flows - 1) == 0
     f32 = jnp.float32
     f = populations.reshape(19, NZ * width, height)
     vmem = pl.BlockSpec(memory_space=pltpu.VMEM)
@@ -402,26 +415,39 @@
     hbm = pl.BlockSpec(memory_space=pltpu.HBM)
     smem = pl.BlockSpec(memory_space=pltpu.SMEM)
     params = pltpu.CompilerParams(vmem_limit_bytes=32 * 1024 * 1024)
-    devices = flows * shears
 
     def body(kernel, *fixed):
         return lambda *refs: kernel(*fixed, *refs)
 
-    rows, near, far = pl.pallas_call(
-        body(pack_kernel, flows, shears, width),
-        out_shape=[
-            jax.ShapeDtypeStruct((devices, 2 * NZ, LANES), f32),
-            jax.ShapeDtypeStruct((13, NZ, LANES), f32),
-            jax.ShapeDtypeStruct((13, NZ, LANES), f32),
-        ],
-        in_specs=[vmem],
-        out_specs=[vmem] * 3,
-        compiler_params=params,
-        name="pack",
-    )(f)
-    rows = lax.all_to_all(rows, ("flow", "shear"), 0, 0, tiled=True)
-    from_far = lax.ppermute(far, "flow", [(i, (i - 1 + i % 2 * 2) % flows) for i in range(flows)])
-    from_near = lax.ppermute(near, "flow", [(i, i + 1 - i % 2 * 2) for i in range(flows)])
+    def vregs(*counts):
+        return jax.ShapeDtypeStruct((*counts, NZ, LANES), f32)
+
+    def call(name, kernel, outs, *arrays):
+        return pl.pallas_call(
+            kernel, out_shape=outs, in_specs=[vmem] * len(arrays),
+            out_specs=[vmem] * len(outs) if isinstance(outs, list) else vmem,
+            compiler_params=params, name=name,
+        )(*arrays)
+
+    def swap(x, axis, partner):
+        return lax.ppermute(x, axis, [(i, partner(i)) for i in range(lax.axis_size(axis))])
+
+    side, gap, own, near, far = call(
+        "pack", body(pack_kernel, shears, width), [vregs(2), vregs(2), vregs(2), vregs(13), vregs(13)], f
+    )
+    side = swap(side, "shear", lambda i: i ^ 1)
+    gap = swap(gap, "shear", lambda i: (i - 1 + i % 2 * 2) % shears)
+    mine = call("block", block_kernel, vregs(1, 3), gap, own)
+    near, far = call("message", message_kernel, [vregs(16), vregs(16)], near, far, side, own)
+    from_far = swap(far, "flow", lambda i: (i - 1 + i % 2 * 2) % flows)
+    count = 1
+    while True:
+        theirs = swap(mine, "flow", lambda i: i ^ count)
+        if count * 2 == flows:
+            break
+        mine = call("join", body(join_kernel, count), vregs(count * 2, 3), mine, theirs)
+        count *= 2
+    from_near = swap(near, "flow", lambda i: i ^ 1)
     streamed = pl.pallas_call(
         body(local_kernel, width),
         out_shape=jax.ShapeDtypeStruct((19, width + 2, NZ, LANES), f32),
@@ -434,7 +460,7 @@
     out = pl.pallas_call(
         body(finish_kernel, flows, shears, width),
         out_shape=jax.ShapeDtypeStruct((19, NZ * width, LANES), f32),
-        in_specs=[vmem, vmem, vmem, vmem, vmem, vmem],
+        in_specs=[vmem] * 9,
         out_specs=anyspace,
         scratch_shapes=[
             pltpu.VMEM((19, NZ * width, LANES), f32),
@@ -442,7 +468,7 @@
         ],
         compiler_params=params,
         name="finish",
-    )(le_cells, le_weight, streamed, rows, from_far, from_near)
+    )(le_cells, le_weight, streamed, mine, theirs, side, own, from_far, from_near)
     return out.reshape(populations.shape)
 
 

time: 23.5 us -> 22.9 us (0.974)
  Pallas kernels: 5.13 us -> 4.5 us
  waiting for transfers between devices: 4.91 us -> 5.24 us
    all_to_all x1 -> x0, starting transfers between devices: 7.3 us -> none  [per_device(): rows = lax.all_to_all(rows, ('flow', 'shear'), 0, 0, tiled=True)]
    ppermute x2 -> x7, starting transfers between devices: 4.6 us -> 11.7 us  [swap(): lax.ppermute(x, axis, [(i, partner(i)) for i in range(lax.axis_size(axis))])]
    pallas_call x1 -> x5, Pallas kernels: 1.34 us -> 0.68 us  [call(): pl.pallas_call(kernel, out_shape=outs, in_specs=[vmem] * len(arrays), out...]
    ppermute x2 -> x7, waiting for transfers between devices: 4.91 us -> 5.24 us  [swap(): lax.ppermute(x, axis, [(i, partner(i)) for i in range(lax.axis_size(axis))])]
  transfers between devices with their start and end apart: 3 -> 7, of which waited for: 1 -> 5; matrix products, arithmetic and copies ran while one was open for 0% -> 0% of each run, Pallas kernels for 6% -> 7%
where the time goes in v5:
time: 22.9 us; the launch traced here: 22.8 us
  starting transfers between devices  11.7 us (51%)
  waiting for transfers between devices  5.24 us (23%)
  Pallas kernels  4.5 us (20%)
  local copies, waits for them, and re-layouts  1.31 us (6%)
    ppermute x7, starting transfers between devices, swap(): lax.ppermute(x, axis, [(i, partner(i)) for i in range(lax.axis_size(axis))])  11.7 us
    ppermute x7, waiting for transfers between devices, swap(): lax.ppermute(x, axis, [(i, partner(i)) for i in range(lax.axis_size(axis))])  5.24 us
    pallas_call x1, Pallas kernels, per_device(): pl.pallas_call(body(finish_kernel, flows, shears, width), out_shape=jax.S...  2.36 us
    pallas_call x1, Pallas kernels, per_device(): pl.pallas_call(body(local_kernel, width), out_shape=jax.ShapeDtypeStruct(...  1.46 us
    unnamed x8, local copies, waits for them, and re-layouts  1.31 us
    pallas_call x5, Pallas kernels, call(): pl.pallas_call(kernel, out_shape=outs, in_specs=[vmem] * len(arrays), out...  0.68 us
  transfers between devices with their start and end apart: 7, of which 5 were waited for; matrix products, arithmetic and copies ran while one was open for 0% of the time, Pallas kernels for 7%

profile of v5, /device:TPU:0, one launch (start us, length us, event | category | flops | bytes accessed | tf_op | source)
XLA Modules:
  0.0 22.8 jit_solution(12305701810227554714)
XLA Ops:
  0.0 0.0 copy-start
  0.0 1.3 %copy-done = f32[19,8,16,128]{3,2,1,0:T(8,128)S(1)} copy-done((f32[19,8,16,128]{3,2,1,0:T(8,128)S(1)}, f32[19,8,16,128]{3,2,1,0:T(8,128)}, u32[]{:S(2)}) %copy-start) | copy-done | bytes 1245208
  1.3 0.0 copy-start.1
  1.3 0.7 %pack.1 = (f32[2,8,128]{2,1,0:T(8,128)S(1)}, f32[2,8,128]{2,1,0:T(8,128)S(1)}, f32[2,8,128]{2,1,0:T(8,128)S(1)}, f32[13,8,128]{2,1,0:T(8,128)S(1)}, f32[13,8,128]{2,1,0:T(8,128)S(1)}) custom-call(f32[19,128,128]{2,1,0:T(8,128)S(1)} %bitcast.2), custom_call_target="tpu_custom_call" | custom-call | tf_op jit(solution)/shard_map/pack/pallas_call | solution.py:426
  2.0 2.5 %collective-permute-start = (f32[2,8,128]{2,1,0:T(8,128)S(1)}, f32[2,8,128]{2,1,0:T(8,128)S(1)}, u32[]{:S(2)}, u32[]{:S(2)}) collective-permute-start(f32[2,8,128]{2,1,0:T(8,128)S(1)} %get-tuple-element.12), channel_id=1, source_target_pairs={{0,3},{1,2},{2,1},{3,0},{4,7},{5,6},{6,5},{7,4},{8,11},{9,10},{10,... | collective-permute-start | bytes 24584 | tf_op jit(solution)/shard_map/ppermute | solution.py:433
  4.4 1.4 %collective-permute-done.gap_ref = f32[2,8,128]{2,1,0:T(8,128)S(1)} collective-permute-done((f32[2,8,128]{2,1,0:T(8,128)S(1)}, f32[2,8,128]{2,1,0:T(8,128)S(1)}, u32[]{:S(2)}, u32[]{:S(2)}) %collective-permute-start) | collective-permute-done | bytes 8224 | tf_op jit(solution)/shard_map/ppermute | solution.py:433
  5.8 2.3 %collective-permute-start.1 = (f32[1,3,8,128]{3,2,1,0:T(8,128)S(1)}, f32[1,3,8,128]{3,2,1,0:T(8,128)S(1)}, u32[]{:S(2)}, u32[]{:S(2)}) collective-permute-start(f32[1,3,8,128]{3,2,1,0:T(8,128)S(1)} %block.1.refs_0_), channel_id=1, source_target_pairs={{0,4},{4,0},{8,12},{12,8},{16,20},{20,16},{24,28},{28,24},{1,5},{5... | collective-permute-start | bytes 36872 | tf_op jit(solution)/shard_map/ppermute | solution.py:433
  8.0 0.0 collective-permute-start.4
  8.1 1.7 %collective-permute-done.1.refs_1_ = f32[1,3,8,128]{3,2,1,0:T(8,128)S(1)} collective-permute-done((f32[1,3,8,128]{3,2,1,0:T(8,128)S(1)}, f32[1,3,8,128]{3,2,1,0:T(8,128)S(1)}, u32[]{:S(2)}, u32[]{:S(2)}) %collective-permute-start.1) | collective-permute-done | bytes 12320 | tf_op jit(solution)/shard_map/ppermute | solution.py:433
  9.7 2.1 %collective-permute-start.2 = (f32[2,3,8,128]{3,2,1,0:T(8,128)S(1)}, f32[2,3,8,128]{3,2,1,0:T(8,128)S(1)}, u32[]{:S(2)}, u32[]{:S(2)}) collective-permute-start(f32[2,3,8,128]{3,2,1,0:T(8,128)S(1)} %join.2.refs_0_), channel_id=1, source_target_pairs={{0,8},{4,12},{8,0},{12,4},{16,24},{20,28},{24,16},{28,20},{1,9},{5... | collective-permute-start | bytes 73736 | tf_op jit(solution)/shard_map/ppermute | solution.py:433
  11.8 0.0 collective-permute-done.4.side_ref.refs_5_
  11.9 3.5 %collective-permute-start.5 = (f32[16,8,128]{2,1,0:T(8,128)S(1)}, f32[16,8,128]{2,1,0:T(8,128)S(1)}, u32[]{:S(2)}, u32[]{:S(2)}) collective-permute-start(f32[16,8,128]{2,1,0:T(8,128)S(1)} %get-tuple-element.17), channel_id=1, source_target_pairs={{0,28},{4,8},{8,4},{12,16},{16,12},{20,24},{24,20},{28,0},{1,29},{... | collective-permute-start | bytes 196616 | tf_op jit(solution)/shard_map/ppermute | solution.py:433
  15.3 0.0 collective-permute-start.6
  15.3 0.0 collective-permute-done.2.refs_1_
  15.3 0.0 copy-start.2
  15.4 0.0 copy-start.3
  15.4 1.4 %collective-permute-start.3 = (f32[4,3,8,128]{3,2,1,0:T(8,128)S(1)}, f32[4,3,8,128]{3,2,1,0:T(8,128)S(1)}, u32[]{:S(2)}, u32[]{:S(2)}) collective-permute-start(f32[4,3,8,128]{3,2,1,0:T(8,128)S(1)} %join.3.refs_3_), channel_id=1, source_target_pairs={{0,16},{4,20},{8,24},{12,28},{16,0},{20,4},{24,8},{28,12},{1,17},{... | collective-permute-start | bytes 147464 | tf_op jit(solution)/shard_map/ppermute | solution.py:433
  16.8 0.0 copy-done.1
  16.8 1.5 %local.1.refs_2_ = f32[19,18,8,128]{3,2,1,0:T(8,128)S(1)} custom-call(f32[19,128,128]{2,1,0:T(8,128)S(1)} %bitcast.3), custom_call_target="tpu_custom_call" | custom-call | flops 8000000 | bytes 2700000 | tf_op jit(solution)/shard_map/local/pallas_call | solution.py:451
  18.2 0.8 %collective-permute-done.5.refs_7_ = f32[16,8,128]{2,1,0:T(8,128)S(1)} collective-permute-done((f32[16,8,128]{2,1,0:T(8,128)S(1)}, f32[16,8,128]{2,1,0:T(8,128)S(1)}, u32[]{:S(2)}, u32[]{:S(2)}) %collective-permute-start.5) | collective-permute-done | bytes 65568 | tf_op jit(solution)/shard_map/ppermute | solution.py:433
  19.0 0.6 %collective-permute-done.6.refs_8_ = f32[16,8,128]{2,1,0:T(8,128)S(1)} collective-permute-done((f32[16,8,128]{2,1,0:T(8,128)S(1)}, f32[16,8,128]{2,1,0:T(8,128)S(1)}, u32[]{:S(2)}, u32[]{:S(2)}) %collective-permute-start.6) | collective-permute-done | bytes 65568 | tf_op jit(solution)/shard_map/ppermute | solution.py:433
  19.6 0.8 %collective-permute-done.3.refs_4_ = f32[4,3,8,128]{3,2,1,0:T(8,128)S(1)} collective-permute-done((f32[4,3,8,128]{3,2,1,0:T(8,128)S(1)}, f32[4,3,8,128]{3,2,1,0:T(8,128)S(1)}, u32[]{:S(2)}, u32[]{:S(2)}) %collective-permute-start.3) | collective-permute-done | bytes 49184 | tf_op jit(solution)/shard_map/ppermute | solution.py:433
  20.4 0.0 copy-done.2
  20.4 0.0 copy-done.3
  20.4 2.4 %finish.1 = f32[19,128,128]{2,1,0:T(8,128)} custom-call(s32[2]{0:T(128)S(1)} %copy-done.2, s32[2]{0:T(128)S(1)} %copy-done.3, f32[19,18,8,128]{3,2,1,0:T(8,128)S(1)} %local.1.refs_2_, f32[4,3,8,128]{3,2,1,0:T(8,128)S(1)} %join.3.refs_3_, f32[4,3,8,128]{3,2,1,0:T(8,128)S(1)} %collective-permute-done.3.refs_4_, ...), custom_call_target="tpu_custom_call" | custom-call | tf_op jit(solution)/shard_map/finish/pallas_call | solution.py:460
  (4 shorter events, 0.0 us)
Async XLA Ops:
  0.0 1.3 %copy-start = (f32[19,8,16,128]{3,2,1,0:T(8,128)S(1)}, f32[19,8,16,128]{3,2,1,0:T(8,128)}, u32[]{:S(2)}) copy-start(f32[19,8,16,128]{3,2,1,0:T(8,128)} %param.3) | copy-start | bytes 3735556
  1.3 15.5 %copy-start.1 = (f32[19,8,16,128]{3,2,1,0:T(8,128)S(1)}, f32[19,8,16,128]{3,2,1,0:T(8,128)}, u32[]{:S(2)}) copy-start(f32[19,8,16,128]{3,2,1,0:T(8,128)} %param.3) | copy-start | bytes 3735556
  2.0 3.8 %collective-permute-start = (f32[2,8,128]{2,1,0:T(8,128)S(1)}, f32[2,8,128]{2,1,0:T(8,128)S(1)}, u32[]{:S(2)}, u32[]{:S(2)}) collective-permute-start(f32[2,8,128]{2,1,0:T(8,128)S(1)} %get-tuple-element.12), channel_id=1, source_target_pairs={{0,3},{1,2},{2,1},{3,0},{4,7},{5,6},{6,5},{7,4},{8,11},{9,10},{10,... | collective-permute-start | bytes 24584 | tf_op jit(solution)/shard_map/ppermute | solution.py:433
  5.8 3.9 %collective-permute-start.1 = (f32[1,3,8,128]{3,2,1,0:T(8,128)S(1)}, f32[1,3,8,128]{3,2,1,0:T(8,128)S(1)}, u32[]{:S(2)}, u32[]{:S(2)}) collective-permute-start(f32[1,3,8,128]{3,2,1,0:T(8,128)S(1)} %block.1.refs_0_), channel_id=1, source_target_pairs={{0,4},{4,0},{8,12},{12,8},{16,20},{20,16},{24,28},{28,24},{1,5},{5... | collective-permute-start | bytes 36872 | tf_op jit(solution)/shard_map/ppermute | solution.py:433
  8.0 3.8 %collective-permute-start.4 = (f32[2,8,128]{2,1,0:T(8,128)S(1)}, f32[2,8,128]{2,1,0:T(8,128)S(1)}, u32[]{:S(2)}, u32[]{:S(2)}) collective-permute-start(f32[2,8,128]{2,1,0:T(8,128)S(1)} %get-tuple-element.14), channel_id=1, source_target_pairs={{0,1},{1,0},{2,3},{3,2},{4,5},{5,4},{6,7},{7,6},{8,9},{9,8},{10,11... | collective-permute-start | bytes 24584 | tf_op jit(solution)/shard_map/ppermute | solution.py:433
  9.7 5.6 %collective-permute-start.2 = (f32[2,3,8,128]{3,2,1,0:T(8,128)S(1)}, f32[2,3,8,128]{3,2,1,0:T(8,128)S(1)}, u32[]{:S(2)}, u32[]{:S(2)}) collective-permute-start(f32[2,3,8,128]{3,2,1,0:T(8,128)S(1)} %join.2.refs_0_), channel_id=1, source_target_pairs={{0,8},{4,12},{8,0},{12,4},{16,24},{20,28},{24,16},{28,20},{1,9},{5... | collective-permute-start | bytes 73736 | tf_op jit(solution)/shard_map/ppermute | solution.py:433
  11.9 7.2 %collective-permute-start.5 = (f32[16,8,128]{2,1,0:T(8,128)S(1)}, f32[16,8,128]{2,1,0:T(8,128)S(1)}, u32[]{:S(2)}, u32[]{:S(2)}) collective-permute-start(f32[16,8,128]{2,1,0:T(8,128)S(1)} %get-tuple-element.17), channel_id=1, source_target_pairs={{0,28},{4,8},{8,4},{12,16},{16,12},{20,24},{24,20},{28,0},{1,29},{... | collective-permute-start | bytes 196616 | tf_op jit(solution)/shard_map/ppermute | solution.py:433
  15.3 4.3 %collective-permute-start.6 = (f32[16,8,128]{2,1,0:T(8,128)S(1)}, f32[16,8,128]{2,1,0:T(8,128)S(1)}, u32[]{:S(2)}, u32[]{:S(2)}) collective-permute-start(f32[16,8,128]{2,1,0:T(8,128)S(1)} %get-tuple-element.18), channel_id=1, source_target_pairs={{0,4},{4,0},{8,12},{12,8},{16,20},{20,16},{24,28},{28,24},{1,5},{5... | collective-permute-start | bytes 196616 | tf_op jit(solution)/shard_map/ppermute | solution.py:433
  15.3 5.1 %copy-start.2 = (s32[2]{0:T(128)S(1)}, s32[2]{0:T(128)}, u32[]{:S(2)}) copy-start(s32[2]{0:T(128)} %refs_0_.1) | copy-start | bytes 28
  15.4 5.1 %copy-start.3 = (s32[2]{0:T(128)S(1)}, s32[2]{0:T(128)}, u32[]{:S(2)}) copy-start(s32[2]{0:T(128)} %refs_1_.1) | copy-start | bytes 28
  15.4 5.1 %collective-permute-start.3 = (f32[4,3,8,128]{3,2,1,0:T(8,128)S(1)}, f32[4,3,8,128]{3,2,1,0:T(8,128)S(1)}, u32[]{:S(2)}, u32[]{:S(2)}) collective-permute-start(f32[4,3,8,128]{3,2,1,0:T(8,128)S(1)} %join.3.refs_3_), channel_id=1, source_target_pairs={{0,16},{4,20},{8,24},{12,28},{16,0},{20,4},{24,8},{28,12},{1,17},{... | collective-permute-start | bytes 147464 | tf_op jit(solution)/shard_map/ppermute | solution.py:433

commit v6 on v5

--- a/solution.py
+++ b/solution.py
@@ -121,6 +121,10 @@
     ]
 
 
+def gather_order(flows):
+    return [1] + [2**k for k in range(flows.bit_length() - 2, 0, -1)]
+
+
 def column(ref, q, x, width):
     return ref[q, pl.ds(x, NZ, stride=width), :]
 
@@ -202,8 +206,9 @@
     out_ref[0, 2] = own_ref[0]
 
 
-def join_kernel(count, mine_ref, theirs_ref, out_ref):
-    mine = lax.rem(lax.div(lax.axis_index("flow"), count), 2)
+def join_kernel(apart, mine_ref, theirs_ref, out_ref):
+    count = mine_ref.shape[0]
+    mine = lax.rem(lax.div(lax.axis_index("flow"), apart), 2)
     out_ref[pl.ds(mine * count, count)] = mine_ref[...]
     out_ref[pl.ds((1 - mine) * count, count)] = theirs_ref[...]
 
@@ -236,8 +241,6 @@
     even = lax.rem(flow, 2) == 0
     at_bottom = shear == 0
     at_top = shear == shears - 1
-    half_flows = flows // 2
-    my_half = lax.div(flow, half_flows)
     k1, k2 = cells[0], cells[1]
     frac = [weight[s].astype(jnp.float32) / WEIGHT_DENOM for s in range(2)]
     one, zero = jnp.float32(1.0), jnp.float32(0.0)
@@ -249,8 +252,12 @@
         return jnp.where(even, near_ref[i], far_ref[i])
 
     def gathered(block, vreg):
-        at = lax.rem(block, half_flows)
-        return jnp.where(lax.div(block, half_flows) == my_half, mine_ref[at, vreg], theirs_ref[at, vreg])
+        *early, last = gather_order(flows)
+        at = 0
+        for place, apart in enumerate(early):
+            at = at + lax.rem(lax.div(block, apart), 2) * 2**place
+        same = lax.rem(lax.div(block, last), 2) == lax.rem(lax.div(flow, last), 2)
+        return jnp.where(same, mine_ref[at, vreg], theirs_ref[at, vreg])
 
     def window(start, shifted, vreg, half):
         first = lax.rem(flow * width + start - BASE + 2 * total_x, total_x)
@@ -440,13 +447,11 @@
     mine = call("block", block_kernel, vregs(1, 3), gap, own)
     near, far = call("message", message_kernel, [vregs(16), vregs(16)], near, far, side, own)
     from_far = swap(far, "flow", lambda i: (i - 1 + i % 2 * 2) % flows)
-    count = 1
-    while True:
-        theirs = swap(mine, "flow", lambda i: i ^ count)
-        if count * 2 == flows:
-            break
-        mine = call("join", body(join_kernel, count), vregs(count * 2, 3), mine, theirs)
-        count *= 2
+    *early, last = gather_order(flows)
+    for apart in early:
+        theirs = swap(mine, "flow", lambda i: i ^ apart)
+        mine = call("join", body(join_kernel, apart), vregs(2 * mine.shape[0], 3), mine, theirs)
+    theirs = swap(mine, "flow", lambda i: i ^ last)
     from_near = swap(near, "flow", lambda i: i ^ 1)
     streamed = pl.pallas_call(
         body(local_kernel, width),

time: 22.9 us -> 22.8 us (level)
  transfers between devices with their start and end apart: 7 -> 7, of which waited for: 5 -> 4; matrix products, arithmetic and copies ran while one was open for 0% -> 0% of each run, Pallas kernels for 7% -> 7%
where the time goes in v6:
time: 22.8 us; the launch traced here: 22.6 us
  starting transfers between devices  11.6 us (51%)
  waiting for transfers between devices  5.07 us (22%)
  Pallas kernels  4.57 us (20%)
  local copies, waits for them, and re-layouts  1.31 us (6%)
    ppermute x7, starting transfers between devices, swap(): lax.ppermute(x, axis, [(i, partner(i)) for i in range(lax.axis_size(axis))])  11.6 us
    ppermute x7, waiting for transfers between devices, swap(): lax.ppermute(x, axis, [(i, partner(i)) for i in range(lax.axis_size(axis))])  5.07 us
    pallas_call x1, Pallas kernels, per_device(): pl.pallas_call(body(finish_kernel, flows, shears, width), out_shape=jax.S...  2.43 us
    pallas_call x1, Pallas kernels, per_device(): pl.pallas_call(body(local_kernel, width), out_shape=jax.ShapeDtypeStruct(...  1.46 us
    unnamed x8, local copies, waits for them, and re-layouts  1.31 us
    pallas_call x5, Pallas kernels, call(): pl.pallas_call(kernel, out_shape=outs, in_specs=[vmem] * len(arrays), out...  0.68 us
  transfers between devices with their start and end apart: 7, of which 4 were waited for; matrix products, arithmetic and copies ran while one was open for 0% of the time, Pallas kernels for 7%

profile of v6, /device:TPU:0, one launch (start us, length us, event | category | flops | bytes accessed | tf_op | source)
XLA Modules:
  0.0 22.6 jit_solution(4151569175013816117)
XLA Ops:
  0.0 0.0 copy-start
  0.0 1.3 %copy-done = f32[19,8,16,128]{3,2,1,0:T(8,128)S(1)} copy-done((f32[19,8,16,128]{3,2,1,0:T(8,128)S(1)}, f32[19,8,16,128]{3,2,1,0:T(8,128)}, u32[]{:S(2)}) %copy-start) | copy-done | bytes 1245208
  1.3 0.0 copy-start.1
  1.3 0.7 %pack.1 = (f32[2,8,128]{2,1,0:T(8,128)S(1)}, f32[2,8,128]{2,1,0:T(8,128)S(1)}, f32[2,8,128]{2,1,0:T(8,128)S(1)}, f32[13,8,128]{2,1,0:T(8,128)S(1)}, f32[13,8,128]{2,1,0:T(8,128)S(1)}) custom-call(f32[19,128,128]{2,1,0:T(8,128)S(1)} %bitcast.2), custom_call_target="tpu_custom_call" | custom-call | tf_op jit(solution)/shard_map/pack/pallas_call | solution.py:433
  2.0 2.5 %collective-permute-start = (f32[2,8,128]{2,1,0:T(8,128)S(1)}, f32[2,8,128]{2,1,0:T(8,128)S(1)}, u32[]{:S(2)}, u32[]{:S(2)}) collective-permute-start(f32[2,8,128]{2,1,0:T(8,128)S(1)} %get-tuple-element.12), channel_id=1, source_target_pairs={{0,3},{1,2},{2,1},{3,0},{4,7},{5,6},{6,5},{7,4},{8,11},{9,10},{10,... | collective-permute-start | bytes 24584 | tf_op jit(solution)/shard_map/ppermute | solution.py:440
  4.4 1.4 %collective-permute-done.gap_ref = f32[2,8,128]{2,1,0:T(8,128)S(1)} collective-permute-done((f32[2,8,128]{2,1,0:T(8,128)S(1)}, f32[2,8,128]{2,1,0:T(8,128)S(1)}, u32[]{:S(2)}, u32[]{:S(2)}) %collective-permute-start) | collective-permute-done | bytes 8224 | tf_op jit(solution)/shard_map/ppermute | solution.py:440
  5.8 2.3 %collective-permute-start.1 = (f32[1,3,8,128]{3,2,1,0:T(8,128)S(1)}, f32[1,3,8,128]{3,2,1,0:T(8,128)S(1)}, u32[]{:S(2)}, u32[]{:S(2)}) collective-permute-start(f32[1,3,8,128]{3,2,1,0:T(8,128)S(1)} %block.1.refs_0_), channel_id=1, source_target_pairs={{0,4},{4,0},{8,12},{12,8},{16,20},{20,16},{24,28},{28,24},{1,5},{5... | collective-permute-start | bytes 36872 | tf_op jit(solution)/shard_map/ppermute | solution.py:440
  8.0 0.0 collective-permute-start.4
  8.1 1.7 %collective-permute-done.1.refs_1_ = f32[1,3,8,128]{3,2,1,0:T(8,128)S(1)} collective-permute-done((f32[1,3,8,128]{3,2,1,0:T(8,128)S(1)}, f32[1,3,8,128]{3,2,1,0:T(8,128)S(1)}, u32[]{:S(2)}, u32[]{:S(2)}) %collective-permute-start.1) | collective-permute-done | bytes 12320 | tf_op jit(solution)/shard_map/ppermute | solution.py:440
  9.7 3.1 %collective-permute-start.2 = (f32[2,3,8,128]{3,2,1,0:T(8,128)S(1)}, f32[2,3,8,128]{3,2,1,0:T(8,128)S(1)}, u32[]{:S(2)}, u32[]{:S(2)}) collective-permute-start(f32[2,3,8,128]{3,2,1,0:T(8,128)S(1)} %join.2.refs_0_), channel_id=1, source_target_pairs={{0,16},{4,20},{8,24},{12,28},{16,0},{20,4},{24,8},{28,12},{1,17},{... | collective-permute-start | bytes 73736 | tf_op jit(solution)/shard_map/ppermute | solution.py:440
  12.8 0.0 collective-permute-done.4.side_ref.refs_5_
  12.9 2.3 %collective-permute-start.5 = (f32[16,8,128]{2,1,0:T(8,128)S(1)}, f32[16,8,128]{2,1,0:T(8,128)S(1)}, u32[]{:S(2)}, u32[]{:S(2)}) collective-permute-start(f32[16,8,128]{2,1,0:T(8,128)S(1)} %get-tuple-element.17), channel_id=1, source_target_pairs={{0,28},{4,8},{8,4},{12,16},{16,12},{20,24},{24,20},{28,0},{1,29},{... | collective-permute-start | bytes 196616 | tf_op jit(solution)/shard_map/ppermute | solution.py:440
  15.2 0.8 %collective-permute-start.6 = (f32[16,8,128]{2,1,0:T(8,128)S(1)}, f32[16,8,128]{2,1,0:T(8,128)S(1)}, u32[]{:S(2)}, u32[]{:S(2)}) collective-permute-start(f32[16,8,128]{2,1,0:T(8,128)S(1)} %get-tuple-element.18), channel_id=1, source_target_pairs={{0,4},{4,0},{8,12},{12,8},{16,20},{20,16},{24,28},{28,24},{1,5},{5... | collective-permute-start | bytes 196616 | tf_op jit(solution)/shard_map/ppermute | solution.py:440
  16.0 0.0 collective-permute-done.2.refs_1_
  16.0 0.0 copy-start.2
  16.0 0.0 copy-start.3
  16.0 0.7 %collective-permute-start.3 = (f32[4,3,8,128]{3,2,1,0:T(8,128)S(1)}, f32[4,3,8,128]{3,2,1,0:T(8,128)S(1)}, u32[]{:S(2)}, u32[]{:S(2)}) collective-permute-start(f32[4,3,8,128]{3,2,1,0:T(8,128)S(1)} %join.3.refs_3_), channel_id=1, source_target_pairs={{0,8},{4,12},{8,0},{12,4},{16,24},{20,28},{24,16},{28,20},{1,9},{5... | collective-permute-start | bytes 147464 | tf_op jit(solution)/shard_map/ppermute | solution.py:440
  16.7 0.0 copy-done.1
  16.7 1.5 %local.1.refs_2_ = f32[19,18,8,128]{3,2,1,0:T(8,128)S(1)} custom-call(f32[19,128,128]{2,1,0:T(8,128)S(1)} %bitcast.3), custom_call_target="tpu_custom_call" | custom-call | flops 8000000 | bytes 2700000 | tf_op jit(solution)/shard_map/local/pallas_call | solution.py:456
  18.1 1.8 %collective-permute-done.5.refs_7_ = f32[16,8,128]{2,1,0:T(8,128)S(1)} collective-permute-done((f32[16,8,128]{2,1,0:T(8,128)S(1)}, f32[16,8,128]{2,1,0:T(8,128)S(1)}, u32[]{:S(2)}, u32[]{:S(2)}) %collective-permute-start.5) | collective-permute-done | bytes 65568 | tf_op jit(solution)/shard_map/ppermute | solution.py:440
  20.0 0.2 collective-permute-done.6.refs_8_
  20.2 0.0 collective-permute-done.3.refs_4_
  20.2 0.0 copy-done.2
  20.2 0.0 copy-done.3
  20.2 2.4 %finish.1 = f32[19,128,128]{2,1,0:T(8,128)} custom-call(s32[2]{0:T(128)S(1)} %copy-done.2, s32[2]{0:T(128)S(1)} %copy-done.3, f32[19,18,8,128]{3,2,1,0:T(8,128)S(1)} %local.1.refs_2_, f32[4,3,8,128]{3,2,1,0:T(8,128)S(1)} %join.3.refs_3_, f32[4,3,8,128]{3,2,1,0:T(8,128)S(1)} %collective-permute-done.3.refs_4_, ...), custom_call_target="tpu_custom_call" | custom-call | tf_op jit(solution)/shard_map/finish/pallas_call | solution.py:465
  (4 shorter events, 0.0 us)
Async XLA Ops:
  0.0 1.3 %copy-start = (f32[19,8,16,128]{3,2,1,0:T(8,128)S(1)}, f32[19,8,16,128]{3,2,1,0:T(8,128)}, u32[]{:S(2)}) copy-start(f32[19,8,16,128]{3,2,1,0:T(8,128)} %param.3) | copy-start | bytes 3735556
  1.3 15.4 %copy-start.1 = (f32[19,8,16,128]{3,2,1,0:T(8,128)S(1)}, f32[19,8,16,128]{3,2,1,0:T(8,128)}, u32[]{:S(2)}) copy-start(f32[19,8,16,128]{3,2,1,0:T(8,128)} %param.3) | copy-start | bytes 3735556
  2.0 3.8 %collective-permute-start = (f32[2,8,128]{2,1,0:T(8,128)S(1)}, f32[2,8,128]{2,1,0:T(8,128)S(1)}, u32[]{:S(2)}, u32[]{:S(2)}) collective-permute-start(f32[2,8,128]{2,1,0:T(8,128)S(1)} %get-tuple-element.12), channel_id=1, source_target_pairs={{0,3},{1,2},{2,1},{3,0},{4,7},{5,6},{6,5},{7,4},{8,11},{9,10},{10,... | collective-permute-start | bytes 24584 | tf_op jit(solution)/shard_map/ppermute | solution.py:440
  5.8 3.9 %collective-permute-start.1 = (f32[1,3,8,128]{3,2,1,0:T(8,128)S(1)}, f32[1,3,8,128]{3,2,1,0:T(8,128)S(1)}, u32[]{:S(2)}, u32[]{:S(2)}) collective-permute-start(f32[1,3,8,128]{3,2,1,0:T(8,128)S(1)} %block.1.refs_0_), channel_id=1, source_target_pairs={{0,4},{4,0},{8,12},{12,8},{16,20},{20,16},{24,28},{28,24},{1,5},{5... | collective-permute-start | bytes 36872 | tf_op jit(solution)/shard_map/ppermute | solution.py:440
  8.0 4.8 %collective-permute-start.4 = (f32[2,8,128]{2,1,0:T(8,128)S(1)}, f32[2,8,128]{2,1,0:T(8,128)S(1)}, u32[]{:S(2)}, u32[]{:S(2)}) collective-permute-start(f32[2,8,128]{2,1,0:T(8,128)S(1)} %get-tuple-element.14), channel_id=1, source_target_pairs={{0,1},{1,0},{2,3},{3,2},{4,5},{5,4},{6,7},{7,6},{8,9},{9,8},{10,11... | collective-permute-start | bytes 24584 | tf_op jit(solution)/shard_map/ppermute | solution.py:440
  9.7 6.2 %collective-permute-start.2 = (f32[2,3,8,128]{3,2,1,0:T(8,128)S(1)}, f32[2,3,8,128]{3,2,1,0:T(8,128)S(1)}, u32[]{:S(2)}, u32[]{:S(2)}) collective-permute-start(f32[2,3,8,128]{3,2,1,0:T(8,128)S(1)} %join.2.refs_0_), channel_id=1, source_target_pairs={{0,16},{4,20},{8,24},{12,28},{16,0},{20,4},{24,8},{28,12},{1,17},{... | collective-permute-start | bytes 73736 | tf_op jit(solution)/shard_map/ppermute | solution.py:440
  12.9 7.1 %collective-permute-start.5 = (f32[16,8,128]{2,1,0:T(8,128)S(1)}, f32[16,8,128]{2,1,0:T(8,128)S(1)}, u32[]{:S(2)}, u32[]{:S(2)}) collective-permute-start(f32[16,8,128]{2,1,0:T(8,128)S(1)} %get-tuple-element.17), channel_id=1, source_target_pairs={{0,28},{4,8},{8,4},{12,16},{16,12},{20,24},{24,20},{28,0},{1,29},{... | collective-permute-start | bytes 196616 | tf_op jit(solution)/shard_map/ppermute | solution.py:440
  15.2 5.0 %collective-permute-start.6 = (f32[16,8,128]{2,1,0:T(8,128)S(1)}, f32[16,8,128]{2,1,0:T(8,128)S(1)}, u32[]{:S(2)}, u32[]{:S(2)}) collective-permute-start(f32[16,8,128]{2,1,0:T(8,128)S(1)} %get-tuple-element.18), channel_id=1, source_target_pairs={{0,4},{4,0},{8,12},{12,8},{16,20},{20,16},{24,28},{28,24},{1,5},{5... | collective-permute-start | bytes 196616 | tf_op jit(solution)/shard_map/ppermute | solution.py:440
  16.0 4.2 %copy-start.2 = (s32[2]{0:T(128)S(1)}, s32[2]{0:T(128)}, u32[]{:S(2)}) copy-start(s32[2]{0:T(128)} %refs_0_.1) | copy-start | bytes 28
  16.0 4.2 %copy-start.3 = (s32[2]{0:T(128)S(1)}, s32[2]{0:T(128)}, u32[]{:S(2)}) copy-start(s32[2]{0:T(128)} %refs_1_.1) | copy-start | bytes 28
  16.0 4.2 %collective-permute-start.3 = (f32[4,3,8,128]{3,2,1,0:T(8,128)S(1)}, f32[4,3,8,128]{3,2,1,0:T(8,128)S(1)}, u32[]{:S(2)}, u32[]{:S(2)}) collective-permute-start(f32[4,3,8,128]{3,2,1,0:T(8,128)S(1)} %join.3.refs_3_), channel_id=1, source_target_pairs={{0,8},{4,12},{8,0},{12,4},{16,24},{20,28},{24,16},{28,20},{1,9},{5... | collective-permute-start | bytes 147464 | tf_op jit(solution)/shard_map/ppermute | solution.py:440

commit v7 on v6

--- a/solution.py
+++ b/solution.py
@@ -30,6 +30,7 @@
 WEIGHTS = [1.0 / 3.0] + [1.0 / 18.0] * 6 + [1.0 / 36.0] * 12
 EAST = [1, 7, 9, 11, 13]
 WEST = [2, 8, 10, 12, 14]
+LEVEL = [0, 1, 2, 5, 6, 11, 12, 13, 14]
 UP = [3, 7, 10, 15, 17]
 DOWN = [4, 8, 9, 16, 18]
 OMEGA = 1.0 / 0.6
@@ -129,7 +130,7 @@
     return ref[q, pl.ds(x, NZ, stride=width), :]
 
 
-def pack_kernel(shears, width, f_ref, side_ref, gap_ref, own_ref, near_ref, far_ref):
+def pack_kernel(shears, width, f_ref, side_ref, gap_ref, own_ref, near_ref, far_ref, edge_ref):
     shear = lax.axis_index("shear")
     lane = lane_iota()
     boost_up = jnp.where(shear == shears - 1, -BOOST, 0.0).astype(jnp.float32)
@@ -144,6 +145,8 @@
     rho, jx, jy, jz = moments(edge)
     post = relax(rho, jx, jy, jz, edge, range(19))
     post = {q: roll_z(post[q], VELOCITY[q][2]) for q in range(19)}
+    for q in range(19):
+        edge_ref[q] = post[q]
     sums = classes(post, "x")
 
     def groups(ghosts, outer, at, far):
@@ -213,25 +216,41 @@
     out_ref[pl.ds((1 - mine) * count, count)] = theirs_ref[...]
 
 
-def local_kernel(width, f_ref, a_ref):
-    def step(x):
+def local_kernel(width, f_ref, edge_ref, a_ref, inner_ref, own_ref):
+    def first(x):
         f = [column(f_ref, q, x, width) for q in range(19)]
         post = relax(*moments(f), f, range(19))
         for q in range(19):
             cx, cy, cz = VELOCITY[q]
             a_ref[q, x + 1 + cx] = roll_y(roll_z(post[q], cz), cy)
 
-    pl.loop(0, width, unroll=2)(step)
-    for q in range(19):
-        cx = VELOCITY[q][0]
-        zero = jnp.zeros((NZ, LANES), jnp.float32)
-        for x in (0, 1, width, width + 1):
-            if not 0 <= x - 1 - cx < width:
-                a_ref[q, x] = zero
+    def second(x):
+        f = [a_ref[q, x + 1] for q in range(19)]
+        post = relax(*moments(f), f, range(19))
+        for q in range(19):
+            cx, cy, cz = VELOCITY[q]
+            inner_ref[q, x + cx] = roll_y(roll_z(post[q], cz), cy)
+
+    pl.loop(0, width, unroll=2)(first)
+    pl.loop(1, width - 1, unroll=2)(second)
+    for at, (lanes, row, far) in enumerate(((DOWN, 2, 3), (UP, 1, 0))):
+        f = {}
+        for q in LEVEL + lanes:
+            f[q] = roll_y(edge_ref[q], (VELOCITY[q][0] + BASE) * GAP - (far if q in lanes else row))
+        totals = [None] * 4
+        for q in LEVEL + lanes:
+            for k, c in enumerate((1,) + VELOCITY[q]):
+                if c:
+                    if totals[k] is None:
+                        totals[k] = f[q] if c > 0 else -f[q]
+                    else:
+                        totals[k] = totals[k] + f[q] if c > 0 else totals[k] - f[q]
+        for k, v in enumerate([f[q] for q in LEVEL] + totals):
+            own_ref[at * 13 + k] = v
 
 
 def finish_kernel(
-    flows, shears, width, cells, weight, a_ref, mine_ref, theirs_ref, side_ref, own_ref,
+    flows, shears, width, cells, weight, a_ref, inner_ref, within_ref, mine_ref, theirs_ref, side_ref, own_ref,
     far_ref, near_ref, out_hbm, out_ref, sem_out,
 ):
     flow = lax.axis_index("flow")
@@ -344,6 +363,7 @@
 
     pairs1 = pairs(up1, down1, True)
     pairs2 = pairs(up2, down2, False)
+    ghosts2 = {**up2, **down2}
 
     def beyond(found, x):
         return [roll_y(v, -1 - (x + BASE) * GAP) for v in found]
@@ -370,7 +390,8 @@
                 v = insert(roll_y(roll_z(post[q], cz), cy), q, edge)
                 out_ref[q, pl.ds(x + cx, NZ, stride=width), :] = v
 
-    for x, halo, entering, leaving in ((-1, from_west, EAST, WEST), (width, from_east, WEST, EAST)):
+    def halo_column(x):
+        halo, entering, leaving = (from_west, EAST, WEST) if x < 0 else (from_east, WEST, EAST)
         edge = beyond(pairs1, x)
         f = {q: insert(halo(i), q, edge) for i, q in enumerate(entering)}
         for q in leaving:
@@ -388,6 +409,37 @@
         jz = (halo(12) + more_z) + ((f[11] - f[12]) + (f[14] - f[13]))
         put(relax(rho, jx, jy, jz, f, entering), x)
 
+    patches = {}
+    for at, lanes, slot in ((0, UP, 2), (1, DOWN, 1)):
+        f = {q: within_ref[at * 13 + k] for k, q in enumerate(LEVEL)}
+        for k, q in enumerate(lanes):
+            f[q] = pairs1[k] if at else roll_y(pairs1[k], -1)
+        totals = [within_ref[at * 13 + 9 + k] for k in range(4)]
+        total = f[lanes[0]] + f[lanes[1]] + f[lanes[2]] + f[lanes[3]] + f[lanes[4]]
+        if at:
+            more = [total, f[9] - f[8], -total, f[18] - f[16]]
+        else:
+            more = [total, f[7] - f[10], total, f[15] - f[17]]
+        post = relax(*[t + m for t, m in zip(totals, more)], f, LEVEL + lanes)
+        for q in LEVEL + lanes:
+            cx, cy, cz = VELOCITY[q]
+            inside = roll_y(roll_z(post[q], cz), (cx - BASE) * GAP + slot + cy)
+            if cy:
+                outside = roll_y(ghosts2[q][0], (cx - BASE) * GAP + slot)
+                patches[q] = jnp.where(lane % GAP == slot, outside, inside)
+            elif at:
+                patches[q] = jnp.where(lane % GAP == slot, inside, patches[q])
+            else:
+                patches[q] = inside
+    mask = {1: lane < 2, -1: lane >= LANES - 2, 0: at_first | at_last}
+
+    def merge(x):
+        for q in range(19):
+            cx, cy, cz = VELOCITY[q]
+            if 1 <= x - cx < width - 1:
+                moved = roll_y(patches[q], -(x * GAP + 2))
+                out_ref[q, pl.ds(x, NZ, stride=width), :] = jnp.where(mask[cy], moved, inner_ref[q, x])
+
     rows_of = (19, NZ, width, LANES)
     half = width // 2
     stores = [
@@ -396,14 +448,17 @@
         )
         for i, a in enumerate((0, half))
     ]
-    for x in range(width):
-        edge = beyond(pairs1, x)
-        f = [insert(arrived(q, x), q, edge) for q in range(19)]
-        post = relax(*moments(f), f, range(19))
-        put(post, x)
-        if x == half:
-            stores[0].start()
-    stores[1].start()
+    for store, rim, halo_at, xs in (
+        (stores[0], 0, -1, range(half)),
+        (stores[1], width - 1, width, range(half, width)),
+    ):
+        halo_column(halo_at)
+        edge = beyond(pairs1, rim)
+        f = [insert(arrived(q, rim), q, edge) for q in range(19)]
+        put(relax(*moments(f), f, range(19)), rim)
+        for x in xs:
+            merge(x)
+        store.start()
     for store in stores:
         store.wait()
 
@@ -439,8 +494,8 @@
     def swap(x, axis, partner):
         return lax.ppermute(x, axis, [(i, partner(i)) for i in range(lax.axis_size(axis))])
 
-    side, gap, own, near, far = call(
-        "pack", body(pack_kernel, shears, width), [vregs(2), vregs(2), vregs(2), vregs(13), vregs(13)], f
+    side, gap, own, near, far, edge = call(
+        "pack", body(pack_kernel, shears, width), [vregs(2), vregs(2), vregs(2), vregs(13), vregs(13), vregs(19)], f
     )
     side = swap(side, "shear", lambda i: i ^ 1)
     gap = swap(gap, "shear", lambda i: (i - 1 + i % 2 * 2) % shears)
@@ -453,19 +508,19 @@
         mine = call("join", body(join_kernel, apart), vregs(2 * mine.shape[0], 3), mine, theirs)
     theirs = swap(mine, "flow", lambda i: i ^ last)
     from_near = swap(near, "flow", lambda i: i ^ 1)
-    streamed = pl.pallas_call(
+    streamed, inner, within = pl.pallas_call(
         body(local_kernel, width),
-        out_shape=jax.ShapeDtypeStruct((19, width + 2, NZ, LANES), f32),
-        in_specs=[vmem],
-        out_specs=vmem,
+        out_shape=[vregs(19, width + 2), vregs(19, width), vregs(26)],
+        in_specs=[vmem, vmem],
+        out_specs=[vmem] * 3,
         compiler_params=params,
-        cost_estimate=pl.CostEstimate(flops=8_000_000, bytes_accessed=2_700_000, transcendentals=0),
+        cost_estimate=pl.CostEstimate(flops=16_000_000, bytes_accessed=4_000_000, transcendentals=0),
         name="local",
-    )(f)
+    )(f, edge)
     out = pl.pallas_call(
         body(finish_kernel, flows, shears, width),
         out_shape=jax.ShapeDtypeStruct((19, NZ * width, LANES), f32),
-        in_specs=[vmem] * 9,
+        in_specs=[vmem] * 11,
         out_specs=anyspace,
         scratch_shapes=[
             pltpu.VMEM((19, NZ * width, LANES), f32),
@@ -473,7 +528,7 @@
         ],
         compiler_params=params,
         name="finish",
-    )(le_cells, le_weight, streamed, mine, theirs, side, own, from_far, from_near)
+    )(le_cells, le_weight, streamed, inner, within, mine, theirs, side, own, from_far, from_near)
     return out.reshape(populations.shape)
 
 

time: 22.8 us -> 22.6 us (level)
  waiting for transfers between devices: 5.07 us -> 4.25 us
  Pallas kernels: 4.57 us -> 5.35 us
    pallas_call x1, Pallas kernels: 1.46 us -> 2.35 us  [per_device(): pl.pallas_call(body(local_kernel, width), out_shape=[vregs(19, width + 2)...]
    ppermute x7, waiting for transfers between devices: 5.07 us -> 4.25 us  [swap(): lax.ppermute(x, axis, [(i, partner(i)) for i in range(lax.axis_size(axis))])]
  transfers between devices with their start and end apart: 7 -> 7, of which waited for: 4 -> 4; matrix products, arithmetic and copies ran while one was open for 0% -> 0% of each run, Pallas kernels for 7% -> 11%
where the time goes in v7:
time: 22.6 us; the launch traced here: 22.5 us
  starting transfers between devices  11.6 us (51%)
  Pallas kernels  5.35 us (24%)
  waiting for transfers between devices  4.25 us (19%)
  local copies, waits for them, and re-layouts  1.3 us (6%)
    ppermute x7, starting transfers between devices, swap(): lax.ppermute(x, axis, [(i, partner(i)) for i in range(lax.axis_size(axis))])  11.6 us
    ppermute x7, waiting for transfers between devices, swap(): lax.ppermute(x, axis, [(i, partner(i)) for i in range(lax.axis_size(axis))])  4.25 us
    pallas_call x1, Pallas kernels, per_device(): pl.pallas_call(body(local_kernel, width), out_shape=[vregs(19, width + 2)...  2.35 us
    pallas_call x1, Pallas kernels, per_device(): pl.pallas_call(body(finish_kernel, flows, shears, width), out_shape=jax.S...  2.31 us
    unnamed x8, local copies, waits for them, and re-layouts  1.3 us
    pallas_call x5, Pallas kernels, call(): pl.pallas_call(kernel, out_shape=outs, in_specs=[vmem] * len(arrays), out...  0.68 us
  transfers between devices with their start and end apart: 7, of which 4 were waited for; matrix products, arithmetic and copies ran while one was open for 0% of the time, Pallas kernels for 11%

profile of v7, /device:TPU:0, one launch (start us, length us, event | category | flops | bytes accessed | tf_op | source)
XLA Modules:
  0.0 22.5 jit_solution(3899611449863599267)
XLA Ops:
  0.0 0.0 copy-start
  0.0 1.3 %copy-done = f32[19,8,16,128]{3,2,1,0:T(8,128)S(1)} copy-done((f32[19,8,16,128]{3,2,1,0:T(8,128)S(1)}, f32[19,8,16,128]{3,2,1,0:T(8,128)}, u32[]{:S(2)}) %copy-start) | copy-done | bytes 1245208
  1.3 0.0 copy-start.1
  1.3 0.0 copy-start.2
  1.3 0.0 copy-start.3
  1.3 0.7 %pack.1 = (f32[2,8,128]{2,1,0:T(8,128)S(1)}, f32[2,8,128]{2,1,0:T(8,128)S(1)}, f32[2,8,128]{2,1,0:T(8,128)S(1)}, f32[13,8,128]{2,1,0:T(8,128)S(1)}, f32[13,8,128...) custom-call(f32[19,128,128]{2,1,0:T(8,128)S(1)} %bitcast.2), custom_call_target="tpu_custom_call" | custom-call | tf_op jit(solution)/shard_map/pack/pallas_call | solution.py:488
  2.0 2.5 %collective-permute-start = (f32[2,8,128]{2,1,0:T(8,128)S(1)}, f32[2,8,128]{2,1,0:T(8,128)S(1)}, u32[]{:S(2)}, u32[]{:S(2)}) collective-permute-start(f32[2,8,128]{2,1,0:T(8,128)S(1)} %get-tuple-element.20), channel_id=1, source_target_pairs={{0,3},{1,2},{2,1},{3,0},{4,7},{5,6},{6,5},{7,4},{8,11},{9,10},{10,... | collective-permute-start | bytes 24584 | tf_op jit(solution)/shard_map/ppermute | solution.py:495
  4.4 1.4 %collective-permute-done.gap_ref = f32[2,8,128]{2,1,0:T(8,128)S(1)} collective-permute-done((f32[2,8,128]{2,1,0:T(8,128)S(1)}, f32[2,8,128]{2,1,0:T(8,128)S(1)}, u32[]{:S(2)}, u32[]{:S(2)}) %collective-permute-start) | collective-permute-done | bytes 8224 | tf_op jit(solution)/shard_map/ppermute | solution.py:495
  5.8 2.3 %collective-permute-start.1 = (f32[1,3,8,128]{3,2,1,0:T(8,128)S(1)}, f32[1,3,8,128]{3,2,1,0:T(8,128)S(1)}, u32[]{:S(2)}, u32[]{:S(2)}) collective-permute-start(f32[1,3,8,128]{3,2,1,0:T(8,128)S(1)} %block.1.refs_0_), channel_id=1, source_target_pairs={{0,4},{4,0},{8,12},{12,8},{16,20},{20,16},{24,28},{28,24},{1,5},{5... | collective-permute-start | bytes 36872 | tf_op jit(solution)/shard_map/ppermute | solution.py:495
  8.1 0.0 collective-permute-start.4
  8.1 1.7 %collective-permute-done.1.refs_1_ = f32[1,3,8,128]{3,2,1,0:T(8,128)S(1)} collective-permute-done((f32[1,3,8,128]{3,2,1,0:T(8,128)S(1)}, f32[1,3,8,128]{3,2,1,0:T(8,128)S(1)}, u32[]{:S(2)}, u32[]{:S(2)}) %collective-permute-start.1) | collective-permute-done | bytes 12320 | tf_op jit(solution)/shard_map/ppermute | solution.py:495
  9.7 3.1 %collective-permute-start.2 = (f32[2,3,8,128]{3,2,1,0:T(8,128)S(1)}, f32[2,3,8,128]{3,2,1,0:T(8,128)S(1)}, u32[]{:S(2)}, u32[]{:S(2)}) collective-permute-start(f32[2,3,8,128]{3,2,1,0:T(8,128)S(1)} %join.2.refs_0_), channel_id=1, source_target_pairs={{0,16},{4,20},{8,24},{12,28},{16,0},{20,4},{24,8},{28,12},{1,17},{... | collective-permute-start | bytes 73736 | tf_op jit(solution)/shard_map/ppermute | solution.py:495
  12.9 0.0 collective-permute-done.4.side_ref.refs_7_
  12.9 2.3 %collective-permute-start.5 = (f32[16,8,128]{2,1,0:T(8,128)S(1)}, f32[16,8,128]{2,1,0:T(8,128)S(1)}, u32[]{:S(2)}, u32[]{:S(2)}) collective-permute-start(f32[16,8,128]{2,1,0:T(8,128)S(1)} %get-tuple-element.25), channel_id=1, source_target_pairs={{0,28},{4,8},{8,4},{12,16},{16,12},{20,24},{24,20},{28,0},{1,29},{... | collective-permute-start | bytes 196616 | tf_op jit(solution)/shard_map/ppermute | solution.py:495
  15.2 0.8 %collective-permute-start.6 = (f32[16,8,128]{2,1,0:T(8,128)S(1)}, f32[16,8,128]{2,1,0:T(8,128)S(1)}, u32[]{:S(2)}, u32[]{:S(2)}) collective-permute-start(f32[16,8,128]{2,1,0:T(8,128)S(1)} %get-tuple-element.26), channel_id=1, source_target_pairs={{0,4},{4,0},{8,12},{12,8},{16,20},{20,16},{24,28},{28,24},{1,5},{5... | collective-permute-start | bytes 196616 | tf_op jit(solution)/shard_map/ppermute | solution.py:495
  16.0 0.0 collective-permute-done.2.refs_1_
  16.0 0.6 %collective-permute-start.3 = (f32[4,3,8,128]{3,2,1,0:T(8,128)S(1)}, f32[4,3,8,128]{3,2,1,0:T(8,128)S(1)}, u32[]{:S(2)}, u32[]{:S(2)}) collective-permute-start(f32[4,3,8,128]{3,2,1,0:T(8,128)S(1)} %join.3.refs_5_), channel_id=1, source_target_pairs={{0,8},{4,12},{8,0},{12,4},{16,24},{20,28},{24,16},{28,20},{1,9},{5... | collective-permute-start | bytes 147464 | tf_op jit(solution)/shard_map/ppermute | solution.py:495
  16.6 0.0 copy-done.1
  16.6 2.4 %local.1 = (f32[19,18,8,128]{3,2,1,0:T(8,128)S(1)}, f32[19,16,8,128]{3,2,1,0:T(8,128)S(1)}, f32[26,8,128]{2,1,0:T(8,128)S(1)}) custom-call(f32[19,128,128]{2,1,0:T(8,128)S(1)} %bitcast.3, f32[19,8,128]{2,1,0:T(8,128)S(1)} %get-tuple-element.16.refs_1_), custom_call_target="tpu_custom_call" | custom-call | flops 16000000 | bytes 4000000 | tf_op jit(solution)/shard_map/local/pallas_call | solution.py:511
  19.0 1.0 %collective-permute-done.5.refs_9_ = f32[16,8,128]{2,1,0:T(8,128)S(1)} collective-permute-done((f32[16,8,128]{2,1,0:T(8,128)S(1)}, f32[16,8,128]{2,1,0:T(8,128)S(1)}, u32[]{:S(2)}, u32[]{:S(2)}) %collective-permute-start.5) | collective-permute-done | bytes 65568 | tf_op jit(solution)/shard_map/ppermute | solution.py:495
  20.0 0.2 collective-permute-done.6.refs_10_
  20.2 0.0 collective-permute-done.3.refs_6_
  20.2 0.0 copy-done.2
  20.2 0.0 copy-done.3
  20.2 2.3 %finish.1 = f32[19,128,128]{2,1,0:T(8,128)} custom-call(s32[2]{0:T(128)S(1)} %copy-done.2, s32[2]{0:T(128)S(1)} %copy-done.3, f32[19,18,8,128]{3,2,1,0:T(8,128)S(1)} %get-tuple-element.17.refs_2_, f32[19,16,8,128]{3,2,1,0:T(8,128)S(1)} %get-tuple-element.18.refs_3_, f32[26,8,128]{2,1,0:T(8,128)S(1)} %get-tuple-element.19.refs_4_, ...), custom_call_target="tpu_custom_call" | custom-call | tf_op jit(solution)/shard_map/finish/pallas_call | solution.py:520
  (4 shorter events, 0.0 us)
Async XLA Ops:
  0.0 1.3 %copy-start = (f32[19,8,16,128]{3,2,1,0:T(8,128)S(1)}, f32[19,8,16,128]{3,2,1,0:T(8,128)}, u32[]{:S(2)}) copy-start(f32[19,8,16,128]{3,2,1,0:T(8,128)} %param.3) | copy-start | bytes 3735556
  1.3 15.3 %copy-start.1 = (f32[19,8,16,128]{3,2,1,0:T(8,128)S(1)}, f32[19,8,16,128]{3,2,1,0:T(8,128)}, u32[]{:S(2)}) copy-start(f32[19,8,16,128]{3,2,1,0:T(8,128)} %param.3) | copy-start | bytes 3735556
  1.3 18.9 %copy-start.2 = (s32[2]{0:T(128)S(1)}, s32[2]{0:T(128)}, u32[]{:S(2)}) copy-start(s32[2]{0:T(128)} %refs_0_.1) | copy-start | bytes 28
  1.3 18.9 %copy-start.3 = (s32[2]{0:T(128)S(1)}, s32[2]{0:T(128)}, u32[]{:S(2)}) copy-start(s32[2]{0:T(128)} %refs_1_.1) | copy-start | bytes 28
  2.0 3.8 %collective-permute-start = (f32[2,8,128]{2,1,0:T(8,128)S(1)}, f32[2,8,128]{2,1,0:T(8,128)S(1)}, u32[]{:S(2)}, u32[]{:S(2)}) collective-permute-start(f32[2,8,128]{2,1,0:T(8,128)S(1)} %get-tuple-element.20), channel_id=1, source_target_pairs={{0,3},{1,2},{2,1},{3,0},{4,7},{5,6},{6,5},{7,4},{8,11},{9,10},{10,... | collective-permute-start | bytes 24584 | tf_op jit(solution)/shard_map/ppermute | solution.py:495
  5.8 3.9 %collective-permute-start.1 = (f32[1,3,8,128]{3,2,1,0:T(8,128)S(1)}, f32[1,3,8,128]{3,2,1,0:T(8,128)S(1)}, u32[]{:S(2)}, u32[]{:S(2)}) collective-permute-start(f32[1,3,8,128]{3,2,1,0:T(8,128)S(1)} %block.1.refs_0_), channel_id=1, source_target_pairs={{0,4},{4,0},{8,12},{12,8},{16,20},{20,16},{24,28},{28,24},{1,5},{5... | collective-permute-start | bytes 36872 | tf_op jit(solution)/shard_map/ppermute | solution.py:495
  8.1 4.8 %collective-permute-start.4 = (f32[2,8,128]{2,1,0:T(8,128)S(1)}, f32[2,8,128]{2,1,0:T(8,128)S(1)}, u32[]{:S(2)}, u32[]{:S(2)}) collective-permute-start(f32[2,8,128]{2,1,0:T(8,128)S(1)} %get-tuple-element.22), channel_id=1, source_target_pairs={{0,1},{1,0},{2,3},{3,2},{4,5},{5,4},{6,7},{7,6},{8,9},{9,8},{10,11... | collective-permute-start | bytes 24584 | tf_op jit(solution)/shard_map/ppermute | solution.py:495
  9.7 6.2 %collective-permute-start.2 = (f32[2,3,8,128]{3,2,1,0:T(8,128)S(1)}, f32[2,3,8,128]{3,2,1,0:T(8,128)S(1)}, u32[]{:S(2)}, u32[]{:S(2)}) collective-permute-start(f32[2,3,8,128]{3,2,1,0:T(8,128)S(1)} %join.2.refs_0_), channel_id=1, source_target_pairs={{0,16},{4,20},{8,24},{12,28},{16,0},{20,4},{24,8},{28,12},{1,17},{... | collective-permute-start | bytes 73736 | tf_op jit(solution)/shard_map/ppermute | solution.py:495
  12.9 7.1 %collective-permute-start.5 = (f32[16,8,128]{2,1,0:T(8,128)S(1)}, f32[16,8,128]{2,1,0:T(8,128)S(1)}, u32[]{:S(2)}, u32[]{:S(2)}) collective-permute-start(f32[16,8,128]{2,1,0:T(8,128)S(1)} %get-tuple-element.25), channel_id=1, source_target_pairs={{0,28},{4,8},{8,4},{12,16},{16,12},{20,24},{24,20},{28,0},{1,29},{... | collective-permute-start | bytes 196616 | tf_op jit(solution)/shard_map/ppermute | solution.py:495
  15.2 5.0 %collective-permute-start.6 = (f32[16,8,128]{2,1,0:T(8,128)S(1)}, f32[16,8,128]{2,1,0:T(8,128)S(1)}, u32[]{:S(2)}, u32[]{:S(2)}) collective-permute-start(f32[16,8,128]{2,1,0:T(8,128)S(1)} %get-tuple-element.26), channel_id=1, source_target_pairs={{0,4},{4,0},{8,12},{12,8},{16,20},{20,16},{24,28},{28,24},{1,5},{5... | collective-permute-start | bytes 196616 | tf_op jit(solution)/shard_map/ppermute | solution.py:495
  16.0 4.2 %collective-permute-start.3 = (f32[4,3,8,128]{3,2,1,0:T(8,128)S(1)}, f32[4,3,8,128]{3,2,1,0:T(8,128)S(1)}, u32[]{:S(2)}, u32[]{:S(2)}) collective-permute-start(f32[4,3,8,128]{3,2,1,0:T(8,128)S(1)} %join.3.refs_5_), channel_id=1, source_target_pairs={{0,8},{4,12},{8,0},{12,4},{16,24},{20,28},{24,16},{28,20},{1,9},{5... | collective-permute-start | bytes 147464 | tf_op jit(solution)/shard_map/ppermute | solution.py:495

commit v8 on v6

--- a/solution.py
+++ b/solution.py
@@ -129,7 +129,7 @@
     return ref[q, pl.ds(x, NZ, stride=width), :]
 
 
-def pack_kernel(shears, width, f_ref, side_ref, gap_ref, own_ref, near_ref, far_ref):
+def pack_kernel(shears, width, f_ref, side_ref, gap_ref, own_ref):
     shear = lax.axis_index("shear")
     lane = lane_iota()
     boost_up = jnp.where(shear == shears - 1, -BOOST, 0.0).astype(jnp.float32)
@@ -174,6 +174,9 @@
     own_ref[0] = jnp.where(low, down0, up0)
     own_ref[1] = jnp.where(low, up0, down0)
 
+
+def columns_kernel(width, f_ref, near_ref, far_ref):
+    lane = lane_iota()
     packs = []
     for near, far, lanes in ((width - 1, width - 2, EAST), (0, 1, WEST)):
         planes = []
@@ -201,7 +204,7 @@
         out[15] = own_ref[1]
 
 
-def block_kernel(gap_ref, own_ref, out_ref):
+def block_kernel(gap_ref, own_ref, ready_ref, out_ref):
     out_ref[0, 0:2] = gap_ref[...]
     out_ref[0, 2] = own_ref[0]
 
@@ -439,12 +442,11 @@
     def swap(x, axis, partner):
         return lax.ppermute(x, axis, [(i, partner(i)) for i in range(lax.axis_size(axis))])
 
-    side, gap, own, near, far = call(
-        "pack", body(pack_kernel, shears, width), [vregs(2), vregs(2), vregs(2), vregs(13), vregs(13)], f
-    )
+    side, gap, own = call("pack", body(pack_kernel, shears, width), [vregs(2)] * 3, f)
+    near, far = call("columns", body(columns_kernel, width), [vregs(13)] * 2, f)
     side = swap(side, "shear", lambda i: i ^ 1)
     gap = swap(gap, "shear", lambda i: (i - 1 + i % 2 * 2) % shears)
-    mine = call("block", block_kernel, vregs(1, 3), gap, own)
+    mine = call("block", block_kernel, vregs(1, 3), gap, own, near)
     near, far = call("message", message_kernel, [vregs(16), vregs(16)], near, far, side, own)
     from_far = swap(far, "flow", lambda i: (i - 1 + i % 2 * 2) % flows)
     *early, last = gather_order(flows)

time: 22.8 us -> 22.7 us (level)
  waiting for transfers between devices: 5.07 us -> 4.83 us
    ppermute x7, waiting for transfers between devices: 5.07 us -> 4.83 us  [swap(): lax.ppermute(x, axis, [(i, partner(i)) for i in range(lax.axis_size(axis))])]
    pallas_call x5 -> x6, Pallas kernels: 0.68 us -> 0.8 us  [call(): pl.pallas_call(kernel, out_shape=outs, in_specs=[vmem] * len(arrays), out...]
  transfers between devices with their start and end apart: 7 -> 7, of which waited for: 4 -> 4; matrix products, arithmetic and copies ran while one was open for 0% -> 0% of each run, Pallas kernels for 7% -> 8%
where the time goes in v8:
time: 22.7 us; the launch traced here: 22.5 us
  starting transfers between devices  11.6 us (51%)
  waiting for transfers between devices  4.83 us (21%)
  Pallas kernels  4.69 us (21%)
  local copies, waits for them, and re-layouts  1.31 us (6%)
    ppermute x7, starting transfers between devices, swap(): lax.ppermute(x, axis, [(i, partner(i)) for i in range(lax.axis_size(axis))])  11.6 us
    ppermute x7, waiting for transfers between devices, swap(): lax.ppermute(x, axis, [(i, partner(i)) for i in range(lax.axis_size(axis))])  4.83 us
    pallas_call x1, Pallas kernels, per_device(): pl.pallas_call(body(finish_kernel, flows, shears, width), out_shape=jax.S...  2.43 us
    pallas_call x1, Pallas kernels, per_device(): pl.pallas_call(body(local_kernel, width), out_shape=jax.ShapeDtypeStruct(...  1.46 us
    unnamed x8, local copies, waits for them, and re-layouts  1.31 us
    pallas_call x6, Pallas kernels, call(): pl.pallas_call(kernel, out_shape=outs, in_specs=[vmem] * len(arrays), out...  0.8 us
  transfers between devices with their start and end apart: 7, of which 4 were waited for; matrix products, arithmetic and copies ran while one was open for 0% of the time, Pallas kernels for 8%

profile of v8, /device:TPU:0, one launch (start us, length us, event | category | flops | bytes accessed | tf_op | source)
XLA Modules:
  0.0 22.5 jit_solution(11080021611919745495)
XLA Ops:
  0.0 0.0 copy-start
  0.0 1.3 %copy-done = f32[19,8,16,128]{3,2,1,0:T(8,128)S(1)} copy-done((f32[19,8,16,128]{3,2,1,0:T(8,128)S(1)}, f32[19,8,16,128]{3,2,1,0:T(8,128)}, u32[]{:S(2)}) %copy-start) | copy-done | bytes 1245208
  1.3 0.0 copy-start.1
  1.3 0.5 %pack.1 = (f32[2,8,128]{2,1,0:T(8,128)S(1)}, f32[2,8,128]{2,1,0:T(8,128)S(1)}, f32[2,8,128]{2,1,0:T(8,128)S(1)}) custom-call(f32[19,128,128]{2,1,0:T(8,128)S(1)} %bitcast.2), custom_call_target="tpu_custom_call" | custom-call | tf_op jit(solution)/shard_map/pack/pallas_call | solution.py:436
  1.8 2.5 %collective-permute-start = (f32[2,8,128]{2,1,0:T(8,128)S(1)}, f32[2,8,128]{2,1,0:T(8,128)S(1)}, u32[]{:S(2)}, u32[]{:S(2)}) collective-permute-start(f32[2,8,128]{2,1,0:T(8,128)S(1)} %get-tuple-element.12), channel_id=1, source_target_pairs={{0,3},{1,2},{2,1},{3,0},{4,7},{5,6},{6,5},{7,4},{8,11},{9,10},{10,... | collective-permute-start | bytes 24584 | tf_op jit(solution)/shard_map/ppermute | solution.py:443
  4.3 0.2 %columns.1 = (f32[13,8,128]{2,1,0:T(8,128)S(1)}, f32[13,8,128]{2,1,0:T(8,128)S(1)}) custom-call(f32[19,128,128]{2,1,0:T(8,128)S(1)} %bitcast.3), custom_call_target="tpu_custom_call" | custom-call | tf_op jit(solution)/shard_map/columns/pallas_call | solution.py:436
  4.6 1.1 %collective-permute-done.gap_ref = f32[2,8,128]{2,1,0:T(8,128)S(1)} collective-permute-done((f32[2,8,128]{2,1,0:T(8,128)S(1)}, f32[2,8,128]{2,1,0:T(8,128)S(1)}, u32[]{:S(2)}, u32[]{:S(2)}) %collective-permute-start) | collective-permute-done | bytes 8224 | tf_op jit(solution)/shard_map/ppermute | solution.py:443
  5.7 2.3 %collective-permute-start.1 = (f32[1,3,8,128]{3,2,1,0:T(8,128)S(1)}, f32[1,3,8,128]{3,2,1,0:T(8,128)S(1)}, u32[]{:S(2)}, u32[]{:S(2)}) collective-permute-start(f32[1,3,8,128]{3,2,1,0:T(8,128)S(1)} %block.1.refs_0_), channel_id=1, source_target_pairs={{0,4},{4,0},{8,12},{12,8},{16,20},{20,16},{24,28},{28,24},{1,5},{5... | collective-permute-start | bytes 36872 | tf_op jit(solution)/shard_map/ppermute | solution.py:443
  7.9 0.0 collective-permute-start.4
  7.9 1.7 %collective-permute-done.1.refs_1_ = f32[1,3,8,128]{3,2,1,0:T(8,128)S(1)} collective-permute-done((f32[1,3,8,128]{3,2,1,0:T(8,128)S(1)}, f32[1,3,8,128]{3,2,1,0:T(8,128)S(1)}, u32[]{:S(2)}, u32[]{:S(2)}) %collective-permute-start.1) | collective-permute-done | bytes 12320 | tf_op jit(solution)/shard_map/ppermute | solution.py:443
  9.6 3.1 %collective-permute-start.2 = (f32[2,3,8,128]{3,2,1,0:T(8,128)S(1)}, f32[2,3,8,128]{3,2,1,0:T(8,128)S(1)}, u32[]{:S(2)}, u32[]{:S(2)}) collective-permute-start(f32[2,3,8,128]{3,2,1,0:T(8,128)S(1)} %join.2.refs_0_), channel_id=1, source_target_pairs={{0,16},{4,20},{8,24},{12,28},{16,0},{20,4},{24,8},{28,12},{1,17},{... | collective-permute-start | bytes 73736 | tf_op jit(solution)/shard_map/ppermute | solution.py:443
  12.7 0.0 collective-permute-done.4.side_ref.refs_5_
  12.8 2.3 %collective-permute-start.5 = (f32[16,8,128]{2,1,0:T(8,128)S(1)}, f32[16,8,128]{2,1,0:T(8,128)S(1)}, u32[]{:S(2)}, u32[]{:S(2)}) collective-permute-start(f32[16,8,128]{2,1,0:T(8,128)S(1)} %get-tuple-element.17), channel_id=1, source_target_pairs={{0,28},{4,8},{8,4},{12,16},{16,12},{20,24},{24,20},{28,0},{1,29},{... | collective-permute-start | bytes 196616 | tf_op jit(solution)/shard_map/ppermute | solution.py:443
  15.1 0.8 %collective-permute-start.6 = (f32[16,8,128]{2,1,0:T(8,128)S(1)}, f32[16,8,128]{2,1,0:T(8,128)S(1)}, u32[]{:S(2)}, u32[]{:S(2)}) collective-permute-start(f32[16,8,128]{2,1,0:T(8,128)S(1)} %get-tuple-element.18), channel_id=1, source_target_pairs={{0,4},{4,0},{8,12},{12,8},{16,20},{20,16},{24,28},{28,24},{1,5},{5... | collective-permute-start | bytes 196616 | tf_op jit(solution)/shard_map/ppermute | solution.py:443
  15.9 0.0 collective-permute-done.2.refs_1_
  15.9 0.0 copy-start.2
  15.9 0.0 copy-start.3
  15.9 0.7 %collective-permute-start.3 = (f32[4,3,8,128]{3,2,1,0:T(8,128)S(1)}, f32[4,3,8,128]{3,2,1,0:T(8,128)S(1)}, u32[]{:S(2)}, u32[]{:S(2)}) collective-permute-start(f32[4,3,8,128]{3,2,1,0:T(8,128)S(1)} %join.3.refs_3_), channel_id=1, source_target_pairs={{0,8},{4,12},{8,0},{12,4},{16,24},{20,28},{24,16},{28,20},{1,9},{5... | collective-permute-start | bytes 147464 | tf_op jit(solution)/shard_map/ppermute | solution.py:443
  16.6 0.0 copy-done.1
  16.6 1.5 %local.1.refs_2_ = f32[19,18,8,128]{3,2,1,0:T(8,128)S(1)} custom-call(f32[19,128,128]{2,1,0:T(8,128)S(1)} %bitcast.4), custom_call_target="tpu_custom_call" | custom-call | flops 8000000 | bytes 2700000 | tf_op jit(solution)/shard_map/local/pallas_call | solution.py:458
  18.0 1.8 %collective-permute-done.5.refs_7_ = f32[16,8,128]{2,1,0:T(8,128)S(1)} collective-permute-done((f32[16,8,128]{2,1,0:T(8,128)S(1)}, f32[16,8,128]{2,1,0:T(8,128)S(1)}, u32[]{:S(2)}, u32[]{:S(2)}) %collective-permute-start.5) | collective-permute-done | bytes 65568 | tf_op jit(solution)/shard_map/ppermute | solution.py:443
  19.9 0.2 collective-permute-done.6.refs_8_
  20.1 0.0 collective-permute-done.3.refs_4_
  20.1 0.0 copy-done.2
  20.1 0.0 copy-done.3
  20.1 2.4 %finish.1 = f32[19,128,128]{2,1,0:T(8,128)} custom-call(s32[2]{0:T(128)S(1)} %copy-done.2, s32[2]{0:T(128)S(1)} %copy-done.3, f32[19,18,8,128]{3,2,1,0:T(8,128)S(1)} %local.1.refs_2_, f32[4,3,8,128]{3,2,1,0:T(8,128)S(1)} %join.3.refs_3_, f32[4,3,8,128]{3,2,1,0:T(8,128)S(1)} %collective-permute-done.3.refs_4_, ...), custom_call_target="tpu_custom_call" | custom-call | tf_op jit(solution)/shard_map/finish/pallas_call | solution.py:467
  (4 shorter events, 0.0 us)
Async XLA Ops:
  0.0 1.3 %copy-start = (f32[19,8,16,128]{3,2,1,0:T(8,128)S(1)}, f32[19,8,16,128]{3,2,1,0:T(8,128)}, u32[]{:S(2)}) copy-start(f32[19,8,16,128]{3,2,1,0:T(8,128)} %param.3) | copy-start | bytes 3735556
  1.3 15.3 %copy-start.1 = (f32[19,8,16,128]{3,2,1,0:T(8,128)S(1)}, f32[19,8,16,128]{3,2,1,0:T(8,128)}, u32[]{:S(2)}) copy-start(f32[19,8,16,128]{3,2,1,0:T(8,128)} %param.3) | copy-start | bytes 3735556
  1.8 3.8 %collective-permute-start = (f32[2,8,128]{2,1,0:T(8,128)S(1)}, f32[2,8,128]{2,1,0:T(8,128)S(1)}, u32[]{:S(2)}, u32[]{:S(2)}) collective-permute-start(f32[2,8,128]{2,1,0:T(8,128)S(1)} %get-tuple-element.12), channel_id=1, source_target_pairs={{0,3},{1,2},{2,1},{3,0},{4,7},{5,6},{6,5},{7,4},{8,11},{9,10},{10,... | collective-permute-start | bytes 24584 | tf_op jit(solution)/shard_map/ppermute | solution.py:443
  5.7 3.9 %collective-permute-start.1 = (f32[1,3,8,128]{3,2,1,0:T(8,128)S(1)}, f32[1,3,8,128]{3,2,1,0:T(8,128)S(1)}, u32[]{:S(2)}, u32[]{:S(2)}) collective-permute-start(f32[1,3,8,128]{3,2,1,0:T(8,128)S(1)} %block.1.refs_0_), channel_id=1, source_target_pairs={{0,4},{4,0},{8,12},{12,8},{16,20},{20,16},{24,28},{28,24},{1,5},{5... | collective-permute-start | bytes 36872 | tf_op jit(solution)/shard_map/ppermute | solution.py:443
  7.9 4.8 %collective-permute-start.4 = (f32[2,8,128]{2,1,0:T(8,128)S(1)}, f32[2,8,128]{2,1,0:T(8,128)S(1)}, u32[]{:S(2)}, u32[]{:S(2)}) collective-permute-start(f32[2,8,128]{2,1,0:T(8,128)S(1)} %get-tuple-element.15), channel_id=1, source_target_pairs={{0,1},{1,0},{2,3},{3,2},{4,5},{5,4},{6,7},{7,6},{8,9},{9,8},{10,11... | collective-permute-start | bytes 24584 | tf_op jit(solution)/shard_map/ppermute | solution.py:443
  9.6 6.2 %collective-permute-start.2 = (f32[2,3,8,128]{3,2,1,0:T(8,128)S(1)}, f32[2,3,8,128]{3,2,1,0:T(8,128)S(1)}, u32[]{:S(2)}, u32[]{:S(2)}) collective-permute-start(f32[2,3,8,128]{3,2,1,0:T(8,128)S(1)} %join.2.refs_0_), channel_id=1, source_target_pairs={{0,16},{4,20},{8,24},{12,28},{16,0},{20,4},{24,8},{28,12},{1,17},{... | collective-permute-start | bytes 73736 | tf_op jit(solution)/shard_map/ppermute | solution.py:443
  12.8 7.1 %collective-permute-start.5 = (f32[16,8,128]{2,1,0:T(8,128)S(1)}, f32[16,8,128]{2,1,0:T(8,128)S(1)}, u32[]{:S(2)}, u32[]{:S(2)}) collective-permute-start(f32[16,8,128]{2,1,0:T(8,128)S(1)} %get-tuple-element.17), channel_id=1, source_target_pairs={{0,28},{4,8},{8,4},{12,16},{16,12},{20,24},{24,20},{28,0},{1,29},{... | collective-permute-start | bytes 196616 | tf_op jit(solution)/shard_map/ppermute | solution.py:443
  15.1 5.0 %collective-permute-start.6 = (f32[16,8,128]{2,1,0:T(8,128)S(1)}, f32[16,8,128]{2,1,0:T(8,128)S(1)}, u32[]{:S(2)}, u32[]{:S(2)}) collective-permute-start(f32[16,8,128]{2,1,0:T(8,128)S(1)} %get-tuple-element.18), channel_id=1, source_target_pairs={{0,4},{4,0},{8,12},{12,8},{16,20},{20,16},{24,28},{28,24},{1,5},{5... | collective-permute-start | bytes 196616 | tf_op jit(solution)/shard_map/ppermute | solution.py:443
  15.9 4.2 %copy-start.2 = (s32[2]{0:T(128)S(1)}, s32[2]{0:T(128)}, u32[]{:S(2)}) copy-start(s32[2]{0:T(128)} %refs_0_.1) | copy-start | bytes 28
  15.9 4.2 %copy-start.3 = (s32[2]{0:T(128)S(1)}, s32[2]{0:T(128)}, u32[]{:S(2)}) copy-start(s32[2]{0:T(128)} %refs_1_.1) | copy-start | bytes 28
  15.9 4.2 %collective-permute-start.3 = (f32[4,3,8,128]{3,2,1,0:T(8,128)S(1)}, f32[4,3,8,128]{3,2,1,0:T(8,128)S(1)}, u32[]{:S(2)}, u32[]{:S(2)}) collective-permute-start(f32[4,3,8,128]{3,2,1,0:T(8,128)S(1)} %join.3.refs_3_), channel_id=1, source_target_pairs={{0,8},{4,12},{8,0},{12,4},{16,24},{20,28},{24,16},{28,20},{1,9},{5... | collective-permute-start | bytes 147464 | tf_op jit(solution)/shard_map/ppermute | solution.py:443

commit v9 on v6

--- a/solution.py
+++ b/solution.py
@@ -129,7 +129,14 @@
     return ref[q, pl.ds(x, NZ, stride=width), :]
 
 
-def pack_kernel(shears, width, f_ref, side_ref, gap_ref, own_ref, near_ref, far_ref):
+def pack_kernel(shears, width, f_hbm, side_ref, gap_ref, own_ref, near_ref, far_ref, f_ref, sems):
+    cuts = [0, 10, 19]
+    copies = [
+        pltpu.make_async_copy(f_hbm.at[a:b], f_ref.at[a:b], sems.at[i])
+        for i, (a, b) in enumerate(zip(cuts, cuts[1:]))
+    ]
+    for copy in copies:
+        copy.start()
     shear = lax.axis_index("shear")
     lane = lane_iota()
     boost_up = jnp.where(shear == shears - 1, -BOOST, 0.0).astype(jnp.float32)
@@ -137,6 +144,8 @@
     here = [(lane >= x * GAP) & (lane < (x + 1) * GAP) for x in range(width)]
     edge = []
     for q in range(19):
+        if q in cuts:
+            copies[cuts.index(q)].wait()
         total = jnp.ones((NZ, LANES), jnp.float32)
         for x in range(width):
             total = jnp.where(here[x], roll_y(column(f_ref, q, x, width), x * GAP + 2), total)
@@ -439,9 +448,15 @@
     def swap(x, axis, partner):
         return lax.ppermute(x, axis, [(i, partner(i)) for i in range(lax.axis_size(axis))])
 
-    side, gap, own, near, far = call(
-        "pack", body(pack_kernel, shears, width), [vregs(2), vregs(2), vregs(2), vregs(13), vregs(13)], f
-    )
+    side, gap, own, near, far = pl.pallas_call(
+        body(pack_kernel, shears, width),
+        out_shape=[vregs(2), vregs(2), vregs(2), vregs(13), vregs(13)],
+        in_specs=[anyspace],
+        out_specs=[vmem] * 5,
+        scratch_shapes=[pltpu.VMEM((19, NZ * width, LANES), f32), pltpu.SemaphoreType.DMA((2,))],
+        compiler_params=pltpu.CompilerParams(vmem_limit_bytes=55400000),
+        name="pack",
+    )(f)
     side = swap(side, "shear", lambda i: i ^ 1)
     gap = swap(gap, "shear", lambda i: (i - 1 + i % 2 * 2) % shears)
     mine = call("block", block_kernel, vregs(1, 3), gap, own)

time: 22.8 us -> 22.7 us (level)
  local copies, waits for them, and re-layouts: 1.31 us -> 0.02 us
  Pallas kernels: 4.57 us -> 5.8 us
    pallas_call x0 -> x1, Pallas kernels: none -> 1.89 us  [per_device(): pl.pallas_call(body(pack_kernel, shears, width), out_shape=[vregs(2), vre...]
    unnamed x8 -> x6, local copies, waits for them, and re-layouts: 1.31 us -> 0.02 us
    pallas_call x5 -> x4, Pallas kernels: 0.68 us -> 0.02 us  [call(): pl.pallas_call(kernel, out_shape=outs, in_specs=[vmem] * len(arrays), out...]
where the time goes in v9:
time: 22.7 us; the launch traced here: 22.6 us
  starting transfers between devices  11.6 us (51%)
  Pallas kernels  5.8 us (26%)
  waiting for transfers between devices  5.07 us (22%)
    ppermute x7, starting transfers between devices, swap(): lax.ppermute(x, axis, [(i, partner(i)) for i in range(lax.axis_size(axis))])  11.6 us
    ppermute x7, waiting for transfers between devices, swap(): lax.ppermute(x, axis, [(i, partner(i)) for i in range(lax.axis_size(axis))])  5.07 us
    pallas_call x1, Pallas kernels, per_device(): pl.pallas_call(body(finish_kernel, flows, shears, width), out_shape=jax.S...  2.43 us
    pallas_call x1, Pallas kernels, per_device(): pl.pallas_call(body(pack_kernel, shears, width), out_shape=[vregs(2), vre...  1.89 us
    pallas_call x1, Pallas kernels, per_device(): pl.pallas_call(body(local_kernel, width), out_shape=jax.ShapeDtypeStruct(...  1.46 us
  transfers between devices with their start and end apart: 7, of which 4 were waited for; matrix products, arithmetic and copies ran while one was open for 0% of the time, Pallas kernels for 7%

profile of v9, /device:TPU:0, one launch (start us, length us, event | category | flops | bytes accessed | tf_op | source)
XLA Modules:
  0.0 22.6 jit_solution(11279262959566652630)
XLA Ops:
  0.0 0.0 copy-start
  0.0 1.9 %pack.1 = (f32[2,8,128]{2,1,0:T(8,128)S(1)}, f32[2,8,128]{2,1,0:T(8,128)S(1)}, f32[2,8,128]{2,1,0:T(8,128)S(1)}, f32[13,8,128]{2,1,0:T(8,128)S(1)}, f32[13,8,128]{2,1,0:T(8,128)S(1)}) custom-call(f32[19,128,128]{2,1,0:T(8,128)} %bitcast.2), custom_call_target="tpu_custom_call" | custom-call | tf_op jit(solution)/shard_map/pack/pallas_call | solution.py:451
  1.9 2.5 %collective-permute-start = (f32[2,8,128]{2,1,0:T(8,128)S(1)}, f32[2,8,128]{2,1,0:T(8,128)S(1)}, u32[]{:S(2)}, u32[]{:S(2)}) collective-permute-start(f32[2,8,128]{2,1,0:T(8,128)S(1)} %get-tuple-element.12), channel_id=1, source_target_pairs={{0,3},{1,2},{2,1},{3,0},{4,7},{5,6},{6,5},{7,4},{8,11},{9,10},{10,... | collective-permute-start | bytes 24584 | tf_op jit(solution)/shard_map/ppermute | solution.py:449
  4.4 1.4 %collective-permute-done.gap_ref = f32[2,8,128]{2,1,0:T(8,128)S(1)} collective-permute-done((f32[2,8,128]{2,1,0:T(8,128)S(1)}, f32[2,8,128]{2,1,0:T(8,128)S(1)}, u32[]{:S(2)}, u32[]{:S(2)}) %collective-permute-start) | collective-permute-done | bytes 8224 | tf_op jit(solution)/shard_map/ppermute | solution.py:449
  5.7 2.3 %collective-permute-start.1 = (f32[1,3,8,128]{3,2,1,0:T(8,128)S(1)}, f32[1,3,8,128]{3,2,1,0:T(8,128)S(1)}, u32[]{:S(2)}, u32[]{:S(2)}) collective-permute-start(f32[1,3,8,128]{3,2,1,0:T(8,128)S(1)} %block.1.refs_0_), channel_id=1, source_target_pairs={{0,4},{4,0},{8,12},{12,8},{16,20},{20,16},{24,28},{28,24},{1,5},{5... | collective-permute-start | bytes 36872 | tf_op jit(solution)/shard_map/ppermute | solution.py:449
  8.0 0.0 collective-permute-start.4
  8.0 1.7 %collective-permute-done.1.refs_1_ = f32[1,3,8,128]{3,2,1,0:T(8,128)S(1)} collective-permute-done((f32[1,3,8,128]{3,2,1,0:T(8,128)S(1)}, f32[1,3,8,128]{3,2,1,0:T(8,128)S(1)}, u32[]{:S(2)}, u32[]{:S(2)}) %collective-permute-start.1) | collective-permute-done | bytes 12320 | tf_op jit(solution)/shard_map/ppermute | solution.py:449
  9.7 3.1 %collective-permute-start.2 = (f32[2,3,8,128]{3,2,1,0:T(8,128)S(1)}, f32[2,3,8,128]{3,2,1,0:T(8,128)S(1)}, u32[]{:S(2)}, u32[]{:S(2)}) collective-permute-start(f32[2,3,8,128]{3,2,1,0:T(8,128)S(1)} %join.2.refs_0_), channel_id=1, source_target_pairs={{0,16},{4,20},{8,24},{12,28},{16,0},{20,4},{24,8},{28,12},{1,17},{... | collective-permute-start | bytes 73736 | tf_op jit(solution)/shard_map/ppermute | solution.py:449
  12.8 0.0 collective-permute-done.4.side_ref.refs_5_
  12.8 2.3 %collective-permute-start.5 = (f32[16,8,128]{2,1,0:T(8,128)S(1)}, f32[16,8,128]{2,1,0:T(8,128)S(1)}, u32[]{:S(2)}, u32[]{:S(2)}) collective-permute-start(f32[16,8,128]{2,1,0:T(8,128)S(1)} %get-tuple-element.17), channel_id=1, source_target_pairs={{0,28},{4,8},{8,4},{12,16},{16,12},{20,24},{24,20},{28,0},{1,29},{... | collective-permute-start | bytes 196616 | tf_op jit(solution)/shard_map/ppermute | solution.py:449
  15.2 0.8 %collective-permute-start.6 = (f32[16,8,128]{2,1,0:T(8,128)S(1)}, f32[16,8,128]{2,1,0:T(8,128)S(1)}, u32[]{:S(2)}, u32[]{:S(2)}) collective-permute-start(f32[16,8,128]{2,1,0:T(8,128)S(1)} %get-tuple-element.18), channel_id=1, source_target_pairs={{0,4},{4,0},{8,12},{12,8},{16,20},{20,16},{24,28},{28,24},{1,5},{5... | collective-permute-start | bytes 196616 | tf_op jit(solution)/shard_map/ppermute | solution.py:449
  15.9 0.0 collective-permute-done.2.refs_1_
  15.9 0.0 copy-start.1
  15.9 0.0 copy-start.2
  16.0 0.7 %collective-permute-start.3 = (f32[4,3,8,128]{3,2,1,0:T(8,128)S(1)}, f32[4,3,8,128]{3,2,1,0:T(8,128)S(1)}, u32[]{:S(2)}, u32[]{:S(2)}) collective-permute-start(f32[4,3,8,128]{3,2,1,0:T(8,128)S(1)} %join.3.refs_3_), channel_id=1, source_target_pairs={{0,8},{4,12},{8,0},{12,4},{16,24},{20,28},{24,16},{28,20},{1,9},{5... | collective-permute-start | bytes 147464 | tf_op jit(solution)/shard_map/ppermute | solution.py:449
  16.6 0.0 copy-done
  16.6 1.5 %local.1.refs_2_ = f32[19,18,8,128]{3,2,1,0:T(8,128)S(1)} custom-call(f32[19,128,128]{2,1,0:T(8,128)S(1)} %bitcast.3), custom_call_target="tpu_custom_call" | custom-call | flops 8000000 | bytes 2700000 | tf_op jit(solution)/shard_map/local/pallas_call | solution.py:471
  18.1 1.8 %collective-permute-done.5.refs_7_ = f32[16,8,128]{2,1,0:T(8,128)S(1)} collective-permute-done((f32[16,8,128]{2,1,0:T(8,128)S(1)}, f32[16,8,128]{2,1,0:T(8,128)S(1)}, u32[]{:S(2)}, u32[]{:S(2)}) %collective-permute-start.5) | collective-permute-done | bytes 65568 | tf_op jit(solution)/shard_map/ppermute | solution.py:449
  19.9 0.2 collective-permute-done.6.refs_8_
  20.1 0.0 collective-permute-done.3.refs_4_
  20.1 0.0 copy-done.1
  20.1 0.0 copy-done.2
  20.1 2.4 %finish.1 = f32[19,128,128]{2,1,0:T(8,128)} custom-call(s32[2]{0:T(128)S(1)} %copy-done.1, s32[2]{0:T(128)S(1)} %copy-done.2, f32[19,18,8,128]{3,2,1,0:T(8,128)S(1)} %local.1.refs_2_, f32[4,3,8,128]{3,2,1,0:T(8,128)S(1)} %join.3.refs_3_, f32[4,3,8,128]{3,2,1,0:T(8,128)S(1)} %collective-permute-done.3.refs_4_, ...), custom_call_target="tpu_custom_call" | custom-call | tf_op jit(solution)/shard_map/finish/pallas_call | solution.py:480
  (4 shorter events, 0.0 us)
Async XLA Ops:
  0.0 16.6 %copy-start = (f32[19,8,16,128]{3,2,1,0:T(8,128)S(1)}, f32[19,8,16,128]{3,2,1,0:T(8,128)}, u32[]{:S(2)}) copy-start(f32[19,8,16,128]{3,2,1,0:T(8,128)} %param.3) | copy-start | bytes 3735556
  1.9 3.8 %collective-permute-start = (f32[2,8,128]{2,1,0:T(8,128)S(1)}, f32[2,8,128]{2,1,0:T(8,128)S(1)}, u32[]{:S(2)}, u32[]{:S(2)}) collective-permute-start(f32[2,8,128]{2,1,0:T(8,128)S(1)} %get-tuple-element.12), channel_id=1, source_target_pairs={{0,3},{1,2},{2,1},{3,0},{4,7},{5,6},{6,5},{7,4},{8,11},{9,10},{10,... | collective-permute-start | bytes 24584 | tf_op jit(solution)/shard_map/ppermute | solution.py:449
  5.7 3.9 %collective-permute-start.1 = (f32[1,3,8,128]{3,2,1,0:T(8,128)S(1)}, f32[1,3,8,128]{3,2,1,0:T(8,128)S(1)}, u32[]{:S(2)}, u32[]{:S(2)}) collective-permute-start(f32[1,3,8,128]{3,2,1,0:T(8,128)S(1)} %block.1.refs_0_), channel_id=1, source_target_pairs={{0,4},{4,0},{8,12},{12,8},{16,20},{20,16},{24,28},{28,24},{1,5},{5... | collective-permute-start | bytes 36872 | tf_op jit(solution)/shard_map/ppermute | solution.py:449
  8.0 4.8 %collective-permute-start.4 = (f32[2,8,128]{2,1,0:T(8,128)S(1)}, f32[2,8,128]{2,1,0:T(8,128)S(1)}, u32[]{:S(2)}, u32[]{:S(2)}) collective-permute-start(f32[2,8,128]{2,1,0:T(8,128)S(1)} %get-tuple-element.14), channel_id=1, source_target_pairs={{0,1},{1,0},{2,3},{3,2},{4,5},{5,4},{6,7},{7,6},{8,9},{9,8},{10,11... | collective-permute-start | bytes 24584 | tf_op jit(solution)/shard_map/ppermute | solution.py:449
  9.7 6.2 %collective-permute-start.2 = (f32[2,3,8,128]{3,2,1,0:T(8,128)S(1)}, f32[2,3,8,128]{3,2,1,0:T(8,128)S(1)}, u32[]{:S(2)}, u32[]{:S(2)}) collective-permute-start(f32[2,3,8,128]{3,2,1,0:T(8,128)S(1)} %join.2.refs_0_), channel_id=1, source_target_pairs={{0,16},{4,20},{8,24},{12,28},{16,0},{20,4},{24,8},{28,12},{1,17},{... | collective-permute-start | bytes 73736 | tf_op jit(solution)/shard_map/ppermute | solution.py:449
  12.8 7.1 %collective-permute-start.5 = (f32[16,8,128]{2,1,0:T(8,128)S(1)}, f32[16,8,128]{2,1,0:T(8,128)S(1)}, u32[]{:S(2)}, u32[]{:S(2)}) collective-permute-start(f32[16,8,128]{2,1,0:T(8,128)S(1)} %get-tuple-element.17), channel_id=1, source_target_pairs={{0,28},{4,8},{8,4},{12,16},{16,12},{20,24},{24,20},{28,0},{1,29},{... | collective-permute-start | bytes 196616 | tf_op jit(solution)/shard_map/ppermute | solution.py:449
  15.2 5.0 %collective-permute-start.6 = (f32[16,8,128]{2,1,0:T(8,128)S(1)}, f32[16,8,128]{2,1,0:T(8,128)S(1)}, u32[]{:S(2)}, u32[]{:S(2)}) collective-permute-start(f32[16,8,128]{2,1,0:T(8,128)S(1)} %get-tuple-element.18), channel_id=1, source_target_pairs={{0,4},{4,0},{8,12},{12,8},{16,20},{20,16},{24,28},{28,24},{1,5},{5... | collective-permute-start | bytes 196616 | tf_op jit(solution)/shard_map/ppermute | solution.py:449
  15.9 4.2 %copy-start.1 = (s32[2]{0:T(128)S(1)}, s32[2]{0:T(128)}, u32[]{:S(2)}) copy-start(s32[2]{0:T(128)} %refs_0_.1) | copy-start | bytes 28
  15.9 4.2 %copy-start.2 = (s32[2]{0:T(128)S(1)}, s32[2]{0:T(128)}, u32[]{:S(2)}) copy-start(s32[2]{0:T(128)} %refs_1_.1) | copy-start | bytes 28
  16.0 4.2 %collective-permute-start.3 = (f32[4,3,8,128]{3,2,1,0:T(8,128)S(1)}, f32[4,3,8,128]{3,2,1,0:T(8,128)S(1)}, u32[]{:S(2)}, u32[]{:S(2)}) collective-permute-start(f32[4,3,8,128]{3,2,1,0:T(8,128)S(1)} %join.3.refs_3_), channel_id=1, source_target_pairs={{0,8},{4,12},{8,0},{12,4},{16,24},{20,28},{24,16},{28,20},{1,9},{5... | collective-permute-start | bytes 147464 | tf_op jit(solution)/shard_map/ppermute | solution.py:449
